TPU v7x, 32 devices: a whole 2x2x4 slice. The times are simulated.
32 devices in a mesh: expert: 4 (over x, core), tensor: 8 (over z, y).
Axes of the slice: x: 2, y: 2, z: 4, core: 2. Of those that a mesh axis runs over, the one named last changes fastest.
Arguments:
- tokens: bfloat16 [8192, 2048], P(('expert', 'tensor')), may hold values from -6 to 6
- segments: int32 [8, 1024], P('expert'), may hold values from 0 to 3, never falling along the last dimension, each value on 1 to 512 neighbouring positions
- routes: int32 [8192, 8], P(('expert', 'tensor')), may hold values from 0 to 15, all different within a row; in each aligned block of 256 rows (0 to 255, 256 to 511, ...) at most 256 rows name the same one
- norm_gain: float32 [2048], replicated, may hold values from 0.5 to 1.5
- w_query: bfloat16 [2048, 2048], P('expert', 'tensor'), may hold values from -0.125 to 0.125
- w_key: bfloat16 [2048, 2048], P('expert', 'tensor'), may hold values from -0.125 to 0.125
- w_value: bfloat16 [2048, 2048], P('expert', 'tensor'), may hold values from -0.125 to 0.125
- query_gain: float32 [128], replicated, may hold values from 0.5 to 1.5
- key_gain: float32 [128], replicated, may hold values from 0.5 to 1.5
- w_out: bfloat16 [2048, 2048], P('tensor', 'expert'), may hold values from -1 to 1
- mix_gain: float32 [2048], replicated, may hold values from 0.5 to 1.5
- w_router: bfloat16 [2048, 16], replicated, may hold values from -0.0625 to 0.0625
- w_gate: bfloat16 [32, 2048, 512], P(('expert', 'tensor')), may hold values from -0.125 to 0.125
- w_up: bfloat16 [32, 2048, 512], P(('expert', 'tensor')), may hold values from -0.125 to 0.125
- w_down: bfloat16 [32, 512, 2048], P(('expert', 'tensor')), may hold values from -0.75 to 0.75
- cotangent: bfloat16 [8192, 2048], P(('expert', 'tensor')), may hold values from -6 to 6
Outputs:
- layer_out: bfloat16 [8192, 2048], P(('expert', 'tensor'))
- grad_tokens: bfloat16 [8192, 2048], P(('expert', 'tensor'))
- grad_norm_gain: float32 [2048], replicated
- grad_w_query: float32 [2048, 2048], P('expert', 'tensor')
- grad_w_key: float32 [2048, 2048], P('expert', 'tensor')
- grad_w_value: float32 [2048, 2048], P('expert', 'tensor')
- grad_query_gain: float32 [128], replicated
- grad_key_gain: float32 [128], replicated
- grad_w_out: float32 [2048, 2048], P('tensor', 'expert')
- grad_mix_gain: float32 [2048], replicated
- grad_w_router: float32 [2048, 16], replicated
- grad_w_gate: float32 [32, 2048, 512], P(('expert', 'tensor'))
- grad_w_up: float32 [32, 2048, 512], P(('expert', 'tensor'))
- grad_w_down: float32 [32, 512, 2048], P(('expert', 'tensor'))
Inputs may be any that keep to these rules, and one draw needn't show every extreme that they name: `segments`: within a sequence the numbers never fall, every document has 1 to half of 1024 tokens, and one document of each sequence has exactly half of 1024. `routes`: each token names 8 different experts; among the 256 tokens of one device no expert is named more than 256 times, and in every draw some device names some expert exactly 256 times.
All inputs are finite; a program needn't handle non-finite values.
Results may differ from a plain program's by a relative error of at most 0.025.
Values may be sent and summed in bfloat16 or wider, within the bound.
No kernel may reach another device: no remote copies, remote signals or barrier semaphores. Data moves between devices by JAX's collectives and lax.ppermute only.
A program may use at most 576 MiB of HBM per device.

v0:
```python
import jax
import jax.numpy as jnp
from jax import lax
from jax.sharding import PartitionSpec as P

WIN = 1024


EPSILON = 1e-05
THETA = 50000.0
MASKED = -1e30
HIGH = lax.Precision.HIGHEST


def inner_rows(left_side, right_side, precision=None):
    return lax.dot_general(
        left_side,
        right_side,
        (((0,), (0,)), ((), ())),
        precision=precision,
        preferred_element_type=jnp.float32,
    )


def outer_rows(left_side, right_side, precision=None):
    return lax.dot_general(
        left_side,
        right_side,
        (((1,), (1,)), ((), ())),
        precision=precision,
        preferred_element_type=jnp.float32,
    )


def rope_tables(length, head_size):
    half_size = head_size // 2
    frequency = THETA ** (-2.0 * jnp.arange(half_size, dtype=jnp.float32) / head_size)
    angles = jnp.arange(length, dtype=jnp.float32)[:, None] * frequency[None, :]
    return (jnp.cos(angles)[:, None, :], jnp.sin(angles)[:, None, :])


def qk_prepare(projected, gain_vec, cos_part, sin_part):
    scaled = (
        projected
        * lax.rsqrt(jnp.mean(projected * projected, axis=-1, keepdims=True) + EPSILON)
        * gain_vec
    )
    half_size = scaled.shape[-1] // 2
    first_half = scaled[..., :half_size]
    second = scaled[..., half_size:]
    return jnp.concatenate(
        [first_half * cos_part - second * sin_part, second * cos_part + first_half * sin_part],
        axis=-1,
    )


def allowed_pairs(seg_row):
    length = seg_row.shape[0]
    position = jnp.arange(length, dtype=jnp.int32)
    near_pairs = jnp.abs(position[:, None] - position[None, :]) < WIN
    return near_pairs & (seg_row[:, None] == seg_row[None, :])


def attend_item(item_list):
    query_block, key_block, value_block, seg_row = item_list
    scaling = query_block.shape[-1] ** (-0.5)
    scores = outer_rows(query_block, key_block) * scaling
    scores = jnp.where(allowed_pairs(seg_row), scores, MASKED)
    row_max = jnp.max(scores, axis=-1, keepdims=True)
    exponent = jnp.exp(scores - row_max)
    row_total = jnp.sum(exponent, axis=-1, keepdims=True)
    prob_vals = (exponent / row_total).astype(jnp.bfloat16)
    attended = jnp.dot(prob_vals, value_block, preferred_element_type=jnp.float32)
    return (attended, (row_max + jnp.log(row_total))[:, 0])


def attend_back(item_list):
    query_block, key_block, value_block, grad_block, log_total, seg_row = item_list
    scaling = query_block.shape[-1] ** (-0.5)
    scores = outer_rows(query_block, key_block) * scaling
    prob_vals = jnp.where(allowed_pairs(seg_row), jnp.exp(scores - log_total[:, None]), 0.0)
    grad_prob = outer_rows(grad_block, value_block).astype(jnp.bfloat16).astype(jnp.float32)
    grad_value = inner_rows(prob_vals.astype(jnp.bfloat16), grad_block)
    centre = jnp.sum(prob_vals * grad_prob, axis=-1, keepdims=True)
    grad_score = (prob_vals * (grad_prob - centre)).astype(jnp.bfloat16)
    grad_query = jnp.dot(grad_score, key_block, preferred_element_type=jnp.float32) * scaling
    grad_key = inner_rows(grad_score, query_block) * scaling
    return (grad_query, grad_key, grad_value)


def swiglu_back(
    expert_rows, gate_pre, up_pre, sigmoid_val, activation, arrived_grad, gate_mat, up_mat, down_mat
):
    silu_val = gate_pre * sigmoid_val
    grad_down_w = inner_rows(activation, arrived_grad)
    grad_act = outer_rows(arrived_grad, down_mat)
    grad_gate_pre = (
        grad_act * up_pre * sigmoid_val * (1.0 + gate_pre * (1.0 - sigmoid_val))
    ).astype(jnp.bfloat16)
    grad_up_pre = (grad_act * silu_val).astype(jnp.bfloat16)
    grad_gate_w = inner_rows(expert_rows, grad_gate_pre)
    grad_up_w = inner_rows(expert_rows, grad_up_pre)
    grad_rows_part = outer_rows(grad_gate_pre, gate_mat) + outer_rows(grad_up_pre, up_mat)
    return (grad_gate_w, grad_up_w, grad_down_w, grad_rows_part)


def per_device(
    tokens,
    segments,
    routes,
    norm_gain,
    w_query,
    w_key,
    w_value,
    query_gain,
    key_gain,
    w_out,
    mix_gain,
    w_router,
    w_gate,
    w_up,
    w_down,
    cotangent,
):
    slab_count = lax.axis_size(("expert", "tensor"))
    expert_count = slab_count // 2
    tok_rows, model_width = tokens.shape
    seq_count, length = segments.shape
    top_count = routes.shape[1]
    head_size = query_gain.shape[0]
    heads_here = w_query.shape[1] // head_size
    capacity = 2 * tok_rows * top_count // expert_count
    group_rows = seq_count * length
    local_width = heads_here * head_size
    shape_heads = (seq_count, length, heads_here, head_size)

    def give_back(partial_rows):
        arrived_back = lax.all_to_all(
            partial_rows.astype(jnp.bfloat16),
            ("expert", "tensor"),
            split_axis=0,
            concat_axis=0,
            tiled=True,
        ).astype(partial_rows.dtype)
        return jnp.sum(arrived_back.reshape(expert_count, 2, capacity, model_width), axis=1).astype(
            jnp.bfloat16
        )

    inputs = tokens.astype(jnp.float32)
    inv_one = lax.rsqrt(jnp.mean(inputs * inputs, axis=-1, keepdims=True) + EPSILON)
    unit_one = inputs * inv_one
    normed_one = (unit_one * norm_gain).astype(jnp.bfloat16)
    normed_all = lax.all_gather(normed_one, "tensor", axis=0, tiled=True)
    query_full, key_full, value_full = (
        lax.all_gather(w_query, "expert", axis=0, tiled=True),
        lax.all_gather(w_key, "expert", axis=0, tiled=True),
        lax.all_gather(w_value, "expert", axis=0, tiled=True),
    )
    out_full = lax.all_gather(w_out, "expert", axis=1, tiled=True)
    query_proj = jnp.dot(normed_all, query_full, preferred_element_type=jnp.float32).reshape(
        shape_heads
    )
    key_proj = jnp.dot(normed_all, key_full, preferred_element_type=jnp.float32).reshape(
        shape_heads
    )
    value_low = (
        jnp.dot(normed_all, value_full, preferred_element_type=jnp.float32)
        .astype(jnp.bfloat16)
        .reshape(shape_heads)
    )
    cos_part, sin_part = rope_tables(length, head_size)
    query_low = qk_prepare(query_proj, query_gain, cos_part, sin_part).astype(jnp.bfloat16)
    key_low = qk_prepare(key_proj, key_gain, cos_part, sin_part).astype(jnp.bfloat16)

    def to_items(heads_arr):
        return heads_arr.transpose(0, 2, 1, 3).reshape(seq_count * heads_here, length, head_size)

    def from_items(item_arr):
        return item_arr.reshape(seq_count, heads_here, length, head_size).transpose(0, 2, 1, 3)

    seg_items = jnp.repeat(segments, heads_here, axis=0)
    query_items = to_items(query_low)
    key_items = to_items(key_low)
    value_items = to_items(value_low)
    attended, log_total = lax.map(attend_item, (query_items, key_items, value_items, seg_items))
    attn_rows = from_items(attended).reshape(group_rows, local_width).astype(jnp.bfloat16)
    branch = lax.psum_scatter(
        jnp.dot(attn_rows, out_full, preferred_element_type=jnp.float32).astype(jnp.bfloat16),
        "tensor",
        scatter_dimension=0,
        tiled=True,
    ).astype(jnp.float32)
    residual = inputs + branch
    inv_two = lax.rsqrt(jnp.mean(residual * residual, axis=-1, keepdims=True) + EPSILON)
    unit_two = residual * inv_two
    normed_two = (unit_two * mix_gain).astype(jnp.bfloat16)
    logits = jnp.dot(normed_two, w_router, preferred_element_type=jnp.float32)
    hit_table = routes[:, :, None] == jnp.arange(expert_count, dtype=jnp.int32)[None, None, :]
    hit_float = hit_table.astype(jnp.float32)
    chosen = jnp.einsum("tke,te->tk", hit_float, logits, precision=HIGH)
    gate_weights = jax.nn.softmax(chosen, axis=-1)
    flat_expert = routes.reshape(-1)
    hit_flat = hit_table.reshape(tok_rows * top_count, expert_count).astype(jnp.int32)
    slot_of = jnp.sum(jnp.cumsum(hit_flat, axis=0) * hit_flat, axis=1) - 1
    token_of = jnp.arange(tok_rows * top_count, dtype=jnp.int32) // top_count
    grad_out = cotangent.astype(jnp.float32)
    grad_expert = (
        (gate_weights[:, :, None] * grad_out[:, None, :])
        .astype(jnp.bfloat16)
        .reshape(tok_rows * top_count, model_width)
    )

    def dispatch_buffer(row_values):
        placed = (
            jnp.zeros((expert_count, capacity, model_width), jnp.bfloat16)
            .at[flat_expert, slot_of]
            .set(row_values)
        )
        return jnp.broadcast_to(placed[:, None], (expert_count, 2, capacity, model_width)).reshape(
            slab_count, capacity, model_width
        )

    arrived = lax.all_to_all(
        dispatch_buffer(normed_two[token_of]),
        ("expert", "tensor"),
        split_axis=0,
        concat_axis=0,
        tiled=True,
    )
    expert_rows = arrived.reshape(slab_count * capacity, model_width)
    gate_pre = jnp.dot(expert_rows, w_gate[0], preferred_element_type=jnp.float32)
    up_pre = jnp.dot(expert_rows, w_up[0], preferred_element_type=jnp.float32)
    sigmoid_val = jax.nn.sigmoid(gate_pre)
    activation = (gate_pre * sigmoid_val * up_pre).astype(jnp.bfloat16)
    partial_out = jnp.dot(activation, w_down[0], preferred_element_type=jnp.float32).reshape(
        slab_count, capacity, model_width
    )
    returned = give_back(partial_out)
    picked = returned[flat_expert, slot_of].reshape(tok_rows, top_count, model_width)
    arrived_grad = lax.all_to_all(
        dispatch_buffer(grad_expert), ("expert", "tensor"), split_axis=0, concat_axis=0, tiled=True
    )
    arrived_grad = arrived_grad.reshape(slab_count * capacity, model_width)
    grad_gate_w, grad_up_w, grad_down_w, grad_rows_part = swiglu_back(
        expert_rows,
        gate_pre,
        up_pre,
        sigmoid_val,
        activation,
        arrived_grad,
        w_gate[0],
        w_up[0],
        w_down[0],
    )
    grad_returned = give_back(grad_rows_part.reshape(slab_count, capacity, model_width))
    grad_picked = grad_returned[flat_expert, slot_of].reshape(tok_rows, top_count, model_width)
    mixture = jnp.sum(gate_weights[:, :, None] * picked, axis=1)
    layer_out = (residual + mixture).astype(jnp.bfloat16)
    grad_gates = jnp.sum(grad_out[:, None, :] * picked, axis=-1)
    grad_chosen = gate_weights * (
        grad_gates - jnp.sum(gate_weights * grad_gates, axis=-1, keepdims=True)
    )
    grad_logits = jnp.einsum("tk,tke->te", grad_chosen, hit_float, precision=HIGH)
    grad_normed_two = jnp.sum(grad_picked.astype(jnp.float32), axis=1) + outer_rows(
        grad_logits, w_router.astype(jnp.float32), HIGH
    )
    grad_router = inner_rows(normed_two.astype(jnp.float32), grad_logits, HIGH)
    grad_unit_two = grad_normed_two * mix_gain
    grad_mix_gain = jnp.sum(grad_normed_two * unit_two, axis=0)
    grad_residual = grad_out + inv_two * (
        grad_unit_two - unit_two * jnp.mean(grad_unit_two * unit_two, axis=-1, keepdims=True)
    )
    grad_branch = grad_residual.astype(jnp.bfloat16)
    grad_branch_all = lax.all_gather(grad_branch, "tensor", axis=0, tiled=True)
    grad_w_out = inner_rows(attn_rows, grad_branch_all)
    grad_attn = outer_rows(grad_branch_all, out_full).astype(jnp.bfloat16)
    grad_items = to_items(grad_attn.reshape(shape_heads))
    grad_query_items, grad_key_items, grad_value_items = lax.map(
        attend_back, (query_items, key_items, value_items, grad_items, log_total, seg_items)
    )
    grad_value_rows = (
        from_items(grad_value_items).reshape(group_rows, local_width).astype(jnp.bfloat16)
    )

    def prepare_heads(projected, gain_vec):
        return qk_prepare(projected, gain_vec, cos_part, sin_part)

    unused_query, pull_query = jax.vjp(prepare_heads, query_proj, query_gain)
    grad_query_proj, grad_query_gain = pull_query(from_items(grad_query_items))
    unused_key, pull_key = jax.vjp(prepare_heads, key_proj, key_gain)
    grad_key_proj, grad_key_gain = pull_key(from_items(grad_key_items))
    grad_query_low = grad_query_proj.reshape(group_rows, local_width).astype(jnp.bfloat16)
    grad_key_low = grad_key_proj.reshape(group_rows, local_width).astype(jnp.bfloat16)
    grad_w_query = inner_rows(normed_all, grad_query_low)
    grad_w_key = inner_rows(normed_all, grad_key_low)
    grad_w_value = inner_rows(normed_all, grad_value_rows)
    owned_query, owned_key, owned_value = (
        lax.psum_scatter(
            grad_w_query.astype(jnp.bfloat16), "expert", scatter_dimension=0, tiled=True
        ).astype(jnp.float32),
        lax.psum_scatter(
            grad_w_key.astype(jnp.bfloat16), "expert", scatter_dimension=0, tiled=True
        ).astype(jnp.float32),
        lax.psum_scatter(
            grad_w_value.astype(jnp.bfloat16), "expert", scatter_dimension=0, tiled=True
        ).astype(jnp.float32),
    )
    owned_out = lax.psum_scatter(
        grad_w_out.astype(jnp.bfloat16), "expert", scatter_dimension=1, tiled=True
    ).astype(jnp.float32)
    grad_normed_one = lax.psum_scatter(
        (
            outer_rows(grad_query_low, query_full)
            + outer_rows(grad_key_low, key_full)
            + outer_rows(grad_value_rows, value_full)
        ).astype(jnp.bfloat16),
        "tensor",
        scatter_dimension=0,
        tiled=True,
    ).astype(jnp.float32)
    grad_unit_one = grad_normed_one * norm_gain
    grad_norm_gain = jnp.sum(grad_normed_one * unit_one, axis=0)
    grad_tokens = grad_residual + inv_one * (
        grad_unit_one - unit_one * jnp.mean(grad_unit_one * unit_one, axis=-1, keepdims=True)
    )
    summed_small = lax.psum(
        (grad_router, grad_norm_gain, grad_mix_gain, grad_query_gain, grad_key_gain),
        ("expert", "tensor"),
    )
    return (
        layer_out,
        grad_tokens.astype(jnp.bfloat16),
        summed_small[1],
        owned_query,
        owned_key,
        owned_value,
        summed_small[3],
        summed_small[4],
        owned_out,
        summed_small[2],
        summed_small[0],
        grad_gate_w[None],
        grad_up_w[None],
        grad_down_w[None],
    )


def solution(mesh):
    in_specs = (
        P(("expert", "tensor"), None),
        P("expert", None),
        P(("expert", "tensor"), None),
        P(),
        P("expert", "tensor"),
        P("expert", "tensor"),
        P("expert", "tensor"),
        P(),
        P(),
        P("tensor", "expert"),
        P(),
        P(),
        P(("expert", "tensor"), None, None),
        P(("expert", "tensor"), None, None),
        P(("expert", "tensor"), None, None),
        P(("expert", "tensor"), None),
    )
    out_specs = (
        P(("expert", "tensor"), None),
        P(("expert", "tensor"), None),
        P(),
        P("expert", "tensor"),
        P("expert", "tensor"),
        P("expert", "tensor"),
        P(),
        P(),
        P("tensor", "expert"),
        P(),
        P(),
        P(("expert", "tensor"), None, None),
        P(("expert", "tensor"), None, None),
        P(("expert", "tensor"), None, None),
    )
    return jax.shard_map(
        per_device, mesh=mesh, in_specs=in_specs, out_specs=out_specs, check_vma=False
    )
```

profile of v0, /device:TPU:0, one launch (start us, length us, event | category | flops | bytes accessed | tf_op | source)
XLA Modules:
  0.0 4252.4 jit_solution(13103539413312916678)
XLA Ops:
  29.1 127.7 %all-gather.7.cloned.1.call-done = bf16[2048,2048]{1,0:T(8,128)(2,1)} async-done(((bf16[256,2048]{1,0:T(8,128)(2,1)}), bf16[2048,2048]{1,0:T(8,128)(2,1)}) %all-gather.7.cloned.1.call-update) | async-done | bytes 8388624 | tf_op jit(solution)/shard_map/all_gather | solution.py:153
  231.3 24.9 while.28
  276.7 139.1 %reduce-scatter.7.cloned.1.call-done = bf16[256,2048]{1,0:T(8,128)(2,1)} async-done(((bf16[2048,2048]{1,0:T(8,128)(2,1)}), bf16[256,2048]{1,0:T(8,128)(2,1)}) %reduce-scatter.7.cloned.1.call-update) | async-done | bytes 1048592 | tf_op jit(solution)/shard_map/reduce_scatter | solution.py:187
  419.1 49.1 %scatter_custom_fusion = bf16[4096,2048]{1,0:T(8,128)(2,1)} fusion(s32[2048]{0:T(1024)S(1)} %get-tuple-element.193, bf16[256,2048]{1,0:T(8,128)(2,1)} %multiply_convert_fusion.3, s32[2048]{0:T(1024)S(1)} %get-tuple-element.192, bf16[]{:T(256)} %constant.104.clone.1), kind=kCustom, calls=%fused_computation.82 | custom fusion | bytes 16777728
  515.9 720.7 %all-to-all-done = bf16[32,256,2048]{2,1,0:T(8,128)(2,1)} async-done(((bf16[32,256,2048]{2,1,0:T(8,128)(2,1)}), bf16[32,256,2048]{2,1,0:T(8,128)(2,1)}, u32[]{:S(2)}, u32[]{:S(2)}) %all-to-all-start) | async-done | bytes 33554464 | tf_op jit(solution)/shard_map/all_to_all | solution.py:223
  1256.8 25.5 fusion.78
  1282.3 24.8 fusion.82
  1307.1 697.6 %all-to-all-done.2 = bf16[32,256,2048]{2,1,0:T(8,128)(2,1)} async-done(((bf16[32,256,2048]{2,1,0:T(8,128)(2,1)}), bf16[32,256,2048]{2,1,0:T(8,128)(2,1)}, u32[]{:S(2)}, u32[]{:S(2)}) %all-to-all-start.2) | async-done | bytes 33554464 | tf_op jit(solution)/shard_map/all_to_all | solution.py:240
  2004.7 37.8 multiply_convert_fusion
  2072.0 29.1 fusion.80
  2101.1 37.9 add_convert_fusion
  2138.9 678.9 %all-to-all-done.1 = bf16[32,256,2048]{2,1,0:T(8,128)(2,1)} async-done(((bf16[32,256,2048]{2,1,0:T(8,128)(2,1)}), bf16[32,256,2048]{2,1,0:T(8,128)(2,1)}, u32[]{:S(2)}, u32[]{:S(2)}) %all-to-all-start.1) | async-done | bytes 33554464 | tf_op jit(solution)/shard_map/all_to_all | solution.py:138
  2822.2 28.3 bitcast_reduce_fusion.1
  2850.5 50.4 %gather_fusion = bf16[2048,2048]{1,0:T(8,128)(2,1)} fusion(bf16[16,256,2048]{2,1,0:T(8,128)(2,1)} %bitcast_reduce_fusion.1, s32[2048]{0:T(1024)S(1)} %bitcast.280), kind=kCustom, calls=%fused_computation.1 | custom fusion | bytes 16793600 | tf_op jit(solution)/shard_map/gather | solution.py:239
  2912.2 658.0 %all-to-all-done.3 = bf16[32,256,2048]{2,1,0:T(8,128)(2,1)} async-done(((bf16[32,256,2048]{2,1,0:T(8,128)(2,1)}), bf16[32,256,2048]{2,1,0:T(8,128)(2,1)}, u32[]{:S(2)}, u32[]{:S(2)}) %all-to-all-start.3) | async-done | bytes 33554464 | tf_op jit(solution)/shard_map/all_to_all | solution.py:138
  3570.2 28.1 bitcast_reduce_fusion
  3598.2 50.8 %gather_fusion.1 = bf16[2048,2048]{1,0:T(8,128)(2,1)} fusion(bf16[16,256,2048]{2,1,0:T(8,128)(2,1)} %bitcast_reduce_fusion, s32[2048]{0:T(1024)S(1)} %bitcast.281), kind=kCustom, calls=%fused_computation.2 | custom fusion | bytes 16793600 | tf_op jit(solution)/shard_map/gather | solution.py:256
  3668.0 121.1 %all-gather.17.cloned.1.call-done = bf16[2048,2048]{1,0:T(8,128)(2,1)} async-done(((bf16[256,2048]{1,0:T(8,128)(2,1)}), bf16[2048,2048]{1,0:T(8,128)(2,1)}) %all-gather.17.cloned.1.call-update) | async-done | bytes 8388624 | tf_op jit(solution)/shard_map/all_gather | solution.py:274
  3803.1 41.6 while.29
  3969.0 25.4 convolution_bitcast_fusion
  3994.4 25.2 convolution_bitcast_fusion.1
  4050.6 65.8 %reduce-scatter.9.cloned.1.call-done = bf16[256,2048]{1,0:T(8,128)(2,1)} async-done(((bf16[2048,2048]{1,0:T(8,128)(2,1)}), bf16[256,2048]{1,0:T(8,128)(2,1)}) %reduce-scatter.9.cloned.1.call-update) | async-done | bytes 1048592 | tf_op jit(solution)/shard_map/reduce_scatter | solution.py:311
  4124.6 39.5 all-reduce.4
  4164.1 80.0 %all-reduce.7.cloned.1.call-done = f32[2048,16]{0,1:T(8,128)} async-done(((f32[2048,16]{0,1:T(8,128)}), f32[2048,16]{0,1:T(8,128)}) %all-reduce.7.cloned.1.call-update) | async-done | bytes 131088 | tf_op jit(solution)/shard_map/psum | solution.py:326
  (393 shorter events, 495.7 us)
Async XLA Ops:
  7.2 1997.6 %copy-start = (bf16[1,512,2048]{2,1,0:T(8,128)(2,1)S(1)}, bf16[1,512,2048]{2,1,0:T(8,128)(2,1)}, u32[]{:S(2)}) copy-start(bf16[1,512,2048]{2,1,0:T(8,128)(2,1)} %param.34) | copy-start | bytes 6291460
  7.2 21.9 all-gather.13.cloned.1.call-start
  7.9 148.8 %all-gather.7.cloned.1.call-start = ((), (), s32[]{:S(2)}) async-start(), calls=%async_computation.10 | async-start | bytes 9437184 | tf_op jit(solution)/shard_map/all_gather | solution.py:153
  12.6 160.6 %all-gather.11.cloned.1.call-start = ((), (), s32[]{:S(2)}) async-start(), calls=%async_computation.12 | async-start | bytes 1310720 | tf_op jit(solution)/shard_map/all_gather | solution.py:156
  13.4 178.0 %all-gather.9.cloned.1.call-start = ((), (), s32[]{:S(2)}) async-start(), calls=%async_computation.11 | async-start | bytes 1310720 | tf_op jit(solution)/shard_map/all_gather | solution.py:155
  13.9 245.5 %all-gather.15.cloned.1.call-start = ((), (), s32[]{:S(2)}) async-start(), calls=%async_computation.14 | async-start | bytes 1310720 | tf_op jit(solution)/shard_map/all_gather | solution.py:159
  14.5 401.4 %reduce-scatter.7.cloned.1.call-start = ((), (), s32[]{:S(2)}) async-start(), calls=%async_computation.15 | async-start | bytes 9437184 | tf_op jit(solution)/shard_map/reduce_scatter | solution.py:187
  14.7 149.0 %copy-start.23 = (bf16[4,1024,128]{2,1,0:T(8,128)(2,1)}, bf16[4,1024,128]{2,1,0:T(8,128)(2,1)S(1)}, u32[]{:S(2)}) copy-start(bf16[4,1024,128]{2,1,0:T(8,128)(2,1)S(1)} %fusion.118) | copy-start | bytes 3145732
  267.4 148.5 %copy-start.3 = (bf16[256,2048]{1,0:T(8,128)(2,1)S(1)}, bf16[256,2048]{1,0:T(8,128)(2,1)}, u32[]{:S(2)}) copy-start(bf16[256,2048]{1,0:T(8,128)(2,1)} %param.20) | copy-start | bytes 3145732
  267.4 150.2 %copy-start.58 = (f32[2048]{0:T(1024)S(1)}, f32[2048]{0:T(1024)}, u32[]{:S(2)}) copy-start(f32[2048]{0:T(1024)} %param.30) | copy-start | bytes 24580
  267.5 223.1 %copy-start.42 = (s32[256,8]{1,0:T(8,128)}, s32[256,8]{1,0:T(8,128)S(1)}, u32[]{:S(2)}) copy-start(s32[256,8]{1,0:T(8,128)S(1)} %copy.73) | copy-start | bytes 24580
  484.1 752.5 %all-to-all-start = ((bf16[32,256,2048]{2,1,0:T(8,128)(2,1)}), bf16[32,256,2048]{2,1,0:T(8,128)(2,1)}, u32[]{:S(2)}, u32[]{:S(2)}) async-start(bf16[32,256,2048]{2,1,0:T(8,128)(2,1)} %bitcast.282), calls=%async_computation.1 | async-start | bytes 67108864 | tf_op jit(solution)/shard_map/all_to_all | solution.py:223
  1252.5 752.3 %all-to-all-start.2 = ((bf16[32,256,2048]{2,1,0:T(8,128)(2,1)}), bf16[32,256,2048]{2,1,0:T(8,128)(2,1)}, u32[]{:S(2)}, u32[]{:S(2)}) async-start(bf16[32,256,2048]{2,1,0:T(8,128)(2,1)} %bitcast.283), calls=%async_computation.3 | async-start | bytes 67108864 | tf_op jit(solution)/shard_map/all_to_all | solution.py:240
  2067.4 750.5 %all-to-all-start.1 = ((bf16[32,256,2048]{2,1,0:T(8,128)(2,1)}), bf16[32,256,2048]{2,1,0:T(8,128)(2,1)}, u32[]{:S(2)}, u32[]{:S(2)}) async-start(bf16[32,256,2048]{2,1,0:T(8,128)(2,1)} %convolution_convert_fusion.1), calls=%async_computation.2 | async-start | bytes 67108864 | tf_op jit(solution)/shard_map/all_to_all | solution.py:138
  2817.9 752.3 %all-to-all-start.3 = ((bf16[32,256,2048]{2,1,0:T(8,128)(2,1)}), bf16[32,256,2048]{2,1,0:T(8,128)(2,1)}, u32[]{:S(2)}, u32[]{:S(2)}) async-start(bf16[32,256,2048]{2,1,0:T(8,128)(2,1)} %bitcast.286), calls=%async_computation.4 | async-start | bytes 67108864 | tf_op jit(solution)/shard_map/all_to_all | solution.py:138
  2822.2 966.9 %all-gather.17.cloned.1.call-start = ((), (), s32[]{:S(2)}) async-start(), calls=%async_computation.16 | async-start | bytes 9437184 | tf_op jit(solution)/shard_map/all_gather | solution.py:274
  2912.1 748.3 %copy-start.49 = (f32[256,1,16]{2,1,0:T(1,128)}, f32[256,1,16]{2,1,0:T(1,128)S(1)}, u32[]{:S(2)}) copy-start(f32[256,1,16]{2,1,0:T(1,128)S(1)} %fusion.95) | copy-start | bytes 49156
  3667.7 375.7 %reduce-scatter.17.cloned.1.call-start = ((), (), s32[]{:S(2)}) async-start(), calls=%async_computation.21 | async-start | bytes 1310720 | tf_op jit(solution)/shard_map/reduce_scatter | solution.py:308
  3803.1 242.2 %reduce-scatter.15.cloned.1.call-start = ((), (), s32[]{:S(2)}) async-start(), calls=%async_computation.20 | async-start | bytes 1310720 | tf_op jit(solution)/shard_map/reduce_scatter | solution.py:304
  3860.0 187.0 %reduce-scatter.13.cloned.1.call-start = ((), (), s32[]{:S(2)}) async-start(), calls=%async_computation.19 | async-start | bytes 1310720 | tf_op jit(solution)/shard_map/reduce_scatter | solution.py:301
  3902.0 146.9 %reduce-scatter.11.cloned.1.call-start = ((), (), s32[]{:S(2)}) async-start(), calls=%async_computation.18 | async-start | bytes 1310720 | tf_op jit(solution)/shard_map/reduce_scatter | solution.py:298
  3935.4 181.0 %reduce-scatter.9.cloned.1.call-start = ((), (), s32[]{:S(2)}) async-start(), calls=%async_computation.17 | async-start | bytes 9437184 | tf_op jit(solution)/shard_map/reduce_scatter | solution.py:311
  3969.0 275.2 %all-reduce.7.cloned.1.call-start = ((), (), s32[]{:S(2)}) async-start(), calls=%async_computation.22 | async-start | bytes 262144 | tf_op jit(solution)/shard_map/psum | solution.py:326
  4118.6 127.1 %copy-start.1 = (bf16[1,512,2048]{2,1,0:T(8,128)(2,1)S(1)}, bf16[1,512,2048]{2,1,0:T(8,128)(2,1)}, u32[]{:S(2)}) copy-start(bf16[1,512,2048]{2,1,0:T(8,128)(2,1)} %param.34) | copy-start | bytes 6291460
  (89 other events, 1161.1 us)
Sparse Core Ops, SparseCore 0:
  9.6 19.4 all-gather.12
  31.8 124.9 all-gather.6
  158.3 14.8 all-gather.10
  174.6 16.7 all-gather.8
  192.8 16.7 all-gather.14
  266.8 148.9 reduce-scatter.6
  3667.8 121.2 all-gather.16
  3803.2 23.0 reduce-scatter.16
  3860.2 23.0 reduce-scatter.14
  3902.1 23.0 reduce-scatter.12
  3935.5 23.0 reduce-scatter.10
  3969.1 147.2 reduce-scatter.8
  4122.5 121.5 all-reduce.6
where the time goes:
time: 4270 us; the launch traced here: 4250 us
  waiting for transfers between devices  3310 us (78%)
  matrix products  403 us (9%)
  local copies, waits for them, and re-layouts  239 us (6%)
  other arithmetic  227 us (5%)
    all_to_all x2, waiting for transfers between devices, give_back(): lax.all_to_all(partial_rows.astype(jnp.bfloat16), ('expert', 'tensor'), s...  1340 us
    all_to_all x1, waiting for transfers between devices, per_device(): lax.all_to_all(dispatch_buffer(normed_two[token_of]), ('expert', 'tensor'...  721 us
    all_to_all x1, waiting for transfers between devices, per_device(): lax.all_to_all(dispatch_buffer(grad_expert), ('expert', 'tensor'), split_...  698 us
    dot_general x20, matrix products, outer_rows(): lax.dot_general(left_side, right_side, (((1,), (1,)), ((), ())), precisio...  171 us
    reduce_scatter x1, waiting for transfers between devices, per_device(): lax.psum_scatter(jnp.dot(attn_rows, out_full, preferred_element_type=jnp....  139 us
    all_gather x1, waiting for transfers between devices, per_device(): normed_all = lax.all_gather(normed_one, 'tensor', axis=0, tiled=True)  128 us
    all_gather x1, waiting for transfers between devices, per_device(): grad_branch_all = lax.all_gather(grad_branch, 'tensor', axis=0, tiled=True)  121 us
    dot_general x16, matrix products, inner_rows(): lax.dot_general(left_side, right_side, (((0,), (0,)), ((), ())), precisio...  111 us
  transfers between devices with their start and end apart: 17, of which 12 were waited for; matrix products, arithmetic and copies ran while one was open for 14% of the time, Pallas kernels for 0%

commit v1 on v0

v1 whole, which is shorter than its diff:
```python
import jax
import jax.numpy as jnp
from jax import lax
from jax.sharding import PartitionSpec as P

WIN = 1024


EPSILON = 1e-05
THETA = 50000.0
MASKED = -1e30
HIGH = lax.Precision.HIGHEST
LOW = jnp.bfloat16
FULL = jnp.float32


def inner_rows(left_side, right_side, precision=None):
    return lax.dot_general(
        left_side,
        right_side,
        (((0,), (0,)), ((), ())),
        precision=precision,
        preferred_element_type=jnp.float32,
    )


def outer_rows(left_side, right_side, precision=None):
    return lax.dot_general(
        left_side,
        right_side,
        (((1,), (1,)), ((), ())),
        precision=precision,
        preferred_element_type=jnp.float32,
    )


def plain_dot(left_side, right_side):
    return jnp.dot(left_side, right_side, preferred_element_type=jnp.float32)


def rope_tables(length, head_size):
    half_size = head_size // 2
    frequency = THETA ** (-2.0 * jnp.arange(half_size, dtype=jnp.float32) / head_size)
    angles = jnp.arange(length, dtype=jnp.float32)[:, None] * frequency[None, :]
    return (jnp.cos(angles), jnp.sin(angles))


def qk_prepare(projected, gain_vec, cos_part, sin_part):
    scaled = (
        projected
        * lax.rsqrt(jnp.mean(projected * projected, axis=-1, keepdims=True) + EPSILON)
        * gain_vec
    )
    half_size = scaled.shape[-1] // 2
    first_half = scaled[..., :half_size]
    second = scaled[..., half_size:]
    return jnp.concatenate(
        [first_half * cos_part - second * sin_part, second * cos_part + first_half * sin_part],
        axis=-1,
    )


def allowed_pairs(seg_row, position):
    same = seg_row[:, None] == seg_row[None, :]
    if position.shape[0] > WIN:
        same = same & (jnp.abs(position[:, None] - position[None, :]) < WIN)
    return same


def attend_item(item_list, mask):
    query_block, key_block, value_block = item_list
    scaling = query_block.shape[-1] ** (-0.5)
    scores = outer_rows(query_block, key_block) * scaling
    scores = jnp.where(mask, scores, MASKED)
    row_max = jnp.max(scores, axis=-1, keepdims=True)
    exponent = jnp.exp(scores - row_max)
    row_total = jnp.sum(exponent, axis=-1, keepdims=True)
    prob_vals = (exponent / row_total).astype(jnp.bfloat16)
    attended = jnp.dot(prob_vals, value_block, preferred_element_type=jnp.float32)
    return (attended.astype(LOW), (row_max + jnp.log(row_total))[:, 0])


def attend_back(item_list, mask):
    query_block, key_block, value_block, grad_block, log_total = item_list
    scaling = query_block.shape[-1] ** (-0.5)
    scores = outer_rows(query_block, key_block) * scaling
    prob_vals = jnp.where(mask, jnp.exp(scores - log_total[:, None]), 0.0)
    grad_prob = outer_rows(grad_block, value_block).astype(jnp.bfloat16).astype(jnp.float32)
    grad_value = inner_rows(prob_vals.astype(jnp.bfloat16), grad_block)
    centre = jnp.sum(prob_vals * grad_prob, axis=-1, keepdims=True)
    grad_score = (prob_vals * (grad_prob - centre)).astype(jnp.bfloat16)
    grad_query = jnp.dot(grad_score, key_block, preferred_element_type=jnp.float32) * scaling
    grad_key = inner_rows(grad_score, query_block) * scaling
    return (grad_query, grad_key, grad_value)


class Ring:
    def __init__(self, axis, size, count):
        self.axis, self.count = axis, count
        self.order = list(range(0, count, 2)) + list(range(count - 1, 0, -2))
        self.rightward = [
            (base + self.order[k], base + self.order[(k + 1) % count])
            for base in range(0, size, count)
            for k in range(count)
        ]
        self.leftward = [(to, start) for start, to in self.rightward]

    def right(self, value):
        return jax.tree.map(lambda v: lax.ppermute(v, self.axis, self.rightward), value)

    def left(self, value):
        return jax.tree.map(lambda v: lax.ppermute(v, self.axis, self.leftward), value)

    def members(self, place):
        order = jnp.array(self.order, jnp.int32)
        spot = jnp.argmax(order == place).astype(jnp.int32)
        shifts = [0]
        for k in range(1, self.count // 2):
            shifts += [-k, k]
        shifts.append(self.count // 2)
        return order[(spot + jnp.array(shifts, jnp.int32)) % self.count]

    def gather(self, value):
        from_left = from_right = value
        blocks = [value]
        for _ in range(1, self.count // 2):
            from_left, from_right = self.right(from_left), self.left(from_right)
            blocks += [from_left, from_right]
        upper = self.right(jax.tree.map(lambda v: v[: v.shape[0] // 2], from_left))
        lower = self.left(jax.tree.map(lambda v: v[v.shape[0] // 2 :], from_right))
        blocks.append(jax.tree.map(lambda u, v: jnp.concatenate([u, v]), upper, lower))
        return blocks

    def scatter(self, blocks):
        half = blocks[-1].shape[0] // 2
        from_left, from_right = self.right(blocks[-1][:half]), self.left(blocks[-1][half:])
        for k in range(self.count // 2 - 1, 0, -1):
            on_left, on_right = blocks[2 * k - 1], blocks[2 * k]
            if from_left.shape[0] == half:
                to_right = jnp.concatenate([on_right[:half] + from_left, on_right[half:]])
                to_left = jnp.concatenate([on_left[:half], on_left[half:] + from_right])
            else:
                to_right, to_left = on_right + from_left, on_left + from_right
            from_left, from_right = self.right(to_right), self.left(to_left)
        return blocks[0].astype(FULL) + from_left.astype(FULL) + from_right.astype(FULL)


def everywhere(value):
    for axis in ("expert", "tensor"):
        size, step = lax.axis_size(axis), 1
        while step < size:
            pairs = [(i, i ^ step) for i in range(size)]
            value = jax.tree.map(lambda v: v + lax.ppermute(v, axis, pairs), value)
            step *= 2
    return value


def expert_chunk(rows, grad_out, gates, gate_mat, up_mat, down_mat):
    gate_pre, up_pre = plain_dot(rows, gate_mat), plain_dot(rows, up_mat)
    sigmoid_val = jax.nn.sigmoid(gate_pre)
    silu_val = gate_pre * sigmoid_val
    activation = (silu_val * up_pre).astype(LOW).astype(FULL)
    plain_grad = outer_rows(grad_out, down_mat)
    grad_gates = jnp.sum(activation * plain_grad, axis=-1)
    grad_act = gates[:, None] * plain_grad
    grad_gate_pre = (
        grad_act * up_pre * sigmoid_val * (1.0 + gate_pre * (1.0 - sigmoid_val))
    ).astype(LOW)
    grad_up_pre = (grad_act * silu_val).astype(LOW)
    weighted = (gates[:, None] * activation).astype(LOW)
    grad_rows = outer_rows(grad_gate_pre, gate_mat) + outer_rows(grad_up_pre, up_mat)
    mixed = plain_dot(weighted, down_mat)
    return mixed, grad_rows, grad_gates, weighted, grad_gate_pre, grad_up_pre


def per_device(
    tokens,
    segments,
    routes,
    norm_gain,
    w_query,
    w_key,
    w_value,
    query_gain,
    key_gain,
    w_out,
    mix_gain,
    w_router,
    w_gate,
    w_up,
    w_down,
    cotangent,
):
    group_count, tensor_count = lax.axis_size("expert"), lax.axis_size("tensor")
    expert_count = w_router.shape[1]
    tok_rows, model_width = tokens.shape
    seq_count, length = segments.shape
    head_size = query_gain.shape[0]
    part_count = tensor_count // seq_count
    block_width = w_query.shape[1]
    local_width = seq_count * block_width
    heads_here = local_width // head_size
    group_at, tensor_at = lax.axis_index("expert"), lax.axis_index("tensor")
    seq_at, part_at = tensor_at // part_count, tensor_at % part_count
    whole_ring = Ring("tensor", tensor_count, tensor_count)
    seq_ring = Ring("tensor", tensor_count, part_count)

    def swap(value, axis, pairs):
        return lax.ppermute(value, axis, pairs)

    core_pairs = [(i, i ^ 1) for i in range(group_count)]

    def chip_pairs(shift):
        return [(i, (i + 2 * shift) % group_count) for i in range(group_count)]

    def seq_pairs(shift):
        return [(t, (t + part_count * shift) % tensor_count) for t in range(tensor_count)]

    def blocks_of(value, axis):
        return jnp.concatenate(
            [value] + [swap(value, "tensor", seq_pairs(s)) for s in range(1, seq_count)], axis=axis
        )

    inputs = tokens.astype(jnp.float32)
    inv_one = lax.rsqrt(jnp.mean(inputs * inputs, axis=-1, keepdims=True) + EPSILON)
    unit_one = inputs * inv_one
    normed_one = (unit_one * norm_gain).astype(jnp.bfloat16)
    query_full, key_full, value_full = (
        lax.all_gather(blocks_of(w, 1), "expert", axis=0, tiled=True)
        for w in (w_query, w_key, w_value)
    )
    out_full = lax.all_gather(blocks_of(w_out, 0), "expert", axis=1, tiled=True)
    normed_all = jnp.concatenate(seq_ring.gather(normed_one))

    members = seq_ring.members(part_at)
    cos_part, sin_part = (
        table.reshape(part_count, tok_rows, 1, head_size // 2)[members].reshape(
            length, 1, head_size // 2
        )
        for table in rope_tables(length, head_size)
    )
    seg_row = segments[seq_at].reshape(part_count, tok_rows)[members].reshape(length)
    position = (
        jnp.arange(length, dtype=jnp.int32).reshape(part_count, tok_rows)[members].reshape(length)
    )
    mask = allowed_pairs(seg_row, position)
    shape_heads = (length, heads_here, head_size)

    query_proj = plain_dot(normed_all, query_full).reshape(shape_heads)
    key_proj = plain_dot(normed_all, key_full).reshape(shape_heads)
    value_low = plain_dot(normed_all, value_full).astype(LOW).reshape(shape_heads)
    query_low = qk_prepare(query_proj, query_gain, cos_part, sin_part).astype(LOW)
    key_low = qk_prepare(key_proj, key_gain, cos_part, sin_part).astype(LOW)

    def to_items(heads_arr):
        return heads_arr.transpose(1, 0, 2)

    def from_items(item_arr):
        return item_arr.transpose(1, 0, 2)

    query_items, key_items, value_items = map(to_items, (query_low, key_low, value_low))
    attended, log_total = lax.map(
        lambda items: attend_item(items, mask), (query_items, key_items, value_items)
    )
    attn_rows = from_items(attended).reshape(length, local_width)
    partial_branch = [
        plain_dot(attn_rows[k * tok_rows : (k + 1) * tok_rows], out_full).astype(LOW)
        for k in range(part_count)
    ]
    residual = inputs + seq_ring.scatter(partial_branch)
    inv_two = lax.rsqrt(jnp.mean(residual * residual, axis=-1, keepdims=True) + EPSILON)
    unit_two = residual * inv_two
    normed_two = (unit_two * mix_gain).astype(jnp.bfloat16)
    logits = jnp.dot(normed_two, w_router, preferred_element_type=jnp.float32)
    hits = jnp.any(
        routes[:, :, None] == jnp.arange(expert_count, dtype=jnp.int32)[None, None, :], axis=1
    )
    top_logit = jnp.max(jnp.where(hits, logits, MASKED), axis=-1, keepdims=True)
    raised = jnp.where(hits, jnp.exp(logits - top_logit), 0.0)
    gate_table = raised / jnp.sum(raised, axis=-1, keepdims=True)

    grad_out = cotangent.astype(jnp.float32)
    cot_blocks = whole_ring.gather(cotangent)
    row_blocks = whole_ring.gather(normed_two)
    gate_blocks = whole_ring.gather(gate_table)
    slabs = []
    for shift in range(group_count // 2):
        mine = [
            w[0] if shift == 0 else swap(w[0], "expert", chip_pairs(shift))
            for w in (w_gate, w_up, w_down)
        ]
        theirs = [swap(w, "expert", core_pairs) for w in mine]
        for cross, mats in ((0, mine), (1, theirs)):
            chip = (group_at // 2 - shift) % (group_count // 2)
            owner = (chip * 2 + (group_at % 2 ^ cross)) * tensor_count + tensor_at
            slabs.append((mats, owner // 2))
    block_count = len(row_blocks)
    mixed_parts, grad_row_parts, grad_gate_parts = [], [], []
    kept = [[] for _ in slabs]
    for k in range(block_count):
        mixed, grad_rows, grad_table = 0.0, 0.0, 0.0
        for s, (mats, expert_at) in enumerate(slabs):
            column = jnp.arange(expert_count) == expert_at
            gates = jnp.sum(jnp.where(column[None, :], gate_blocks[k], 0.0), axis=1)
            mixed_s, rows_s, gates_s, *keep = expert_chunk(
                row_blocks[k], cot_blocks[k], gates, *mats
            )
            mixed, grad_rows = mixed + mixed_s, grad_rows + rows_s
            grad_table = grad_table + jnp.where(column[None, :], gates_s[:, None], 0.0)
            kept[s].append(keep)
        mixed_parts.append(mixed.astype(LOW))
        grad_row_parts.append(grad_rows.astype(LOW))
        grad_gate_parts.append(grad_table)
    grad_gates = whole_ring.scatter(grad_gate_parts)
    grad_rows_sum = whole_ring.scatter(grad_row_parts)
    mixture = whole_ring.scatter(mixed_parts)
    layer_out = (residual + mixture).astype(jnp.bfloat16)

    all_rows, all_cot = jnp.concatenate(row_blocks), jnp.concatenate(cot_blocks)
    slab_grads = []
    for keep in kept:
        weighted, grad_gate_pre, grad_up_pre = (
            jnp.concatenate([block[part] for block in keep]) for part in range(3)
        )
        slab_grads.append(
            [
                inner_rows(all_rows, grad_gate_pre).astype(LOW),
                inner_rows(all_rows, grad_up_pre).astype(LOW),
                inner_rows(weighted, all_cot).astype(LOW),
            ]
        )
    expert_grads = [0.0, 0.0, 0.0]
    for shift in range(group_count // 2):
        for part in range(3):
            chip_sum = slab_grads[2 * shift][part].astype(FULL) + swap(
                slab_grads[2 * shift + 1][part], "expert", core_pairs
            ).astype(FULL)
            if shift:
                chip_sum = swap(chip_sum.astype(LOW), "expert", chip_pairs(-shift)).astype(FULL)
            expert_grads[part] = expert_grads[part] + chip_sum

    grad_logits = gate_table * (
        grad_gates - jnp.sum(gate_table * grad_gates, axis=-1, keepdims=True)
    )
    grad_normed_two = grad_rows_sum + outer_rows(grad_logits, w_router.astype(jnp.float32), HIGH)
    grad_router = inner_rows(grad_logits, normed_two.astype(jnp.float32), HIGH)
    grad_unit_two = grad_normed_two * mix_gain
    grad_mix_gain = jnp.sum(grad_normed_two * unit_two, axis=0)
    grad_residual = grad_out + inv_two * (
        grad_unit_two - unit_two * jnp.mean(grad_unit_two * unit_two, axis=-1, keepdims=True)
    )
    grad_branch = grad_residual.astype(jnp.bfloat16)
    grad_branch_all = jnp.concatenate(seq_ring.gather(grad_branch))
    grad_w_out = inner_rows(attn_rows, grad_branch_all)
    grad_attn = outer_rows(grad_branch_all, out_full).astype(jnp.bfloat16)
    grad_items = to_items(grad_attn.reshape(shape_heads))
    grad_query_items, grad_key_items, grad_value_items = lax.map(
        lambda items: attend_back(items, mask),
        (query_items, key_items, value_items, grad_items, log_total),
    )
    grad_value_rows = from_items(grad_value_items).reshape(length, local_width).astype(LOW)

    def prepare_heads(projected, gain_vec):
        return qk_prepare(projected, gain_vec, cos_part, sin_part)

    unused_query, pull_query = jax.vjp(prepare_heads, query_proj, query_gain)
    grad_query_proj, grad_query_gain = pull_query(from_items(grad_query_items))
    unused_key, pull_key = jax.vjp(prepare_heads, key_proj, key_gain)
    grad_key_proj, grad_key_gain = pull_key(from_items(grad_key_items))
    grad_query_low = grad_query_proj.reshape(length, local_width).astype(LOW)
    grad_key_low = grad_key_proj.reshape(length, local_width).astype(LOW)
    partial_normed = [
        (
            outer_rows(grad_query_low[rows], query_full)
            + outer_rows(grad_key_low[rows], key_full)
            + outer_rows(grad_value_rows[rows], value_full)
        ).astype(LOW)
        for rows in (slice(k * tok_rows, (k + 1) * tok_rows) for k in range(part_count))
    ]
    grad_normed_one = seq_ring.scatter(partial_normed)
    grad_weights = [
        inner_rows(normed_all, grad) for grad in (grad_query_low, grad_key_low, grad_value_rows)
    ]
    grad_norm_gain = sum(
        jnp.sum(grad * full.astype(FULL), axis=1)
        for grad, full in zip(grad_weights, (query_full, key_full, value_full))
    ) / norm_gain

    def own_part(grad, axis):
        spread = lax.psum_scatter(
            grad.astype(LOW), "expert", scatter_dimension=1 - axis, tiled=True
        )
        blocks = jnp.split(spread, seq_count, axis=axis)
        total = blocks[0].astype(FULL)
        for s in range(1, seq_count):
            total = total + swap(blocks[s], "tensor", seq_pairs(-s)).astype(FULL)
        return total

    owned_query, owned_key, owned_value = (own_part(grad, 1) for grad in grad_weights)
    owned_out = own_part(grad_w_out, 0)
    grad_unit_one = grad_normed_one * norm_gain
    grad_tokens = grad_residual + inv_one * (
        grad_unit_one - unit_one * jnp.mean(grad_unit_one * unit_one, axis=-1, keepdims=True)
    )
    early_router, early_mix = everywhere((grad_router, grad_mix_gain))
    late_norm, late_query, late_key = everywhere((grad_norm_gain, grad_query_gain, grad_key_gain))
    return (
        layer_out,
        grad_tokens.astype(jnp.bfloat16),
        late_norm,
        owned_query,
        owned_key,
        owned_value,
        late_query,
        late_key,
        owned_out,
        early_mix,
        early_router.T,
        expert_grads[0][None],
        expert_grads[1][None],
        expert_grads[2][None],
    )


def solution(mesh):
    in_specs = (
        P(("expert", "tensor"), None),
        P("expert", None),
        P(("expert", "tensor"), None),
        P(),
        P("expert", "tensor"),
        P("expert", "tensor"),
        P("expert", "tensor"),
        P(),
        P(),
        P("tensor", "expert"),
        P(),
        P(),
        P(("expert", "tensor"), None, None),
        P(("expert", "tensor"), None, None),
        P(("expert", "tensor"), None, None),
        P(("expert", "tensor"), None),
    )
    out_specs = (
        P(("expert", "tensor"), None),
        P(("expert", "tensor"), None),
        P(),
        P("expert", "tensor"),
        P("expert", "tensor"),
        P("expert", "tensor"),
        P(),
        P(),
        P("tensor", "expert"),
        P(),
        P(),
        P(("expert", "tensor"), None, None),
        P(("expert", "tensor"), None, None),
        P(("expert", "tensor"), None, None),
    )
    return jax.shard_map(
        per_device, mesh=mesh, in_specs=in_specs, out_specs=out_specs, check_vma=False
    )
```

time: 4270 us -> 1400 us (0.33)
  waiting for transfers between devices: 3310 us -> 397 us
  matrix products: 403 us -> 621 us
  local copies, waits for them, and re-layouts: 239 us -> 119 us
  other arithmetic: 227 us -> 116 us
  starting transfers between devices: 18.5 us -> 117 us
    all_to_all x4 -> x0, waiting for transfers between devices: 2760 us -> none  [the longest x2 1340 us: give_back(): lax.all_to_all(partial_rows.astype(jnp.bfloat16), ('expert', 'tensor'), s...]
    ppermute x0 -> x115, waiting for transfers between devices: none -> 397 us  [the longest x32 184 us: left(): lax.ppermute(v, self.axis, self.leftward)]
    all_gather x6 -> x4, waiting for transfers between devices: 267 us -> 0.03 us  [the longest x3 0.02 us: per_device(): lax.all_gather(blocks_of(w, 1), 'expert', axis=0, tiled=True)]
    reduce_scatter x6 -> x4, waiting for transfers between devices: 205 us -> 0.01 us  [own_part(): lax.psum_scatter(grad.astype(LOW), 'expert', scatter_dimension=1 - axis,...]
    ppermute x0 -> x115, starting transfers between devices: none -> 117 us  [the longest x32 37 us: right(): lax.ppermute(v, self.axis, self.rightward)]
    dot_general x20 -> x122, matrix products: 171 us -> 272 us  [outer_rows(): lax.dot_general(left_side, right_side, (((1,), (1,)), ((), ())), precisio...]
    gather x2 -> x4, local copies, waits for them, and re-layouts: 101 us -> 2.33 us  [the longest x2 1.13 us: per_device(): table.reshape(part_count, tok_rows, 1, head_size // 2)[members]]
    reduce_sum x11 -> x2, other arithmetic: 89.6 us -> 0.22 us  [the longest x1 0.19 us: per_device(): jnp.sum(gate_table * grad_gates, axis=-1, keepdims=True)]
  transfers between devices with their start and end apart: 17 -> 123, of which waited for: 12 -> 46; matrix products, arithmetic and copies ran while one was open for 14% -> 58% of each run, Pallas kernels for 0% -> 0%
where the time goes in v1:
time: 1400 us; the launch traced here: 1390 us
  matrix products  621 us (44%)
  waiting for transfers between devices  397 us (28%)
  local copies, waits for them, and re-layouts  119 us (8%)
  starting transfers between devices  117 us (8%)
  other arithmetic  116 us (8%)
  between operations  18.9 us (1%)
    dot_general x122, matrix products, outer_rows(): lax.dot_general(left_side, right_side, (((1,), (1,)), ((), ())), precisio...  272 us
    ppermute x32, waiting for transfers between devices, left(): lax.ppermute(v, self.axis, self.leftward)  184 us
    dot_general x103, matrix products, plain_dot(): return jnp.dot(left_side, right_side, preferred_element_type=jnp.float32)  182 us
    dot_general x25, matrix products, inner_rows(): lax.dot_general(left_side, right_side, (((0,), (0,)), ((), ())), precisio...  146 us
    ppermute x26, waiting for transfers between devices, swap(): return lax.ppermute(value, axis, pairs)  90.4 us
    ppermute x32, waiting for transfers between devices, right(): lax.ppermute(v, self.axis, self.rightward)  75.3 us
    unnamed x727, local copies, waits for them, and re-layouts  60.3 us
    ppermute x25, waiting for transfers between devices, everywhere(): value = jax.tree.map(lambda v: v + lax.ppermute(v, axis, pairs), value)  47 us
  transfers between devices with their start and end apart: 123, of which 46 were waited for; matrix products, arithmetic and copies ran while one was open for 58% of the time, Pallas kernels for 0%

profile of v1, /device:TPU:0, one launch (start us, length us, event | category | flops | bytes accessed | tf_op | source)
XLA Modules:
  0.0 1389.4 jit_solution(8153572687901311921)
XLA Ops:
  12.5 11.9 collective-permute-done.5
  25.6 14.0 %collective-permute-done.4 = bf16[512,256]{0,1:T(8,128)(2,1)S(1)} collective-permute-done((bf16[512,256]{0,1:T(8,128)(2,1)S(1)}, bf16[512,256]{0,1:T(8,128)(2,1)S(1)}, u32[]{:S(2)}, u32[]{:S(2)}) %collective-permute-start.4) | collective-permute-done | bytes 262176 | tf_op jit(solution)/shard_map/ppermute | solution.py:209
  40.7 13.1 collective-permute-done.6
  61.5 25.1 %collective-permute-done.45 = bf16[256,2048]{1,0:T(8,128)(2,1)} collective-permute-done((bf16[256,2048]{1,0:T(8,128)(2,1)S(1)}, bf16[256,2048]{1,0:T(8,128)(2,1)}, u32[]{:S(2)}, u32[]{:S(2)}) %collective-permute-start.45) | collective-permute-done | bytes 1048608 | tf_op jit(solution)/shard_map/ppermute | solution.py:112
  94.3 10.1 collective-permute-done
  108.8 21.6 %collective-permute-done.46 = bf16[256,2048]{1,0:T(8,128)(2,1)} collective-permute-done((bf16[256,2048]{1,0:T(8,128)(2,1)}, bf16[256,2048]{1,0:T(8,128)(2,1)}, u32[]{:S(2)}, u32[]{:S(2)}) %collective-permute-start.46) | collective-permute-done | bytes 1048608 | tf_op jit(solution)/shard_map/ppermute | solution.py:112
  145.2 20.6 %collective-permute-done.3 = bf16[128,2048]{1,0:T(8,128)(2,1)S(1)} collective-permute-done((bf16[128,2048]{1,0:T(8,128)(2,1)S(1)}, bf16[128,2048]{1,0:T(8,128)(2,1)S(1)}, u32[]{:S(2)}, u32[]{:S(2)}) %collective-permute-start.3) | collective-permute-done | bytes 524320 | tf_op jit(solution)/shard_map/ppermute | solution.py:112
  200.8 37.0 %while.28 = (s32[]{:T(128)}, bf16[4,1024,128]{1,2,0:T(8,128)(2,1)}, f32[4,1024]{1,0:T(4,128)}, bf16[4,1024,128]{2,1,0:T(8,128)(2,1)}, bf16[4,1024,128]{2,1,0:T(8...) while((s32[]{:T(128)}, bf16[4,1024,128]{1,2,0:T(8,128)(2,1)}, ...), condition=%wide.region_7.8_spmd.clone, body=%wide.region_4.7_spmd.clone.sunk | while | flops 552729600 | bytes 14742641 | solution.py:262
  271.6 17.6 %collective-permute-done.11 = bf16[256,2048]{1,0:T(8,128)(2,1)} collective-permute-done((bf16[256,2048]{1,0:T(8,128)(2,1)}, bf16[256,2048]{1,0:T(8,128)(2,1)}, u32[]{:S(2)}, u32[]{:S(2)}) %collective-permute-start.11) | collective-permute-done | bytes 1048608 | tf_op jit(solution)/shard_map/ppermute | solution.py:112
  321.9 17.7 %collective-permute-done.23 = f32[256,16]{0,1:T(8,128)S(1)} collective-permute-done((f32[256,16]{0,1:T(8,128)S(1)}, f32[256,16]{0,1:T(8,128)S(1)}, u32[]{:S(2)}, u32[]{:S(2)}) %collective-permute-start.23) | collective-permute-done | bytes 16416 | tf_op jit(solution)/shard_map/ppermute | solution.py:112
  660.2 10.0 convolution_convert_fusion.11
  718.3 9.9 convolution_convert_fusion.9
  897.5 22.8 %collective-permute-done.105 = f32[16,2048]{1,0:T(8,128)S(1)} collective-permute-done((f32[16,2048]{1,0:T(8,128)S(1)}, f32[16,2048]{1,0:T(8,128)S(1)}, u32[]{:S(2)}, u32[]{:S(2)}) %collective-permute-start.105) | collective-permute-done | bytes 131104 | tf_op jit(solution)/shard_map/ppermute | solution.py:153
  927.1 19.7 %collective-permute-done.42 = bf16[256,2048]{1,0:T(8,128)(2,1)} collective-permute-done((bf16[256,2048]{1,0:T(8,128)(2,1)}, bf16[256,2048]{1,0:T(8,128)(2,1)}, u32[]{:S(2)}, u32[]{:S(2)}) %collective-permute-start.42) | collective-permute-done | bytes 1048608 | tf_op jit(solution)/shard_map/ppermute | solution.py:112
  950.7 15.4 %collective-permute-done.59 = bf16[256,2048]{1,0:T(8,128)(2,1)S(1)} collective-permute-done((bf16[256,2048]{1,0:T(8,128)(2,1)S(1)}, bf16[256,2048]{1,0:T(8,128)(2,1)S(1)}, u32[]{:S(2)}, u32[]{:S(2)}) %collective-permute-start.59) | collective-permute-done | bytes 1048608 | tf_op jit(solution)/shard_map/ppermute | solution.py:112
  977.6 15.4 %collective-permute-done.60 = bf16[256,2048]{1,0:T(8,128)(2,1)S(1)} collective-permute-done((bf16[256,2048]{1,0:T(8,128)(2,1)S(1)}, bf16[256,2048]{1,0:T(8,128)(2,1)S(1)}, u32[]{:S(2)}, u32[]{:S(2)}) %collective-permute-start.60) | collective-permute-done | bytes 1048608 | tf_op jit(solution)/shard_map/ppermute | solution.py:112
  998.2 16.8 %collective-permute-done.43 = bf16[256,2048]{1,0:T(8,128)(2,1)S(1)} collective-permute-done((bf16[256,2048]{1,0:T(8,128)(2,1)}, bf16[256,2048]{1,0:T(8,128)(2,1)S(1)}, u32[]{:S(2)}, u32[]{:S(2)}) %collective-permute-start.43) | collective-permute-done | bytes 1048608 | tf_op jit(solution)/shard_map/ppermute | solution.py:112
  1023.3 16.6 %collective-permute-done.69 = bf16[256,2048]{1,0:T(8,128)(2,1)S(1)} collective-permute-done((bf16[256,2048]{1,0:T(8,128)(2,1)S(1)}, bf16[256,2048]{1,0:T(8,128)(2,1)S(1)}, u32[]{:S(2)}, u32[]{:S(2)}) %collective-permute-start.69) | collective-permute-done | bytes 1048608 | tf_op jit(solution)/shard_map/ppermute | solution.py:109
  1058.5 65.0 %while.29 = (s32[]{:T(128)}, f32[4,1024,128]{1,2,0:T(8,128)}, f32[4,1024,128]{1,2,0:T(8,128)}, bf16[4,1024,128]{1,2,0:T(8,128)(2,1)}, bf16[4,1024,128]{2,1,0:T(8...) while((s32[]{:T(128)}, f32[4,1024,128]{1,2,0:T(8,128)}, ...), condition=%wide.region_80.81_spmd.clone, body=%wide.region_78.80_spmd.clone.sunk | while | flops 1356069888 | bytes 66354448 | solution.py:357
  1194.4 17.2 %collective-permute-done.40 = bf16[256,2048]{1,0:T(8,128)(2,1)S(1)} collective-permute-done((bf16[256,2048]{1,0:T(8,128)(2,1)S(1)}, bf16[256,2048]{1,0:T(8,128)(2,1)S(1)}, u32[]{:S(2)}, u32[]{:S(2)}) %collective-permute-start.40) | collective-permute-done | bytes 1048608 | tf_op jit(solution)/shard_map/ppermute | solution.py:109
  1226.8 18.8 %collective-permute-done.111 = bf16[2048,512]{1,0:T(8,128)(2,1)} collective-permute-done((bf16[2048,512]{1,0:T(8,128)(2,1)}, bf16[2048,512]{1,0:T(8,128)(2,1)}, u32[]{:S(2)}, u32[]{:S(2)}) %collective-permute-start.111) | collective-permute-done | bytes 2097184 | tf_op jit(solution)/shard_map/ppermute | solution.py:209
  1306.2 13.8 collective-permute-done.94
  1334.6 15.8 %collective-permute-done.114 = bf16[512,2048]{1,0:T(8,128)(2,1)} collective-permute-done((bf16[512,2048]{1,0:T(8,128)(2,1)}, bf16[512,2048]{1,0:T(8,128)(2,1)}, u32[]{:S(2)}, u32[]{:S(2)}) %collective-permute-start.114) | collective-permute-done | bytes 2097184 | tf_op jit(solution)/shard_map/ppermute | solution.py:209
  1363.7 11.2 collective-permute-done.84
  (1474 shorter events, 1014.7 us)
Async XLA Ops:
  7.2 163.4 %all-gather.7.cloned.1.call-start = ((), (), s32[]{:S(2)}) async-start(), calls=%async_computation.5 | async-start | bytes 2621440 | tf_op jit(solution)/shard_map/all_gather | solution.py:229
  25.3 151.9 %all-gather.5.cloned.1.call-start = ((), (), s32[]{:S(2)}) async-start(), calls=%async_computation.4 | async-start | bytes 2621440 | tf_op jit(solution)/shard_map/all_gather | solution.py:229
  40.5 151.9 %all-gather.9.cloned.1.call-start = ((), (), s32[]{:S(2)}) async-start(), calls=%async_computation.6 | async-start | bytes 2621440 | tf_op jit(solution)/shard_map/all_gather | solution.py:229
  54.7 185.2 %all-gather.11.cloned.1.call-start = ((), (), s32[]{:S(2)}) async-start(), calls=%async_computation.7 | async-start | bytes 2621440 | tf_op jit(solution)/shard_map/all_gather | solution.py:232
  104.4 166.6 %collective-permute-start.16 = (bf16[2048,512]{1,0:T(8,128)(2,1)}, bf16[2048,512]{1,0:T(8,128)(2,1)}, u32[]{:S(2)}, u32[]{:S(2)}) collective-permute-start(bf16[2048,512]{1,0:T(8,128)(2,1)} %bitcast.16), channel_id=1, source_target_pairs={{0,16},{8,24},{16,0},{24,8},{1,17},{9,25},{17,1},{25,9},{2,18},{10... | collective-permute-start | bytes 6291464 | tf_op jit(solution)/shard_map/ppermute | solution.py:209
  135.5 1194.0 %reduce-scatter.5.cloned.1.call-start = ((), (), s32[]{:S(2)}) async-start(), calls=%async_computation.8 | async-start | bytes 2621440 | tf_op jit(solution)/shard_map/reduce_scatter | solution.py:390
  142.4 128.7 %collective-permute-start.15 = (bf16[2048,512]{1,0:T(8,128)(2,1)}, bf16[2048,512]{1,0:T(8,128)(2,1)}, u32[]{:S(2)}, u32[]{:S(2)}) collective-permute-start(bf16[2048,512]{1,0:T(8,128)(2,1)} %bitcast.15), channel_id=1, source_target_pairs={{0,16},{8,24},{16,0},{24,8},{1,17},{9,25},{17,1},{25,9},{2,18},{10... | collective-permute-start | bytes 6291464 | tf_op jit(solution)/shard_map/ppermute | solution.py:209
  165.8 105.7 %collective-permute-start.17 = (bf16[512,2048]{1,0:T(8,128)(2,1)S(1)}, bf16[512,2048]{1,0:T(8,128)(2,1)}, u32[]{:S(2)}, u32[]{:S(2)}) collective-permute-start(bf16[512,2048]{1,0:T(8,128)(2,1)S(1)} %bitcast.647), channel_id=1, source_target_pairs={{0,16},{8,24},{16,0},{24,8},{1,17},{9,25},{17,1},{25,9},{2,18},{10... | collective-permute-start | bytes 6291464 | tf_op jit(solution)/shard_map/ppermute | solution.py:209
  345.2 197.6 %collective-permute-start.31 = (f32[128,16]{0,1:T(8,128)S(1)}, f32[128,16]{0,1:T(8,128)S(1)}, u32[]{:S(2)}, u32[]{:S(2)}) collective-permute-start(f32[128,16]{0,1:T(8,128)S(1)} %slice.330), channel_id=1, source_target_pairs={{2,0},{4,2},{6,4},{7,6},{5,7},{3,5},{1,3},{0,1},{10,8},{12,10},{14... | collective-permute-start | bytes 24584 | tf_op jit(solution)/shard_map/ppermute | solution.py:112
  554.5 336.6 %collective-permute-start.41 = (bf16[128,2048]{1,0:T(8,128)(2,1)}, bf16[128,2048]{1,0:T(8,128)(2,1)}, u32[]{:S(2)}, u32[]{:S(2)}) collective-permute-start(bf16[128,2048]{1,0:T(8,128)(2,1)} %get-tuple-element.727), channel_id=1, source_target_pairs={{2,0},{4,2},{6,4},{7,6},{5,7},{3,5},{1,3},{0,1},{10,8},{12,10},{14... | collective-permute-start | bytes 1572872 | tf_op jit(solution)/shard_map/ppermute | solution.py:112
  556.1 336.6 %collective-permute-start.37 = (bf16[128,2048]{1,0:T(8,128)(2,1)}, bf16[128,2048]{1,0:T(8,128)(2,1)}, u32[]{:S(2)}, u32[]{:S(2)}) collective-permute-start(bf16[128,2048]{1,0:T(8,128)(2,1)} %get-tuple-element.726), channel_id=1, source_target_pairs={{0,2},{2,4},{4,6},{6,7},{7,5},{5,3},{3,1},{1,0},{8,10},{10,12},{12... | collective-permute-start | bytes 1572872 | tf_op jit(solution)/shard_map/ppermute | solution.py:109
  633.7 248.4 %collective-permute-start.57 = (bf16[128,2048]{1,0:T(8,128)(2,1)}, bf16[128,2048]{1,0:T(8,128)(2,1)}, u32[]{:S(2)}, u32[]{:S(2)}) collective-permute-start(bf16[128,2048]{1,0:T(8,128)(2,1)} %get-tuple-element.721), channel_id=1, source_target_pairs={{2,0},{4,2},{6,4},{7,6},{5,7},{3,5},{1,3},{0,1},{10,8},{12,10},{14... | collective-permute-start | bytes 1572872 | tf_op jit(solution)/shard_map/ppermute | solution.py:112
  640.1 243.8 %collective-permute-start.53 = (bf16[128,2048]{1,0:T(8,128)(2,1)}, bf16[128,2048]{1,0:T(8,128)(2,1)}, u32[]{:S(2)}, u32[]{:S(2)}) collective-permute-start(bf16[128,2048]{1,0:T(8,128)(2,1)} %get-tuple-element.720), channel_id=1, source_target_pairs={{0,2},{2,4},{4,6},{6,7},{7,5},{5,3},{3,1},{1,0},{8,10},{10,12},{12... | collective-permute-start | bytes 1572872 | tf_op jit(solution)/shard_map/ppermute | solution.py:109
  650.7 219.4 %collective-permute-start.101 = (f32[16,2048]{1,0:T(8,128)}, f32[16,2048]{1,0:T(8,128)}, u32[]{:S(2)}, u32[]{:S(2)}) collective-permute-start(f32[16,2048]{1,0:T(8,128)} %fusion.279), channel_id=1, source_target_pairs={{0,8},{8,0},{16,24},{24,16},{1,9},{9,1},{17,25},{25,17},{2,10},{10... | collective-permute-start | bytes 393224 | tf_op jit(solution)/shard_map/ppermute | solution.py:153
  882.2 85.9 %collective-permute-start.107 = (bf16[2048,512]{1,0:T(8,128)(2,1)}, bf16[2048,512]{1,0:T(8,128)(2,1)}, u32[]{:S(2)}, u32[]{:S(2)}) collective-permute-start(bf16[2048,512]{1,0:T(8,128)(2,1)} %convolution_convert_fusion.10), channel_id=1, source_target_pairs={{0,8},{8,0},{16,24},{24,16},{1,9},{9,1},{17,25},{25,17},{2,10},{10... | collective-permute-start | bytes 6291464 | tf_op jit(solution)/shard_map/ppermute | solution.py:209
  882.2 91.3 %collective-permute-start.110 = (bf16[2048,512]{1,0:T(8,128)(2,1)}, bf16[2048,512]{1,0:T(8,128)(2,1)}, u32[]{:S(2)}, u32[]{:S(2)}) collective-permute-start(bf16[2048,512]{1,0:T(8,128)(2,1)} %convolution_convert_fusion.6), channel_id=1, source_target_pairs={{0,8},{8,0},{16,24},{24,16},{1,9},{9,1},{17,25},{25,17},{2,10},{10... | collective-permute-start | bytes 6291464 | tf_op jit(solution)/shard_map/ppermute | solution.py:209
  949.8 271.0 %collective-permute-start.106 = (bf16[2048,512]{1,0:T(8,128)(2,1)}, bf16[2048,512]{1,0:T(8,128)(2,1)}, u32[]{:S(2)}, u32[]{:S(2)}) collective-permute-start(bf16[2048,512]{1,0:T(8,128)(2,1)} %convolution_convert_fusion.12), channel_id=1, source_target_pairs={{0,8},{8,0},{16,24},{24,16},{1,9},{9,1},{17,25},{25,17},{2,10},{10... | collective-permute-start | bytes 6291464 | tf_op jit(solution)/shard_map/ppermute | solution.py:209
  966.1 260.7 %collective-permute-start.109 = (bf16[2048,512]{1,0:T(8,128)(2,1)}, bf16[2048,512]{1,0:T(8,128)(2,1)}, u32[]{:S(2)}, u32[]{:S(2)}) collective-permute-start(bf16[2048,512]{1,0:T(8,128)(2,1)} %convolution_convert_fusion.8), channel_id=1, source_target_pairs={{0,8},{8,0},{16,24},{24,16},{1,9},{9,1},{17,25},{25,17},{2,10},{10... | collective-permute-start | bytes 6291464 | tf_op jit(solution)/shard_map/ppermute | solution.py:209
  994.4 226.5 %collective-permute-start.108 = (bf16[2048,512]{1,0:T(8,128)(2,1)}, bf16[2048,512]{1,0:T(8,128)(2,1)}, u32[]{:S(2)}, u32[]{:S(2)}) collective-permute-start(bf16[2048,512]{1,0:T(8,128)(2,1)} %add_convert_fusion.2), channel_id=1, source_target_pairs={{0,16},{8,24},{16,0},{24,8},{1,17},{9,25},{17,1},{25,9},{2,18},{10... | collective-permute-start | bytes 6291464 | tf_op jit(solution)/shard_map/ppermute | solution.py:209
  1052.9 133.5 %collective-permute-start.44 = (bf16[256,2048]{1,0:T(8,128)(2,1)}, bf16[256,2048]{1,0:T(8,128)(2,1)}, u32[]{:S(2)}, u32[]{:S(2)}) collective-permute-start(bf16[256,2048]{1,0:T(8,128)(2,1)} %fusion.120), channel_id=1, source_target_pairs={{2,0},{4,2},{6,4},{7,6},{5,7},{3,5},{1,3},{0,1},{10,8},{12,10},{14... | collective-permute-start | bytes 3145736 | tf_op jit(solution)/shard_map/ppermute | solution.py:112
  1055.3 89.5 %collective-permute-start.96 = (f32[2048]{0:T(1024)S(1)}, f32[2048]{0:T(1024)S(1)}, u32[]{:S(2)}, u32[]{:S(2)}) collective-permute-start(f32[2048]{0:T(1024)S(1)} %get-tuple-element.291), channel_id=1, source_target_pairs={{0,8},{8,0},{16,24},{24,16},{1,9},{9,1},{17,25},{25,17},{2,10},{10... | collective-permute-start | bytes 24584 | tf_op jit(solution)/shard_map/ppermute | solution.py:153
  1133.6 199.8 %reduce-scatter.7.cloned.1.call-start = ((), (), s32[]{:S(2)}) async-start(), calls=%async_computation.9 | async-start | bytes 2621440 | tf_op jit(solution)/shard_map/reduce_scatter | solution.py:390
  1163.9 192.6 %reduce-scatter.9.cloned.1.call-start = ((), (), s32[]{:S(2)}) async-start(), calls=%async_computation.10 | async-start | bytes 2621440 | tf_op jit(solution)/shard_map/reduce_scatter | solution.py:390
  1220.8 137.6 %reduce-scatter.11.cloned.1.call-start = ((), (), s32[]{:S(2)}) async-start(), calls=%async_computation.11 | async-start | bytes 2621440 | tf_op jit(solution)/shard_map/reduce_scatter | solution.py:390
  (467 other events, 8936.2 us)
Sparse Core Ops, SparseCore 0:
  25.4 23.7 all-gather.6
  51.4 22.5 all-gather.4
  76.1 22.5 all-gather.8
  135.6 32.1 all-gather.10
  1133.7 30.8 reduce-scatter.4
  1167.1 39.9 reduce-scatter.6
  1220.9 33.8 reduce-scatter.8
  1264.9 30.5 reduce-scatter.10

commit v2 on v1

v2 whole, which is shorter than its diff:
```python
import functools

import jax
import jax.numpy as jnp
import numpy as np
from jax import lax
from jax.experimental import pallas as pl
from jax.experimental.pallas import tpu as pltpu
from jax.sharding import PartitionSpec as P

WIN = 1024


EPSILON = 1e-05
THETA = 50000.0
MASKED = -1e30
HIGH = lax.Precision.HIGHEST
LOW = jnp.bfloat16
FULL = jnp.float32
ROOM = 58 << 20
ANYWHERE = pl.BlockSpec(memory_space=pl.ANY)
NEAR = pl.BlockSpec(memory_space=pltpu.VMEM)
Shape = jax.ShapeDtypeStruct


def inner_rows(left_side, right_side, precision=None):
    return lax.dot_general(
        left_side,
        right_side,
        (((0,), (0,)), ((), ())),
        precision=precision,
        preferred_element_type=jnp.float32,
    )


def outer_rows(left_side, right_side, precision=None):
    return lax.dot_general(
        left_side,
        right_side,
        (((1,), (1,)), ((), ())),
        precision=precision,
        preferred_element_type=jnp.float32,
    )


def plain_dot(left_side, right_side):
    return jnp.dot(left_side, right_side, preferred_element_type=jnp.float32)


def cost(flops, moved, exps=0):
    return pl.CostEstimate(
        flops=int(flops) // 3, bytes_accessed=int(moved) // 3, transcendentals=int(exps) // 3
    )


def roomy():
    return pltpu.CompilerParams(vmem_limit_bytes=ROOM)


def fixed_block(shape):
    return pl.BlockSpec(shape, lambda *at: (0,) * len(shape))


def nothing(*refs):
    pass


def after(value, *tokens):
    leaves, tree = jax.tree.flatten(value)
    tokens = jax.tree.leaves(tokens)
    out = pl.pallas_call(
        nothing,
        in_specs=[ANYWHERE] * (len(leaves) + len(tokens)),
        out_specs=[ANYWHERE] * len(leaves),
        out_shape=[Shape(leaf.shape, leaf.dtype) for leaf in leaves],
        input_output_aliases={i: i for i in range(len(leaves))},
        cost_estimate=cost(0, 0),
        name="after",
    )(*leaves, *tokens)
    return jax.tree.unflatten(tree, out)


def fresh_body(value, *refs):
    refs[-1][...] = value[...]


def fresh(value, first, rows, *tokens, steps=2):
    tokens = jax.tree.leaves(tokens)
    step = rows // steps
    at = first // step
    return pl.pallas_call(
        fresh_body,
        grid=(steps,),
        in_specs=[pl.BlockSpec((step, value.shape[1]), lambda i: (at + i, 0))]
        + [ANYWHERE] * len(tokens),
        out_specs=pl.BlockSpec((step, value.shape[1]), lambda i: (i, 0)),
        out_shape=Shape((rows, value.shape[1]), value.dtype),
        compiler_params=roomy(),
        cost_estimate=cost(0, 4 * rows * value.shape[1]),
        name="fresh",
    )(value, *tokens)


def experts_body(blocks, experts, pieces, begun, given, ids_at, spots_at, numbers, *refs):
    refs, slabs = list(refs), len(pieces)

    def take(count):
        return [refs.pop(0) for _ in range(count)]

    rows_in, cot_in = take(blocks), take(blocks)
    mats = [[take(count) for count in counts] for counts in pieces]
    start_rows, start_mixed = take(blocks * begun), take(blocks * begun)
    take(given)
    rows_out, mixed_out, kept_w_out, kept_g_out = take(blocks), take(blocks), *take(2)
    copies = take(0 if begun else 2)
    rows, cot, both, down, rows_sum, mixed_sum, begin, end, kept_w, kept_g, *refs = refs[-15:]
    extra, extra_begin, extra_end, sems, out_sems = refs
    size, hidden, width = rows_in[0].shape[0], down.shape[1], rows.shape[1]
    spans = [pl.ds(b * size, size) for b in range(blocks)]
    spots = [pl.ds(pl.multiple_of(numbers[at], size), size) for at in spots_at]
    loads, stores = [], []

    def load(source, target):
        copy = pltpu.make_async_copy(source, target, sems.at[len(loads)])
        copy.start()
        loads.append(copy)
        return copy

    def store(source, target):
        copy = pltpu.make_async_copy(source, target, out_sems.at[len(stores)])
        copy.start()
        stores.append(copy)

    main, rest = pl.ds(0, width), pl.ds(width, extra.shape[1])
    rows_loads = [load(rows_in[b].at[:, main], rows.at[spans[b]]) for b in range(blocks)]
    extra_loads = [load(rows_in[b].at[:, rest], extra.at[spans[b]]) for b in range(blocks)]
    if begun:
        extra_loads += [
            load(start_rows[b].at[:, rest], extra_begin.at[spans[b]]) for b in range(blocks)
        ]

    def load_mat(parts, target):
        height = parts[0].shape[0]
        return [load(part, target.at[pl.ds(p * height, height)]) for p, part in enumerate(parts)]

    def load_pre(s):
        gate, up, _ = mats[s]
        return load_mat(gate, both.at[s, :, pl.ds(0, hidden)]) + load_mat(
            up, both.at[s, :, pl.ds(hidden, hidden)]
        )

    mat_loads = [load_pre(0)]
    cot_loads = [load(cot_in[b], cot.at[spans[b]]) for b in range(blocks)]
    down_loads = [load_mat(mats[0][2], down.at[0])]
    if begun:
        begin_loads = [
            [load(start_rows[b].at[:, main], begin.at[0, spans[b]]) for b in range(blocks)],
            [load(start_mixed[b], begin.at[1, spans[b]]) for b in range(blocks)],
        ]
    for s in range(1, slabs):
        mat_loads.append(load_pre(s))
        down_loads.append(load_mat(mats[s][2], down.at[s]))
    for copy in extra_loads:
        copy.wait()
    gates = extra[:, :experts].astype(FULL) + extra[:, experts : 2 * experts].astype(FULL)
    table = extra_begin[:, :experts].astype(FULL) if begun else jnp.zeros(gates.shape, FULL)
    for copy in rows_loads:
        copy.wait()
    for s in range(slabs):
        last = s == slabs - 1
        for copy in mat_loads[s]:
            copy.wait()
        pre = plain_dot(rows[...], both[s])
        if s == 0:
            for copy in cot_loads:
                copy.wait()
            for held, copy_out in zip((rows, cot), copies):
                for b in range(blocks):
                    store(held.at[spans[b]], copy_out.at[spots[b]])
        for copy in down_loads[s]:
            copy.wait()
        plain_grad = outer_rows(cot[...], down[s])
        hit = lax.broadcasted_iota(jnp.int32, gates.shape, 1) == numbers[ids_at[s]]
        gate = jnp.sum(jnp.where(hit, gates, 0.0), axis=1, keepdims=True)
        gate_pre, up_pre = pre[:, :hidden], pre[:, hidden:]
        sigmoid_val = 0.5 * jnp.tanh(0.5 * gate_pre) + 0.5
        silu_val = gate_pre * sigmoid_val
        activation = (silu_val * up_pre).astype(LOW).astype(FULL)
        table = table + jnp.where(
            hit, jnp.sum(activation * plain_grad, axis=1, keepdims=True), 0.0
        )
        grad_act = gate * plain_grad
        kept_w[s] = (gate * activation).astype(LOW)
        kept_g[s, :, :hidden] = (
            grad_act * up_pre * (sigmoid_val + silu_val * (1.0 - sigmoid_val))
        ).astype(LOW)
        kept_g[s, :, hidden:] = (grad_act * silu_val).astype(LOW)
        for b in range(blocks):
            store(kept_w.at[s, spans[b]], kept_w_out.at[spots[b], pl.ds(s * hidden, hidden)])
            store(
                kept_g.at[s, spans[b]], kept_g_out.at[spots[b], pl.ds(2 * s * hidden, 2 * hidden)]
            )
        for i, sums in enumerate((rows_sum, mixed_sum)):
            if s == 0 and begun:
                for copy in begin_loads[i]:
                    copy.wait()
            for p in range(2):
                columns = pl.ds(p * (width // 2), width // 2)
                if i == 0:
                    part = outer_rows(kept_g[s], both[s, columns, :])
                else:
                    part = plain_dot(kept_w[s], down[s, :, columns])
                if s > 0:
                    part = part + sums[:, columns]
                elif begun:
                    part = part + begin[i, :, columns].astype(FULL)
                if last:
                    end[i, :, columns] = part.astype(LOW)
                    for b in range(blocks):
                        out = (rows_out, mixed_out)[i][b]
                        store(end.at[i, spans[b], columns], out.at[:, columns])
                else:
                    sums[:, columns] = part
    extra_end[...] = jnp.zeros(extra_end.shape, LOW)
    extra_end[:, :experts] = table.astype(LOW)
    for b in range(blocks):
        store(extra_end.at[spans[b]], rows_out[b].at[:, rest])
    for copy in stores:
        copy.wait()


def experts_call(
    experts, numbers, ids_at, spots_at, rows, cot, mats, start, shared, total_rows, tokens
):
    blocks, slabs = len(rows), len(mats)
    size, width = cot[0].shape
    extra = rows[0].shape[1] - width
    hidden, total = mats[0][0][0].shape[1], blocks * size
    pieces = [[len(parts) for parts in trio] for trio in mats]
    piece_count = sum(map(sum, pieces))
    operands = [numbers, *rows, *cot]
    specs = [pl.BlockSpec(memory_space=pltpu.SMEM)] + [ANYWHERE] * (2 * blocks)
    for trio in mats:
        operands += [part for parts in trio for part in parts]
    specs += [ANYWHERE] * piece_count
    if start is not None:
        operands += [*start[0], *start[1]]
        specs += [ANYWHERE] * (2 * blocks)
    aliases, given = {}, 0
    outs = 2 * blocks
    for j, part in enumerate(shared):
        if part is not None:
            aliases[len(operands)] = outs + j
            operands.append(part)
            specs.append(ANYWHERE)
            given += 1
    given += len(tokens)
    operands += tokens
    specs += [ANYWHERE] * len(tokens)
    wide, hidden_all = Shape((total_rows, width), LOW), slabs * hidden
    out = pl.pallas_call(
        functools.partial(
            experts_body,
            blocks,
            experts,
            pieces,
            int(start is not None),
            given,
            ids_at,
            spots_at,
        ),
        in_specs=specs,
        out_specs=[ANYWHERE] * (outs + len(shared)),
        out_shape=[Shape((size, width + extra), LOW)] * blocks
        + [Shape((size, width), LOW)] * blocks
        + [Shape((total_rows, hidden_all), LOW), Shape((total_rows, 2 * hidden_all), LOW)]
        + [wide] * (len(shared) - 2),
        input_output_aliases=aliases,
        scratch_shapes=[
            pltpu.VMEM((total, width), LOW),
            pltpu.VMEM((total, width), LOW),
            pltpu.VMEM((slabs, width, 2 * hidden), LOW),
            pltpu.VMEM((slabs, hidden, width), LOW),
            pltpu.VMEM((total, width), FULL),
            pltpu.VMEM((total, width), FULL),
            pltpu.VMEM((2, total, width), LOW),
            pltpu.VMEM((2, total, width), LOW),
            pltpu.VMEM((slabs, total, hidden), LOW),
            pltpu.VMEM((slabs, total, 2 * hidden), LOW),
            pltpu.VMEM((total, extra), LOW),
            pltpu.VMEM((total, extra), LOW),
            pltpu.VMEM((total, extra), LOW),
            pltpu.SemaphoreType.DMA((6 * blocks + piece_count,)),
            pltpu.SemaphoreType.DMA((2 * slabs * blocks + 7 * blocks,)),
        ],
        compiler_params=roomy(),
        cost_estimate=cost(
            12 * total * width * hidden * slabs,
            6 * width * hidden * slabs + 8 * total * width + 6 * total * hidden * slabs,
            total * hidden * slabs,
        ),
        name="experts",
    )(*operands)
    return out[:blocks], out[blocks:outs], out[outs:]


def slab_grads_body(swapped, parts, term_count, rows, kept, *refs):
    terms, outs = refs[: term_count * parts], refs[-parts:]
    found = inner_rows(kept[...], rows[...])
    if swapped:
        found = found.astype(LOW).T.astype(FULL)
    steps = pl.num_programs(0) // parts

    def put(part):
        total = found
        for term in terms[part::parts]:
            total = total + term[...].astype(FULL)
        outs[part][...] = total.astype(LOW)

    for part in range(parts):
        pl.when(pl.program_id(0) // steps == part)(functools.partial(put, part))


def slab_grads_call(rows, kept, first, count, parts, swapped, terms, tokens, step=256):
    total, width = rows.shape
    at, steps = first // step, count // step

    def spec(part):
        def place(i):
            return jnp.clip(i - part * steps, 0, steps - 1)

        if swapped:
            return pl.BlockSpec((width, step), lambda i: (0, place(i)))
        return pl.BlockSpec((step, width), lambda i: (place(i), 0))

    specs = [spec(part) for part in range(parts)]
    return pl.pallas_call(
        functools.partial(slab_grads_body, swapped, parts, len(terms)),
        grid=(parts * steps,),
        in_specs=[
            pl.BlockSpec((total, width), lambda i: (0, 0), pipeline_mode=pl.Buffered(1)),
            pl.BlockSpec((total, step), lambda i: (0, at + i)),
        ]
        + specs * len(terms)
        + [ANYWHERE] * len(tokens),
        out_specs=specs,
        out_shape=[Shape((width, count) if swapped else (count, width), LOW)] * parts,
        compiler_params=roomy(),
        cost_estimate=cost(
            2 * total * width * count * parts,
            2 * total * width + 2 * (total + width) * count * parts,
        ),
        name="slab_grads",
    )(rows, kept, *[part for term in terms for part in term], *tokens)


def rope_tables(length, head_size):
    half_size = head_size // 2
    frequency = THETA ** (-2.0 * np.arange(half_size) / head_size)
    angles = np.arange(length)[:, None] * frequency[None, :]
    cos_part, sin_part = np.cos(angles), np.sin(angles)
    return np.concatenate([cos_part, cos_part, -sin_part, sin_part], axis=1).astype(np.float32)


def half_turn(vectors):
    return pltpu.roll(vectors, vectors.shape[1] // 2, 1)


def project_body(rows, query, query_rest, key, key_rest, value, value_rest, gains, tables, *refs):
    query_proj, query_low, key_proj, key_low, value_low = refs
    half = query.shape[0]

    def both_halves(mat, rest):
        return plain_dot(rows[:, :half], mat[...]) + plain_dot(rows[:, half:], rest[...])

    size = gains.shape[1]
    cos_two, sin_two = tables[:, :size], tables[:, size:]
    for mat, rest, gain, proj_out, low_out in (
        (query, query_rest, gains[0:1], query_proj, query_low),
        (key, key_rest, gains[1:2], key_proj, key_low),
    ):
        proj = both_halves(mat, rest)
        proj_out[...] = proj
        for h in range(mat.shape[1] // size):
            columns = slice(h * size, (h + 1) * size)
            head = proj[:, columns]
            head = head * lax.rsqrt(jnp.mean(head * head, axis=-1, keepdims=True) + EPSILON)
            head = head * gain
            low_out[:, columns] = (head * cos_two + half_turn(head) * sin_two).astype(LOW)
    value_low[...] = both_halves(value, value_rest).astype(LOW)


def project_call(rows, mats, gains, tables):
    total, width = rows.shape
    mats = [half for halves in mats for half in halves]
    columns, step = mats[0].shape[1], min(256, total)
    row_block = pl.BlockSpec((step, columns), lambda i: (i, 0))
    full, low = Shape((total, columns), FULL), Shape((total, columns), LOW)
    return pl.pallas_call(
        project_body,
        grid=(total // step,),
        in_specs=[pl.BlockSpec((step, width), lambda i: (i, 0))]
        + [fixed_block(mat.shape) for mat in mats]
        + [fixed_block(gains.shape), pl.BlockSpec((step, tables.shape[1]), lambda i: (i, 0))],
        out_specs=[row_block] * 5,
        out_shape=[full, low, full, low, low],
        compiler_params=roomy(),
        cost_estimate=cost(
            6 * total * width * columns, 2 * total * width + 6 * width * columns + 14 * total * columns
        ),
        name="project",
    )(rows, *mats, gains, tables)


def held_pairs(seg_col, seg_row, pos_col, pos_row):
    same = seg_col == seg_row
    if seg_row.shape[1] > WIN:
        same = same & (jnp.abs(pos_col - pos_row) < WIN)
    return same


def softmax_rows(query, key, held):
    scores = outer_rows(query, key) * (query.shape[1] ** -0.5)
    scores = jnp.where(held, scores, MASKED)
    raised = jnp.exp(scores - jnp.max(scores, axis=-1, keepdims=True))
    return raised * (1.0 / jnp.sum(raised, axis=-1, keepdims=True))


def attend_body(query, key, value, seg_col, seg_row, pos_col, pos_row, *refs):
    out = refs[-1]
    held = held_pairs(seg_col[...], seg_row[...], pos_col[...], pos_row[...])
    probs = softmax_rows(query[...], key[...], held).astype(LOW)
    out[...] = plain_dot(probs, value[...]).astype(LOW)


def attend_call(query, key, value, places, size, first, rows, tokens):
    total, columns = query.shape
    heads = columns // size
    at = first // rows
    column_block = pl.BlockSpec((total, size), lambda h: (0, h))
    col = pl.BlockSpec((rows, 1), lambda h: (at, 0))
    row = fixed_block((1, total))
    return pl.pallas_call(
        attend_body,
        grid=(heads,),
        in_specs=[
            pl.BlockSpec((rows, size), lambda h: (at, h)),
            column_block,
            column_block,
            col,
            row,
            col,
            row,
        ]
        + [ANYWHERE] * len(tokens),
        out_specs=pl.BlockSpec((rows, size), lambda h: (0, h)),
        out_shape=Shape((rows, columns), LOW),
        compiler_params=roomy(),
        cost_estimate=cost(
            4 * rows * total * columns, 4 * (total + rows) * columns, rows * total * heads
        ),
        name="attend",
    )(query, key, value, *places, *tokens)


def unprepare(grad, proj, gain, cos_two, sin_two):
    inverse = lax.rsqrt(jnp.mean(proj * proj, axis=-1, keepdims=True) + EPSILON)
    unit = proj * inverse
    grad = grad * cos_two + half_turn(grad * sin_two)
    gain_grad = jnp.sum(grad * unit, axis=0, keepdims=True)
    grad = grad * gain
    return inverse * (grad - unit * jnp.mean(grad * unit, axis=-1, keepdims=True)), gain_grad


def attend_back_body(
    step,
    query,
    key,
    value,
    grad,
    query_proj,
    key_proj,
    gains,
    tables,
    seg_col,
    seg_row,
    pos_col,
    pos_row,
    grad_query,
    grad_key,
    grad_value,
    grad_gains,
    query_sum,
    key_sum,
    value_sum,
):
    total, size = query.shape
    scaling = size**-0.5
    for q in range(total // step):
        at = pl.ds(q * step, step)
        held = held_pairs(seg_col[at], seg_row[...], pos_col[at], pos_row[...])
        probs = softmax_rows(query[at], key[...], held)
        grad_probs = outer_rows(grad[at], value[...]).astype(LOW).astype(FULL)
        weighted = probs * grad_probs
        centre = jnp.sum(weighted, axis=-1, keepdims=True)
        grad_scores = (weighted - probs * centre).astype(LOW)
        query_sum[at] = plain_dot(grad_scores, key[...]) * scaling
        key_part = inner_rows(grad_scores, query[at])
        value_part = inner_rows(probs.astype(LOW), grad[at])
        if q == 0:
            key_sum[...] = key_part
            value_sum[...] = value_part
        else:
            key_sum[...] += key_part
            value_sum[...] += value_part
    grad_value[...] = value_sum[...].astype(LOW)
    turns = (tables[:, :size], tables[:, size:])
    query_part, query_gain_part = unprepare(
        query_sum[...], query_proj[...], gains[0:1], *turns
    )
    key_part, key_gain_part = unprepare(
        key_sum[...] * scaling, key_proj[...], gains[1:2], *turns
    )
    grad_query[...] = query_part.astype(LOW)
    grad_key[...] = key_part.astype(LOW)

    @pl.when(pl.program_id(0) == 0)
    def _():
        grad_gains[...] = jnp.zeros_like(grad_gains)

    grad_gains[0:1] += query_gain_part
    grad_gains[1:2] += key_gain_part


def attend_back_call(query, key, value, grad, query_proj, key_proj, gains, tables, places):
    total, columns = query.shape
    size = gains.shape[1]
    heads, step = columns // size, min(256, total)
    head = pl.BlockSpec((total, size), lambda h: (0, h))
    fixed = (gains, tables, *places)
    return pl.pallas_call(
        functools.partial(attend_back_body, step),
        grid=(heads,),
        in_specs=[head] * 6 + [fixed_block(a.shape) for a in fixed],
        out_specs=[head] * 3 + [fixed_block((2, size))],
        out_shape=[Shape((total, columns), LOW)] * 3 + [Shape((2, size), FULL)],
        scratch_shapes=[pltpu.VMEM((total, size), FULL)] * 3,
        compiler_params=roomy(),
        cost_estimate=cost(
            10 * total * total * columns, 22 * total * columns, total * total * heads
        ),
        name="attend_back",
    )(query, key, value, grad, query_proj, key_proj, *fixed)


def rows_back_body(count, *refs):
    grads, firsts, rests = (refs[k * count : (k + 1) * count] for k in range(3))
    outs = refs[3 * count :]
    step, steps, size = pl.program_id(0), pl.num_programs(0), outs[0].shape[0]

    def run(mats):
        total = outer_rows(grads[0][...], mats[0][...])
        for grad, mat in zip(grads[1:], mats[1:]):
            total = total + outer_rows(grad[...], mat[...])
        for b, out in enumerate(outs):
            out[...] = total[b * size : (b + 1) * size].astype(LOW)

    pl.when(step < steps // 2)(lambda: run(firsts))
    pl.when(step >= steps // 2)(lambda: run(rests))


def rows_back_call(grads, mats, size, tokens):
    (rows, columns), count = grads[0].shape, len(grads)
    half, blocks = mats[0][0].shape[0], rows // size
    step = half // 2

    def body(*refs):
        rows_back_body(count, *refs[: 3 * count], *refs[3 * count + len(tokens) :])

    return pl.pallas_call(
        body,
        grid=(4,),
        in_specs=[fixed_block((rows, columns))] * count
        + [pl.BlockSpec((step, columns), lambda i: (jnp.minimum(i, 1), 0))] * count
        + [pl.BlockSpec((step, columns), lambda i: (jnp.maximum(i - 2, 0), 0))] * count
        + [ANYWHERE] * len(tokens),
        out_specs=[pl.BlockSpec((size, step), lambda i: (0, i))] * blocks,
        out_shape=[Shape((size, 2 * half), LOW)] * blocks,
        compiler_params=roomy(),
        cost_estimate=cost(
            4 * count * rows * columns * half,
            2 * count * (rows * columns + 2 * columns * half) + 4 * rows * half,
        ),
        name="rows_back",
    )(*grads, *[mat[0] for mat in mats], *[mat[1] for mat in mats], *tokens)


def weight_back_body(columns, rows, branch, query, key, value, attended, *refs):
    out = refs[-1]
    for place, (left, right) in enumerate(
        ((rows, query), (rows, key), (rows, value), (branch, attended))
    ):
        out[:, place * columns : (place + 1) * columns] = inner_rows(
            left[...], right[...]
        ).astype(LOW)


def weight_back_call(rows, branch, grads, attended, half, tokens, step=512):
    (total, width), columns = rows.shape, attended.shape[1]
    steps = width // 2 // step
    part = pl.BlockSpec((total, step), lambda i: (0, half * steps + i))
    return pl.pallas_call(
        functools.partial(weight_back_body, columns),
        grid=(steps,),
        in_specs=[part, part] + [fixed_block((total, columns))] * 4 + [ANYWHERE] * len(tokens),
        out_specs=pl.BlockSpec((step, 4 * columns), lambda i: (i, 0)),
        out_shape=Shape((width // 2, 4 * columns), LOW),
        compiler_params=roomy(),
        cost_estimate=cost(
            4 * total * width * columns, 2 * total * width + 8 * (total + width // 2) * columns
        ),
        name="weight_back",
    )(rows, branch, *grads, attended, *tokens)


class Ring:
    def __init__(self, axis, size, count):
        self.axis, self.count = axis, count
        self.order = list(range(0, count, 2)) + list(range(count - 1, 0, -2))
        self.rightward = [
            (base + self.order[k], base + self.order[(k + 1) % count])
            for base in range(0, size, count)
            for k in range(count)
        ]
        self.leftward = [(to, start) for start, to in self.rightward]

    def right(self, value):
        return jax.tree.map(lambda v: lax.ppermute(v, self.axis, self.rightward), value)

    def left(self, value):
        return jax.tree.map(lambda v: lax.ppermute(v, self.axis, self.leftward), value)

    def members(self, at):
        count = self.count
        spot = jnp.where(at % 2 == 0, at // 2, count - (at + 1) // 2)
        shifts = [0]
        for k in range(1, count // 2):
            shifts += [-k, k]
        shifts.append(count // 2)
        spots = [(spot + shift + count) % count for shift in shifts]
        return [jnp.where(p < count // 2, 2 * p, 2 * (count - p) - 1) for p in spots]

    def gather(self, value, use, between):
        from_left = from_right = value
        use(0, [value])
        for k in range(1, self.count // 2):
            from_left, from_right = between(k, (self.right(from_left), self.left(from_right)))
            use(k, [from_left, from_right])
        upper = self.right(jax.tree.map(lambda v: v[: v.shape[0] // 2], from_left))
        lower = self.left(jax.tree.map(lambda v: v[v.shape[0] // 2 :], from_right))
        upper, lower = between(self.count // 2, (upper, lower))
        use(
            self.count // 2,
            [jax.tree.map(lambda u, v: jnp.concatenate([u, v]), upper, lower)],
        )

    def scatter(self, make, finish=lambda pair: pair):
        steps = Reduction(self)
        tokens = []
        for k in range(self.count // 2, 0, -1):
            tokens = steps.hop(make(k, tokens))
        (own,) = make(0, tokens)
        steps.pair = finish(steps.pair)
        return steps.total(own)


class Spread:
    def __init__(self, ring, value):
        self.ring, self.pair, self.blocks, self.hops = ring, (value, value), [value], 0

    def hop(self, *tokens):
        ring = self.ring
        if self.hops:
            self.settle(*tokens)
        left, right = self.pair
        self.hops += 1
        if self.hops == ring.count // 2:
            left, right = left[: left.shape[0] // 2], right[right.shape[0] // 2 :]
        self.pair = (ring.right(left), ring.left(right))

    def settle(self, *tokens):
        self.pair = after(self.pair, *tokens)
        if self.hops == self.ring.count // 2:
            self.blocks.append(jnp.concatenate(self.pair))
        else:
            self.blocks.extend(self.pair)


class Reduction:
    def __init__(self, ring):
        self.ring, self.pair = ring, None

    def hop(self, terms, *tokens):
        ring = self.ring
        if self.pair is None:
            (far,) = terms
            if tokens:
                far = after(far, *tokens)
            half = far.shape[0] // 2
            sent = [far]
            self.pair = (ring.right(far[:half]), ring.left(far[half:]))
        else:
            on_left, on_right = terms
            from_left, from_right = self.pair
            half = from_left.shape[0]
            if half < on_left.shape[0]:
                to_right = jnp.concatenate([on_right[:half] + from_left, on_right[half:]])
                to_left = jnp.concatenate([on_left[:half], on_left[half:] + from_right])
            else:
                to_right, to_left = on_right + from_left, on_left + from_right
            sent = [to_right, to_left]
            if tokens:
                sent = after(sent, *tokens)
            self.pair = (ring.right(sent[0]), ring.left(sent[1]))
        return sent

    def total(self, own):
        return own.astype(FULL) + self.pair[0].astype(FULL) + self.pair[1].astype(FULL)


class Owners:
    def __init__(self):
        self.count = lax.axis_size("expert")
        self.chips = self.count // 2
        self.here = lax.axis_index("expert")

    def cross(self, value):
        pairs = [(i, i ^ 1) for i in range(self.count)]
        return jax.tree.map(lambda v: lax.ppermute(v, "expert", pairs), value)

    def along(self, value, shift):
        pairs = [(i, (i + 2 * shift) % self.count) for i in range(self.count)]
        return jax.tree.map(lambda v: lax.ppermute(v, "expert", pairs), value)

    def listed(self):
        chip, core = self.here // 2, self.here % 2
        return [
            (chip - shift + self.chips) % self.chips * 2 + (core ^ other)
            for other in range(2)
            for shift in range(self.chips)
        ]

    def places(self):
        chip, core = self.here // 2, self.here % 2
        return [
            (core ^ (at % 2)) * self.chips + (chip - at // 2 + self.chips) % self.chips
            for at in range(self.count)
        ]

    def scatter(self, parts):
        mine, other = parts[: self.chips], parts[self.chips :]
        other = self.cross(jnp.concatenate(other, axis=0))
        rows = mine[0].shape[0]
        total = None
        for shift in reversed(range(self.chips)):
            part = mine[shift].astype(FULL) + other[shift * rows : (shift + 1) * rows].astype(FULL)
            if shift:
                part = self.along(part.astype(LOW), -shift).astype(FULL)
            total = part if total is None else total + part
        return total

    def pick_columns(self, rows, places):
        size = rows.shape[1] // self.count
        return jnp.concatenate(
            [lax.dynamic_slice_in_dim(rows, at * size, size, 1) for at in places], axis=1
        )

    def list_columns(self, rows):
        return self.pick_columns(rows, self.listed())

    def unlist_columns(self, rows):
        return self.pick_columns(rows, self.places())


def everywhere(value):
    for axis in ("expert", "tensor"):
        size, step = lax.axis_size(axis), 1
        while step < size:
            pairs = [(i, i ^ step) for i in range(size)]
            value = jax.tree.map(lambda v: v + lax.ppermute(v, axis, pairs), value)
            step *= 2
    return value


def per_device(
    tokens,
    segments,
    routes,
    norm_gain,
    w_query,
    w_key,
    w_value,
    query_gain,
    key_gain,
    w_out,
    mix_gain,
    w_router,
    w_gate,
    w_up,
    w_down,
    cotangent,
):
    tensor_count = lax.axis_size("tensor")
    expert_count = w_router.shape[1]
    tok_rows, model_width = tokens.shape
    seq_count, length = segments.shape
    head_size = query_gain.shape[0]
    part_count = tensor_count // seq_count
    block_width = w_query.shape[1]
    local_width = seq_count * block_width
    tensor_at = lax.axis_index("tensor")
    seq_at, part_at = tensor_at // part_count, tensor_at % part_count
    whole_ring = Ring("tensor", tensor_count, tensor_count)
    seq_ring = Ring("tensor", tensor_count, part_count)
    owners = Owners()

    def seq_swap(value, shift):
        pairs = [(t, (t + part_count * shift) % tensor_count) for t in range(tensor_count)]
        return lax.ppermute(value, "tensor", pairs)

    inputs = tokens.astype(jnp.float32)
    inv_one = lax.rsqrt(jnp.mean(inputs * inputs, axis=-1, keepdims=True) + EPSILON)
    unit_one = inputs * inv_one
    normed_one = owners.list_columns((unit_one * norm_gain).astype(jnp.bfloat16))

    seq_shifts, chip_shifts = range(1, seq_count), range(1, owners.chips)
    hidden, total_rows = w_down.shape[1], tensor_count * tok_rows
    own_slab = (w_gate[0], w_up[0], w_down[0])
    copies = [
        fresh(cotangent, 0, tok_rows, normed_one),
        fresh(own_slab[0], 0, model_width, normed_one),
        fresh(own_slab[1], 0, model_width, normed_one),
        fresh(own_slab[2], 0, hidden // 2, normed_one),
        fresh(own_slab[2], hidden // 2, hidden // 2, normed_one),
    ]
    query_key = jnp.concatenate([w_query, w_key], axis=1)
    wave = [
        *[seq_swap(query_key, s) for s in seq_shifts],
        *[owners.along(w, s) for w in (w_value, w_out) for s in chip_shifts],
    ]
    gathered, found = [], {}

    def between(k, pair):
        nonlocal wave
        if k == 1:
            pair, moved, copies[:] = after((pair, wave, copies))
            moved, others = moved[seq_count - 1 :], moved[: seq_count - 1]
            heads = [query_key, *others]
            found["pair"] = jnp.concatenate(
                [h[:, :block_width] for h in heads] + [h[:, block_width:] for h in heads], axis=1
            )
            count = owners.chips - 1
            found["value"] = jnp.concatenate([w_value, *moved[:count]], axis=0)
            found["out"] = jnp.concatenate([w_out, *moved[count:]], axis=1)
            wave = [
                *[owners.along(found["pair"], s) for s in chip_shifts],
                *[seq_swap(found["value"], s) for s in seq_shifts],
            ]
        elif k == part_count // 2:
            pair, moved = after((pair, wave))
            count = owners.chips - 1
            found["pair"] = jnp.concatenate([found["pair"], *moved[:count]], axis=0)
            found["value"] = jnp.concatenate([found["value"], *moved[count:]], axis=1)
            wave = moved[:1]
        return pair

    seq_ring.gather(normed_one, lambda k, blocks: gathered.extend(blocks), between)
    normed_all = jnp.concatenate(gathered)
    pair_rest, value_rest = owners.cross(found["pair"]), owners.cross(found["value"])
    full_mats = [
        (found["pair"][:, :local_width], pair_rest[:, :local_width]),
        (found["pair"][:, local_width:], pair_rest[:, local_width:]),
        (found["value"], value_rest),
    ]
    own_cot, own_gate, own_up, *own_down = copies
    cot_steps = Spread(whole_ring, after(own_cot, wave))
    cot_steps.hop()
    far_gate = [owners.along(after(own_gate, wave), s) for s in chip_shifts]
    far_up = [owners.along(after(own_up, far_gate), s) for s in chip_shifts]

    whole_members = whole_ring.members(tensor_at)
    seq_members = seq_ring.members(part_at)
    numbers = jnp.stack(
        [at * tok_rows for at in whole_members]
        + [(at * tensor_count + tensor_at) // 2 for at in owners.listed()]
    )
    ids_from = tensor_count

    def from_place(table):
        return jnp.concatenate(
            [
                lax.dynamic_slice_in_dim(table, at * tok_rows, tok_rows, 0)
                for at in seq_members
            ]
        )

    tables = from_place(jnp.array(rope_tables(length, head_size)))
    seg_row = lax.dynamic_index_in_dim(segments, seq_at, 0, keepdims=False)
    marks = from_place(jnp.stack([seg_row, jnp.arange(length, dtype=jnp.int32)], axis=1))
    places = (marks[:, :1], marks[:, :1].T, marks[:, 1:], marks[:, 1:].T)
    gains = jnp.stack([query_gain, key_gain])

    query_proj, query_low, key_proj, key_low, value_low = project_call(
        normed_all, full_mats, gains, tables
    )

    def place_of(ring, k):
        return {0: [0], ring.count // 2: [ring.count - 1]}.get(k, [2 * k - 1, 2 * k])

    cot_steps.hop(query_low)
    out_chips = after(found["out"], pair_rest)
    out_heads = jnp.concatenate(
        [out_chips, *after([seq_swap(out_chips, s) for s in seq_shifts], query_low)], axis=0
    )
    out_full = jnp.concatenate([out_heads, owners.cross(out_heads)], axis=1)
    attended = [None] * part_count

    def branch_parts(k, tokens):
        parts = []
        tokens = list(tokens) + (far_gate if k == 0 else [])
        for b in place_of(seq_ring, k):
            attended[b] = attend_call(
                query_low,
                key_low,
                value_low,
                places,
                head_size,
                b * tok_rows,
                tok_rows,
                tokens,
            )
            parts.append(plain_dot(attended[b], out_full).astype(LOW))
        return parts

    def branch_done(pair):
        cot_steps.hop(pair)
        return pair

    residual = inputs + owners.unlist_columns(seq_ring.scatter(branch_parts, branch_done))
    attn_rows = jnp.concatenate(attended)
    inv_two = lax.rsqrt(jnp.mean(residual * residual, axis=-1, keepdims=True) + EPSILON)
    unit_two = residual * inv_two
    normed_two = (unit_two * mix_gain).astype(jnp.bfloat16)
    logits = jnp.dot(normed_two, w_router, preferred_element_type=jnp.float32)
    hits = jnp.any(
        routes[:, :, None] == jnp.arange(expert_count, dtype=jnp.int32)[None, None, :], axis=1
    )
    top_logit = jnp.max(jnp.where(hits, logits, MASKED), axis=-1, keepdims=True)
    raised = jnp.where(hits, jnp.exp(logits - top_logit), 0.0)
    gate_table = raised / jnp.sum(raised, axis=-1, keepdims=True)

    grad_out = cotangent.astype(jnp.float32)
    far_down = []
    slab_mats = {0: [[[w] for w in own_slab], [[w] for w in owners.cross(own_slab)]]}
    row_blocks, sums, mixed = ([None] * tensor_count for _ in range(3))
    shared_all = []

    def run_experts(shift, k, tokens):
        at = place_of(whole_ring, k)
        if len(shared_all) == shift:
            shared_all.append([None] * (2 if shift else 4))
        parts, mixed_parts, shared_all[shift] = experts_call(
            expert_count,
            numbers,
            [ids_from + shift, ids_from + owners.chips + shift],
            at,
            [row_blocks[b] for b in at],
            [cot_steps.blocks[b] for b in at],
            slab_mats[shift],
            [[part[b] for b in at] for part in (sums, mixed)] if shift else None,
            shared_all[shift],
            total_rows,
            tokens,
        )
        for b, part, mixed_part in zip(at, parts, mixed_parts):
            sums[b], mixed[b] = part, mixed_part
        return [sums[b] for b in at]

    def first_pair(k, blocks):
        for b, rows in zip(place_of(whole_ring, k), blocks):
            row_blocks[b] = rows
        run_experts(0, k, [])

    def next_hop(k, pair):
        done = [sums[b] for b in place_of(whole_ring, k - 1)]
        if k == 1:
            while cot_steps.hops < tensor_count // 2:
                cot_steps.hop(pair)
            pair, far_up[:] = after((pair, far_up), *done)
        elif k <= 3:
            pair, far_down[-1] = after((pair, far_down[-1]), *done)
            if k == 2:
                cot_steps.settle(pair)
        elif k < tensor_count // 2:
            pair = after(pair, *done)
        if k <= 2:
            piece = after(own_down[k - 1], pair[0])
            far_down.append([owners.along(piece, s) for s in chip_shifts])
        return pair

    high = lax.reduce_precision(gate_table, 8, 7)
    room = -2 * expert_count % 128
    payload = jnp.concatenate(
        [
            normed_two,
            high.astype(LOW),
            (gate_table - high).astype(LOW),
            jnp.zeros((tok_rows, room), LOW),
        ],
        axis=1,
    )
    whole_ring.gather(payload, first_pair, next_hop)
    for shift in chip_shifts:
        mine = [[far_gate[shift - 1]], [far_up[shift - 1]], [piece[shift - 1] for piece in far_down]]
        slab_mats[shift] = [mine, owners.cross(mine)]
    for shift in range(1, owners.chips - 1):
        for k in range(tensor_count // 2 + 1):
            run_experts(shift, k, [])

    def last_pair(k, tokens):
        return run_experts(owners.chips - 1, k, jax.tree.leaves(tokens))

    def down_grads(shift, other, terms, tokens):
        kept, all_cot = shared_all[shift][0], shared_all[0][3]
        return slab_grads_call(
            all_cot, kept, other * hidden, hidden, 1, False, [[t] for t in terms], tokens
        )[0]

    def pre_grads(shift, other, terms, tokens):
        kept, rows = shared_all[shift][1], shared_all[0][2]
        return slab_grads_call(
            rows, kept, 2 * other * hidden, hidden, 2, True, terms, tokens
        )

    def far_down_grads(tokens):
        others = [owners.cross(down_grads(s, 1, [], tokens)) for s in chip_shifts]
        return [down_grads(s, 0, [other], tokens) for s, other in zip(chip_shifts, others)]

    def finish(pair):
        pair, found["down"] = after((pair, far_down_grads([sums[0]])))
        return pair

    summed_rows = whole_ring.scatter(last_pair, finish)
    grad_rows_sum = summed_rows[:, :model_width]
    grad_gates = summed_rows[:, model_width : model_width + expert_count]
    sent_down = [owners.along(part, -s) for s, part in zip(chip_shifts, found["down"])]

    grad_logits = gate_table * (
        grad_gates - jnp.sum(gate_table * grad_gates, axis=-1, keepdims=True)
    )
    grad_normed_two = grad_rows_sum + outer_rows(grad_logits, w_router.astype(jnp.float32), HIGH)
    grad_router = inner_rows(grad_logits, normed_two.astype(jnp.float32), HIGH)
    grad_unit_two = grad_normed_two * mix_gain
    grad_mix_gain = jnp.sum(grad_normed_two * unit_two, axis=0)
    grad_residual = grad_out + inv_two * (
        grad_unit_two - unit_two * jnp.mean(grad_unit_two * unit_two, axis=-1, keepdims=True)
    )
    grad_branch = owners.list_columns(grad_residual.astype(jnp.bfloat16))
    gathered_back = []

    def back_hop(k, pair):
        if k == 1:
            others = [owners.cross(pre_grads(s, 1, [], [grad_branch])) for s in chip_shifts]
            pair = after(pair)
            found["pre"] = [
                pre_grads(s, 0, [other], [pair[0]]) for s, other in zip(chip_shifts, others)
            ]
        elif k == part_count // 2:
            pair, sent_down[:] = after((pair, sent_down), found["pre"])
        return pair

    seq_ring.gather(grad_branch, lambda k, blocks: gathered_back.extend(blocks), back_hop)
    sent_gate = [owners.along(part[0], -s) for s, part in zip(chip_shifts, found["pre"])]
    mixture_steps = Reduction(whole_ring)
    mixture_steps.hop(mixed[-1:], gathered_back[-1])
    grad_attn = jnp.concatenate(
        [outer_rows(block, out_full).astype(jnp.bfloat16) for block in gathered_back]
    )
    *head_grads, grad_gains = attend_back_call(
        query_low, key_low, value_low, grad_attn, query_proj, key_proj, gains, tables, places
    )

    def mixture_hop(k, *tokens):
        mixture_steps.hop([mixed[b] for b in place_of(whole_ring, k)], *tokens)

    mixture_hop(tensor_count // 2 - 1, head_grads[0])
    grad_branch_all = jnp.concatenate(gathered_back)
    own_other_half = weight_back_call(
        normed_all, grad_branch_all, head_grads, attn_rows, 1, []
    )
    other_half = owners.cross(own_other_half)
    mine_half = weight_back_call(
        normed_all, grad_branch_all, head_grads, attn_rows, 0, [own_other_half]
    )
    normed_parts = rows_back_call(head_grads, full_mats, tok_rows, [mine_half, *sent_gate])
    own_other_down = owners.cross(down_grads(0, 1, [], [normed_parts[0]]))
    chip_rows = model_width // owners.count
    piece_rows = chip_rows // 2
    pieces = [slice(p * piece_rows, (p + 1) * piece_rows) for p in range(2)]

    def both_cores(shift, rows, columns=slice(None)):
        rows = slice(shift * chip_rows + rows.start, shift * chip_rows + rows.stop)
        return mine_half[rows, columns].astype(FULL) + other_half[rows, columns].astype(FULL)

    sent_parts = [[both_cores(s, rows).astype(LOW) for s in chip_shifts] for rows in pieces]
    come = []

    def give_parts(k, tokens):
        parts = [normed_parts[b] for b in place_of(seq_ring, k)]
        if k == 1:
            parts, sent_parts[:] = after((parts, sent_parts))
        if k == 0:
            sent = after(sent_parts[0], tokens)
            come.append([owners.along(part, -s) for s, part in zip(chip_shifts, sent)])
            found["own_other"] = pre_grads(0, 1, [], tokens)
        return parts

    def normed_done(pair):
        pair, come[0] = after((pair, come[0]), found["own_other"])
        return pair

    back_steps = seq_ring.scatter(give_parts, normed_done)
    grad_normed_one = owners.unlist_columns(back_steps)
    done = come[0][0]
    mixture_hop(max(tensor_count // 2 - 2, 1), done)
    sent = after(sent_parts[1], done)
    come.append([owners.along(part, -s) for s, part in zip(chip_shifts, sent)])
    own_other = owners.cross(found["own_other"])
    own_down_grad = down_grads(0, 0, [own_other_down], [done])
    own_pre_grads = pre_grads(0, 0, [own_other], [done])
    for k in range(tensor_count // 2 - 3, 0, -1):
        mixture_hop(k, own_pre_grads)
    layer_out = (residual + mixture_steps.total(mixed[0])).astype(jnp.bfloat16)

    def columns_of(place, seq):
        first = (place * seq_count + seq) * block_width
        return slice(first, first + block_width)

    def summed_piece(p, columns):
        return both_cores(0, pieces[p], columns) + sum(
            part[:, columns].astype(FULL) for part in come[p]
        )

    owned = [[] for _ in range(4)]
    for p in range(2):
        swapped = [
            seq_swap(
                jnp.concatenate(
                    [summed_piece(p, columns_of(place, s)).astype(LOW) for place in range(4)],
                    axis=1,
                ),
                -s,
            )
            for s in seq_shifts
        ]
        for place in range(4):
            columns = slice(place * block_width, (place + 1) * block_width)
            owned[place].append(
                summed_piece(p, columns_of(place, 0))
                + sum(part[:, columns].astype(FULL) for part in swapped)
            )
    owned_query, owned_key, owned_value, owned_out = map(jnp.concatenate, owned)
    owned_out = owned_out.T
    sent_up = [
        owners.along(after(part[1], come[1]), -s) for s, part in zip(chip_shifts, found["pre"])
    ]

    def together(own, *parts):
        return own.astype(FULL) + sum(part.astype(FULL) for part in parts)

    grad_gate = together(own_pre_grads[0], *sent_gate)
    grad_up = together(own_pre_grads[1], *sent_up)
    grad_down = together(own_down_grad, *sent_down)
    def gain_part(grad, place):
        return sum(
            jnp.sum(
                grad[:, m * local_width : (m + 1) * local_width].astype(FULL)
                * mat[place].astype(FULL),
                axis=1,
            )
            for m, mat in enumerate(full_mats)
        )

    listed_norm = jnp.concatenate([gain_part(mine_half, 0), gain_part(own_other_half, 1)])
    grad_norm_gain = owners.unlist_columns(listed_norm[None])[0] / norm_gain

    grad_unit_one = grad_normed_one * norm_gain
    grad_tokens = grad_residual + inv_one * (
        grad_unit_one - unit_one * jnp.mean(grad_unit_one * unit_one, axis=-1, keepdims=True)
    )
    early = lax.psum(
        jnp.concatenate([grad_router, grad_mix_gain[None]]), ("expert", "tensor")
    )
    early = after(early, done)
    late = everywhere(
        after(jnp.concatenate([grad_norm_gain.reshape(-1, head_size), grad_gains]), done)
    )
    return (
        layer_out,
        grad_tokens.astype(jnp.bfloat16),
        late[:-2].reshape(-1),
        owned_query,
        owned_key,
        owned_value,
        late[-2],
        late[-1],
        owned_out,
        early[-1],
        early[:-1].T,
        grad_gate[None],
        grad_up[None],
        grad_down[None],
    )


def solution(mesh):
    in_specs = (
        P(("expert", "tensor"), None),
        P("expert", None),
        P(("expert", "tensor"), None),
        P(),
        P("expert", "tensor"),
        P("expert", "tensor"),
        P("expert", "tensor"),
        P(),
        P(),
        P("tensor", "expert"),
        P(),
        P(),
        P(("expert", "tensor"), None, None),
        P(("expert", "tensor"), None, None),
        P(("expert", "tensor"), None, None),
        P(("expert", "tensor"), None),
    )
    out_specs = (
        P(("expert", "tensor"), None),
        P(("expert", "tensor"), None),
        P(),
        P("expert", "tensor"),
        P("expert", "tensor"),
        P("expert", "tensor"),
        P(),
        P(),
        P("tensor", "expert"),
        P(),
        P(),
        P(("expert", "tensor"), None, None),
        P(("expert", "tensor"), None, None),
        P(("expert", "tensor"), None, None),
    )
    return jax.shard_map(
        per_device, mesh=mesh, in_specs=in_specs, out_specs=out_specs, check_vma=False
    )
```

time: 1400 us -> 928 us (0.66)
  matrix products: 621 us -> 23.8 us
  Pallas kernels: 0 us -> 380 us
  waiting for transfers between devices: 397 us -> 247 us
  local copies, waits for them, and re-layouts: 119 us -> 68.3 us
  starting transfers between devices: 117 us -> 83.1 us
  other arithmetic: 116 us -> 96.5 us
    pallas_call x0 -> x62, Pallas kernels: none -> 380 us  [the longest x10 172 us: experts_call(): pl.pallas_call(functools.partial(experts_body, blocks, experts, pieces, i...]
    dot_general x122 -> x5, matrix products: 272 us -> 12.3 us  [outer_rows(): lax.dot_general(left_side, right_side, (((1,), (1,)), ((), ())), precisio...]
    dot_general x103 -> x4, matrix products: 182 us -> 9.53 us  [plain_dot(): return jnp.dot(left_side, right_side, preferred_element_type=jnp.float32)]
    dot_general x25 -> x1, matrix products: 146 us -> 1.54 us  [inner_rows(): lax.dot_general(left_side, right_side, (((0,), (0,)), ((), ())), precisio...]
    ppermute x32 -> x24, waiting for transfers between devices: 184 us -> 53.5 us  [left(): lax.ppermute(v, self.axis, self.leftward)]
    unnamed x32 -> x1, other arithmetic: 41.6 us -> 1.25 us
    ppermute x25 -> x5, waiting for transfers between devices: 47 us -> 18.1 us  [everywhere(): value = jax.tree.map(lambda v: v + lax.ppermute(v, axis, pairs), value)]
    unnamed x727 -> x296, local copies, waits for them, and re-layouts: 60.3 us -> 32.6 us
  transfers between devices with their start and end apart: 123 -> 88, of which waited for: 46 -> 33; matrix products, arithmetic and copies ran while one was open for 58% -> 15% of each run, Pallas kernels for 0% -> 34%
where the time goes in v2:
time: 928 us; the launch traced here: 915 us
  Pallas kernels  380 us (41%)
  waiting for transfers between devices  247 us (27%)
  other arithmetic  96.5 us (10%)
  starting transfers between devices  83.1 us (9%)
  local copies, waits for them, and re-layouts  68.3 us (7%)
  matrix products  23.8 us (3%)
  between operations  16.1 us (2%)
    pallas_call x10, Pallas kernels, experts_call(): pl.pallas_call(functools.partial(experts_body, blocks, experts, pieces, i...  172 us
    pallas_call x8, Pallas kernels, slab_grads_call(): pl.pallas_call(functools.partial(slab_grads_body, swapped, parts, len(ter...  107 us
    ppermute x24, waiting for transfers between devices, right(): lax.ppermute(v, self.axis, self.rightward)  61.5 us
    ppermute x5, waiting for transfers between devices, seq_swap(): return lax.ppermute(value, 'tensor', pairs)  57.9 us
    ppermute x12, waiting for transfers between devices, along(): return jax.tree.map(lambda v: lax.ppermute(v, 'expert', pairs), value)  54.3 us
    ppermute x24, waiting for transfers between devices, left(): lax.ppermute(v, self.axis, self.leftward)  53.5 us
    ppermute x24, starting transfers between devices, right(): lax.ppermute(v, self.axis, self.rightward)  35.6 us
    unnamed x296, local copies, waits for them, and re-layouts  32.6 us
  transfers between devices with their start and end apart: 88, of which 33 were waited for; matrix products, arithmetic and copies ran while one was open for 15% of the time, Pallas kernels for 34%

profile of v2, /device:TPU:0, one launch (start us, length us, event | category | flops | bytes accessed | tf_op | source)
XLA Modules:
  0.0 915.5 jit_solution(11119677676577845472)
XLA Ops:
  31.5 17.0 %collective-permute-done.2.refs_2_ = bf16[512,512]{1,0:T(8,128)(2,1)S(1)} collective-permute-done((bf16[512,512]{1,0:T(8,128)(2,1)S(1)}, bf16[512,512]{1,0:T(8,128)(2,1)S(1)}, u32[]{:S(2)}, u32[]{:S(2)}) %collective-permute-start.2) | collective-permute-done | bytes 524320 | tf_op jit(solution)/shard_map/ppermute | solution.py:829
  60.0 19.9 %collective-permute-done.8.refs_3_ = bf16[1024,256]{1,0:T(8,128)(2,1)S(1)} collective-permute-done((bf16[1024,256]{1,0:T(8,128)(2,1)S(1)}, bf16[1024,256]{1,0:T(8,128)(2,1)S(1)}, u32[]{:S(2)}, u32[]{:S(2)}) %collective-permute-start.8) | collective-permute-done | bytes 524320 | tf_op jit(solution)/shard_map/ppermute | solution.py:829
  200.9 12.1 %collective-permute-done.32.refs_0_ = bf16[256,2048]{1,0:T(8,128)(2,1)} collective-permute-done((bf16[256,2048]{1,0:T(8,128)(2,1)S(1)}, bf16[256,2048]{1,0:T(8,128)(2,1)}, u32[]{:S(2)}, u32[]{:S(2)}) %collective-permute-start.32) | collective-permute-done | bytes 1048608 | tf_op jit(solution)/shard_map/ppermute | solution.py:638
  217.8 12.1 %experts.10 = (bf16[256,2176]{1,0:T(8,128)(2,1)}, bf16[256,2048]{1,0:T(8,128)(2,1)}, bf16[2048,1024]{1,0:T(8,128)(2,1)}, bf16[2048,2048]{1,0:T(8,128)(2,1)}, bf1...) custom-call(s32[12]{0:T(128)} %stack.72.numbers, bf16[256,2176]{1,0:T(8,128)(2,1)} %concatenate.136.refs_0_, ...), custom_call_target="tpu_custom_call" | custom-call | flops 2147483648 | bytes 6116693 | tf_op jit(solution)/shard_map/experts/pallas_call | solution.py:261
  229.8 31.0 %collective-permute-done.38.refs_0_ = bf16[256,2048]{1,0:T(8,128)(2,1)S(1)} collective-permute-done((bf16[256,2048]{1,0:T(8,128)(2,1)}, bf16[256,2048]{1,0:T(8,128)(2,1)S(1)}, u32[]{:S(2)}, u32[]{:S(2)}) %collective-permute-start.38) | collective-permute-done | bytes 1048608 | tf_op jit(solution)/shard_map/ppermute | solution.py:638
  266.8 19.7 %experts.11 = (bf16[256,2176]{1,0:T(8,128)(2,1)}, bf16[256,2176]{1,0:T(8,128)(2,1)}, bf16[256,2048]{1,0:T(8,128)(2,1)}, bf16[256,2048]{1,0:T(8,128)(2,1)}, bf16[...) custom-call(s32[12]{0:T(128)} %stack.72.numbers, ...), custom_call_target="tpu_custom_call", output_to_operand_aliasing={{4}: (11, {}), {5}: (12, {}), {6}: (13, {}), {7}: (14, {})} | custom-call | flops 4294967296 | bytes 8039082 | tf_op jit(solution)/shard_map/experts/pallas_call | solution.py:261
  299.0 13.4 %collective-permute-done.31.refs_2_ = bf16[256,2048]{1,0:T(8,128)(2,1)S(1)} collective-permute-done((bf16[256,2048]{1,0:T(8,128)(2,1)}, bf16[256,2048]{1,0:T(8,128)(2,1)S(1)}, u32[]{:S(2)}, u32[]{:S(2)}) %collective-permute-start.31) | collective-permute-done | bytes 1048608 | tf_op jit(solution)/shard_map/ppermute | solution.py:743
  317.4 19.8 %experts.12 = (bf16[256,2176]{1,0:T(8,128)(2,1)}, bf16[256,2176]{1,0:T(8,128)(2,1)}, bf16[256,2048]{1,0:T(8,128)(2,1)}, bf16[256,2048]{1,0:T(8,128)(2,1)}, bf16[...) custom-call(s32[12]{0:T(128)} %stack.72.numbers, ...), custom_call_target="tpu_custom_call", output_to_operand_aliasing={{4}: (11, {}), {5}: (12, {}), {6}: (13, {}), {7}: (14, {})} | custom-call | flops 4294967296 | bytes 8039082 | tf_op jit(solution)/shard_map/experts/pallas_call | solution.py:261
  355.6 19.8 %experts.13 = (bf16[256,2176]{1,0:T(8,128)(2,1)}, bf16[256,2176]{1,0:T(8,128)(2,1)}, bf16[256,2048]{1,0:T(8,128)(2,1)}, bf16[256,2048]{1,0:T(8,128)(2,1)}, bf16[...) custom-call(s32[12]{0:T(128)} %stack.72.numbers, ...), custom_call_target="tpu_custom_call", output_to_operand_aliasing={{4}: (11, {}), {5}: (12, {}), {6}: (13, {}), {7}: (14, {})} | custom-call | flops 4294967296 | bytes 8039082 | tf_op jit(solution)/shard_map/experts/pallas_call | solution.py:261
  378.2 12.5 %experts.14 = (bf16[256,2176]{1,0:T(8,128)(2,1)}, bf16[256,2048]{1,0:T(8,128)(2,1)}, bf16[2048,1024]{1,0:T(8,128)(2,1)}, bf16[2048,2048]{1,0:T(8,128)(2,1)}, bf1...) custom-call(s32[12]{0:T(128)} %stack.72.numbers, ...), custom_call_target="tpu_custom_call", output_to_operand_aliasing={{2}: (9, {}), {3}: (10, {}), {4}: (11, {}), {5}: (12, {})} | custom-call | flops 2147483648 | bytes 6116693 | tf_op jit(solution)/shard_map/experts/pallas_call | solution.py:261
  391.8 12.9 %experts.15 = (bf16[256,2176]{1,0:T(8,128)(2,1)}, bf16[256,2048]{1,0:T(8,128)(2,1)}, bf16[2048,1024]{1,0:T(8,128)(2,1)}, bf16[2048,2048]{1,0:T(8,128)(2,1)}) custom-call(s32[12]{0:T(128)} %stack.72.numbers, bf16[256,2176]{1,0:T(8,128)(2,1)} %constant_dynamic-update-slice_fusion.7.refs_0_, bf16[256,2048]{1,0:T(8,128)(2,1)} %copy-done.46, ...), custom_call_target="tpu_custom_call" | custom-call | flops 2147483648 | bytes 6116693 | tf_op jit(solution)/shard_map/experts/pallas_call | solution.py:261
  408.1 20.8 %experts.16 = (bf16[256,2176]{1,0:T(8,128)(2,1)}, bf16[256,2176]{1,0:T(8,128)(2,1)}, bf16[256,2048]{1,0:T(8,128)(2,1)}, bf16[256,2048]{1,0:T(8,128)(2,1)}, bf16[...) custom-call(s32[12]{0:T(128)} %stack.72.numbers, ...), custom_call_target="tpu_custom_call", output_to_operand_aliasing={{4}: (17, {}), {5}: (18, {})} | custom-call | flops 4294967296 | bytes 8039082 | tf_op jit(solution)/shard_map/experts/pallas_call | solution.py:261
  433.4 20.7 %experts.17 = (bf16[256,2176]{1,0:T(8,128)(2,1)}, bf16[256,2176]{1,0:T(8,128)(2,1)}, bf16[256,2048]{1,0:T(8,128)(2,1)}, bf16[256,2048]{1,0:T(8,128)(2,1)}, bf16[...) custom-call(s32[12]{0:T(128)} %stack.72.numbers, ...), custom_call_target="tpu_custom_call", output_to_operand_aliasing={{4}: (17, {}), {5}: (18, {})} | custom-call | flops 4294967296 | bytes 8039082 | tf_op jit(solution)/shard_map/experts/pallas_call | solution.py:261
  461.7 20.8 %experts.18 = (bf16[256,2176]{1,0:T(8,128)(2,1)}, bf16[256,2176]{1,0:T(8,128)(2,1)}, bf16[256,2048]{1,0:T(8,128)(2,1)}, bf16[256,2048]{1,0:T(8,128)(2,1)}, bf16[...) custom-call(s32[12]{0:T(128)} %stack.72.numbers, ...), custom_call_target="tpu_custom_call", output_to_operand_aliasing={{4}: (17, {}), {5}: (18, {})} | custom-call | flops 4294967296 | bytes 8039082 | tf_op jit(solution)/shard_map/experts/pallas_call | solution.py:261
  488.9 12.7 %experts.19 = (bf16[256,2176]{1,0:T(8,128)(2,1)}, bf16[256,2048]{1,0:T(8,128)(2,1)}, bf16[2048,1024]{1,0:T(8,128)(2,1)}, bf16[2048,2048]{1,0:T(8,128)(2,1)}) custom-call(s32[12]{0:T(128)} %stack.72.numbers, bf16[256,2176]{1,0:T(8,128)(2,1)} %concatenate.136.refs_0_, ...), custom_call_target="tpu_custom_call", output_to_operand_aliasing={{2}: (13, {}), {3}: (14, {})} | custom-call | flops 2147483648 | bytes 6116693 | tf_op jit(solution)/shard_map/experts/pallas_call | solution.py:261
  527.0 11.4 %collective-permute-done.51.refs_1_ = bf16[256,2176]{1,0:T(8,128)(2,1)S(1)} collective-permute-done((bf16[256,2176]{1,0:T(8,128)(2,1)S(1)}, bf16[256,2176]{1,0:T(8,128)(2,1)S(1)}, u32[]{:S(2)}, u32[]{:S(2)}) %collective-permute-start.51) | collective-permute-done | bytes 1114144 | tf_op jit(solution)/shard_map/ppermute | solution.py:641
  549.1 15.4 %slab_grads.10 = (bf16[2048,512]{1,0:T(8,128)(2,1)}, bf16[2048,512]{1,0:T(8,128)(2,1)}) custom-call(bf16[2048,2048]{1,0:T(8,128)(2,1)} %get-tuple-element.243.rows, bf16[2048,2048]{1,0:T(8,128)(2,1)} %get-tuple-element.244.kept, bf16[256,2048]{1,0:T(8,128)(2,1)} %copy-done.73), custom_call_target="tpu_custom_call" | custom-call | flops 2863311616 | bytes 5592405 | tf_op jit(solution)/shard_map/slab_grads/pallas_call | solution.py:337
  587.5 17.2 %slab_grads.11 = (bf16[2048,512]{1,0:T(8,128)(2,1)}, bf16[2048,512]{1,0:T(8,128)(2,1)}) custom-call(bf16[2048,2048]{1,0:T(8,128)(2,1)} %get-tuple-element.243.rows, bf16[2048,2048]{1,0:T(8,128)(2,1)} %get-tuple-element.244.kept, bf16[2048,512]{1,0:T(8,128)(2,1)} %collective-permute-done.58.refs_0_, bf16[2048,512]{1,0:T(8,128)(2,1)} %collective-permute-done.59.refs_1_, ...), custom_call_target="tpu_custom_call" | custom-call | flops 2863311616 | bytes 5592405 | tf_op jit(solution)/shard_map/slab_grads/pallas_call | solution.py:337
  620.2 26.9 %attend_back.1 = (bf16[1024,512]{1,0:T(8,128)(2,1)}, bf16[1024,512]{1,0:T(8,128)(2,1)}, bf16[1024,512]{1,0:T(8,128)(2,1)}, f32[2,128]{1,0:T(2,128)}) custom-call(bf16[1024,512]{1,0:T(8,128)(2,1)} %get-tuple-element.157.query.refs_1_.refs_2_, bf16[1024,512]{1,0:T(8,128)(2,1)} %get-tuple-element.158.key, bf16[1024,512]{1,0:T(8,128)(2,1)} %get-tuple-element.159.value, ...), custom_call_target="tpu_custom_call" | custom-call | flops 1789569664 | bytes 3844778 | tf_op jit(solution)/shard_map/attend_back/pallas_call | solution.py:541
  685.5 22.0 %collective-permute-done.64.refs_10_ = bf16[2048,512]{1,0:T(8,128)(2,1)S(1)} collective-permute-done((bf16[2048,512]{1,0:T(8,128)(2,1)}, bf16[2048,512]{1,0:T(8,128)(2,1)S(1)}, u32[]{:S(2)}, u32[]{:S(2)}) %collective-permute-start.64) | collective-permute-done | bytes 2097184 | tf_op jit(solution)/shard_map/ppermute | solution.py:743
  708.7 11.6 %rows_back.1 = (bf16[256,2048]{1,0:T(8,128)(2,1)}, bf16[256,2048]{1,0:T(8,128)(2,1)}, bf16[256,2048]{1,0:T(8,128)(2,1)}, bf16[256,2048]{1,0:T(8,128)(2,1)}) custom-call(bf16[1024,512]{1,0:T(8,128)(2,1)} %get-tuple-element.254.refs_2_.query.refs_0_, bf16[1024,512]{1,0:T(8,128)(2,1)} %get-tuple-element.258.key.refs_1_, ...), custom_call_target="tpu_custom_call" | custom-call | flops 2147483648 | bytes 4543829 | tf_op jit(solution)/shard_map/rows_back/pallas_call | solution.py:580
  757.6 15.3 %slab_grads.12 = (bf16[2048,512]{1,0:T(8,128)(2,1)}, bf16[2048,512]{1,0:T(8,128)(2,1)}) custom-call(bf16[2048,2048]{1,0:T(8,128)(2,1)} %get-tuple-element.243.rows, bf16[2048,2048]{1,0:T(8,128)(2,1)} %get-tuple-element.266.kept, bf16[256,2048]{1,0:T(8,128)(2,1)} %copy-done.38, bf16[256,2048]{1,0:T(8,128)(2,1)} %copy-done.37), custom_call_target="tpu_custom_call" | custom-call | flops 2863311616 | bytes 5592405 | tf_op jit(solution)/shard_map/slab_grads/pallas_call | solution.py:337
  834.9 17.0 %slab_grads.13 = (bf16[2048,512]{1,0:T(8,128)(2,1)}, bf16[2048,512]{1,0:T(8,128)(2,1)}) custom-call(bf16[2048,2048]{1,0:T(8,128)(2,1)} %get-tuple-element.243.rows, bf16[2048,2048]{1,0:T(8,128)(2,1)} %get-tuple-element.266.kept, bf16[2048,512]{1,0:T(8,128)(2,1)} %collective-permute-done.73.refs_0_, bf16[2048,512]{1,0:T(8,128)(2,1)} %collective-permute-done.74.refs_1_, ...), custom_call_target="tpu_custom_call" | custom-call | flops 2863311616 | bytes 5592405 | tf_op jit(solution)/shard_map/slab_grads/pallas_call | solution.py:337
  869.2 12.5 %collective-permute-done.84 = bf16[256,1024]{1,0:T(8,128)(2,1)} collective-permute-done((bf16[256,1024]{1,0:T(8,128)(2,1)}, bf16[256,1024]{1,0:T(8,128)(2,1)}, u32[]{:S(2)}, u32[]{:S(2)}) %collective-permute-start.84) | collective-permute-done | bytes 524320 | tf_op jit(solution)/shard_map/ppermute | solution.py:829
  (641 shorter events, 484.7 us)
Async XLA Ops:
  7.2 789.9 %all-reduce.2.cloned.1.call-start = ((), (), s32[]{:S(2)}) async-start(), calls=%async_computation | async-start | bytes 393216 | tf_op jit(solution)/shard_map/psum | solution.py:1201
  126.8 47.7 %collective-permute-start.15 = (bf16[2048,512]{1,0:T(8,128)(2,1)}, bf16[2048,512]{1,0:T(8,128)(2,1)S(1)}, u32[]{:S(2)}, u32[]{:S(2)}) collective-permute-start(bf16[2048,512]{1,0:T(8,128)(2,1)} %after.34), channel_id=1, source_target_pairs={{0,16},{8,24},{16,0},{24,8},{1,17},{9,25},{17,1},{25,9},{2,18},{10... | collective-permute-start | bytes 6291464 | tf_op jit(solution)/shard_map/ppermute | solution.py:743
  167.1 47.9 %collective-permute-start.21 = (bf16[2048,512]{1,0:T(8,128)(2,1)}, bf16[2048,512]{1,0:T(8,128)(2,1)}, u32[]{:S(2)}, u32[]{:S(2)}) collective-permute-start(bf16[2048,512]{1,0:T(8,128)(2,1)} %bitcast.62), channel_id=1, source_target_pairs={{0,8},{8,0},{16,24},{24,16},{1,9},{9,1},{17,25},{25,17},{2,10},{10... | collective-permute-start | bytes 6291464 | tf_op jit(solution)/shard_map/ppermute | solution.py:739
  196.1 67.2 %collective-permute-start.20 = (bf16[2048,512]{1,0:T(8,128)(2,1)}, bf16[2048,512]{1,0:T(8,128)(2,1)}, u32[]{:S(2)}, u32[]{:S(2)}) collective-permute-start(bf16[2048,512]{1,0:T(8,128)(2,1)} %after.36), channel_id=1, source_target_pairs={{0,16},{8,24},{16,0},{24,8},{1,17},{9,25},{17,1},{25,9},{2,18},{10... | collective-permute-start | bytes 6291464 | tf_op jit(solution)/shard_map/ppermute | solution.py:743
  213.0 48.3 %collective-permute-start.18 = (bf16[256,2176]{1,0:T(8,128)(2,1)}, bf16[256,2176]{1,0:T(8,128)(2,1)S(1)}, u32[]{:S(2)}, u32[]{:S(2)}) collective-permute-start(bf16[256,2176]{1,0:T(8,128)(2,1)} %concatenate.136.refs_0_), channel_id=1, source_target_pairs={{0,2},{2,4},{4,6},{6,7},{7,5},{5,3},{3,1},{1,0},{8,10},{10,12},{12... | collective-permute-start | bytes 3342344 | tf_op jit(solution)/shard_map/ppermute | solution.py:638
  214.1 47.2 %collective-permute-start.19 = (bf16[256,2176]{1,0:T(8,128)(2,1)}, bf16[256,2176]{1,0:T(8,128)(2,1)S(1)}, u32[]{:S(2)}, u32[]{:S(2)}) collective-permute-start(bf16[256,2176]{1,0:T(8,128)(2,1)} %concatenate.136.refs_0_), channel_id=1, source_target_pairs={{2,0},{4,2},{6,4},{7,6},{5,7},{3,5},{1,3},{0,1},{10,8},{12,10},{14... | collective-permute-start | bytes 3342344 | tf_op jit(solution)/shard_map/ppermute | solution.py:641
  215.1 45.8 %collective-permute-start.38 = (bf16[256,2048]{1,0:T(8,128)(2,1)}, bf16[256,2048]{1,0:T(8,128)(2,1)S(1)}, u32[]{:S(2)}, u32[]{:S(2)}) collective-permute-start(bf16[256,2048]{1,0:T(8,128)(2,1)} %get-tuple-element.181.refs_2_), channel_id=1, source_target_pairs={{0,2},{2,4},{4,6},{6,7},{7,5},{5,3},{3,1},{1,0},{8,10},{10,12},{12... | collective-permute-start | bytes 3145736 | tf_op jit(solution)/shard_map/ppermute | solution.py:638
  216.2 45.1 %collective-permute-start.39 = (bf16[256,2048]{1,0:T(8,128)(2,1)}, bf16[256,2048]{1,0:T(8,128)(2,1)}, u32[]{:S(2)}, u32[]{:S(2)}) collective-permute-start(bf16[256,2048]{1,0:T(8,128)(2,1)} %get-tuple-element.182.refs_3_), channel_id=1, source_target_pairs={{2,0},{4,2},{6,4},{7,6},{5,7},{3,5},{1,3},{0,1},{10,8},{12,10},{14... | collective-permute-start | bytes 3145736 | tf_op jit(solution)/shard_map/ppermute | solution.py:641
  292.5 44.7 %collective-permute-start.30 = (bf16[256,2176]{1,0:T(8,128)(2,1)}, bf16[256,2176]{1,0:T(8,128)(2,1)S(1)}, u32[]{:S(2)}, u32[]{:S(2)}) collective-permute-start(bf16[256,2176]{1,0:T(8,128)(2,1)} %get-tuple-element.179.refs_1_.refs_3_), channel_id=1, source_target_pairs={{2,0},{4,2},{6,4},{7,6},{5,7},{3,5},{1,3},{0,1},{10,8},{12,10},{14... | collective-permute-start | bytes 3342344 | tf_op jit(solution)/shard_map/ppermute | solution.py:641
  294.7 47.1 %collective-permute-start.42 = (bf16[128,2048]{1,0:T(8,128)(2,1)}, bf16[128,2048]{1,0:T(8,128)(2,1)}, u32[]{:S(2)}, u32[]{:S(2)}) collective-permute-start(bf16[128,2048]{1,0:T(8,128)(2,1)} %slice.359), channel_id=1, source_target_pairs={{0,2},{2,4},{4,6},{6,7},{7,5},{5,3},{3,1},{1,0},{8,10},{10,12},{12... | collective-permute-start | bytes 1572872 | tf_op jit(solution)/shard_map/ppermute | solution.py:638
  298.3 43.8 %collective-permute-start.43 = (bf16[128,2048]{1,0:T(8,128)(2,1)}, bf16[128,2048]{1,0:T(8,128)(2,1)}, u32[]{:S(2)}, u32[]{:S(2)}) collective-permute-start(bf16[128,2048]{1,0:T(8,128)(2,1)} %slice.360), channel_id=1, source_target_pairs={{2,0},{4,2},{6,4},{7,6},{5,7},{3,5},{1,3},{0,1},{10,8},{12,10},{14... | collective-permute-start | bytes 1572872 | tf_op jit(solution)/shard_map/ppermute | solution.py:641
  312.4 78.3 %collective-permute-start.34 = (bf16[2048,512]{1,0:T(8,128)(2,1)S(1)}, bf16[2048,512]{1,0:T(8,128)(2,1)}, u32[]{:S(2)}, u32[]{:S(2)}) collective-permute-start(bf16[2048,512]{1,0:T(8,128)(2,1)S(1)} %copy-done.2), channel_id=1, source_target_pairs={{0,8},{8,0},{16,24},{24,16},{1,9},{9,1},{17,25},{25,17},{2,10},{10... | collective-permute-start | bytes 6291464 | tf_op jit(solution)/shard_map/ppermute | solution.py:739
  317.4 73.3 %collective-permute-start.35 = (bf16[2048,512]{1,0:T(8,128)(2,1)}, bf16[2048,512]{1,0:T(8,128)(2,1)}, u32[]{:S(2)}, u32[]{:S(2)}) collective-permute-start(bf16[2048,512]{1,0:T(8,128)(2,1)} %get-tuple-element.165.refs_3_.refs_5_), channel_id=1, source_target_pairs={{0,8},{8,0},{16,24},{24,16},{1,9},{9,1},{17,25},{25,17},{2,10},{10... | collective-permute-start | bytes 6291464 | tf_op jit(solution)/shard_map/ppermute | solution.py:739
  341.8 48.9 %collective-permute-start.36 = (bf16[256,2048]{1,0:T(8,128)(2,1)S(1)}, bf16[256,2048]{1,0:T(8,128)(2,1)}, u32[]{:S(2)}, u32[]{:S(2)}) collective-permute-start(bf16[256,2048]{1,0:T(8,128)(2,1)S(1)} %copy-done.13), channel_id=1, source_target_pairs={{0,8},{8,0},{16,24},{24,16},{1,9},{9,1},{17,25},{25,17},{2,10},{10... | collective-permute-start | bytes 3145736 | tf_op jit(solution)/shard_map/ppermute | solution.py:739
  565.0 47.7 %collective-permute-start.57 = (bf16[512,2048]{1,0:T(8,128)(2,1)S(1)}, bf16[512,2048]{1,0:T(8,128)(2,1)}, u32[]{:S(2)}, u32[]{:S(2)}) collective-permute-start(bf16[512,2048]{1,0:T(8,128)(2,1)S(1)} %copy-done.41), channel_id=1, source_target_pairs={{0,16},{8,24},{16,0},{24,8},{1,17},{9,25},{17,1},{25,9},{2,18},{10... | collective-permute-start | bytes 6291464 | tf_op jit(solution)/shard_map/ppermute | solution.py:743
  656.1 75.8 %collective-permute-start.65 = (bf16[1024,2048]{1,0:T(8,128)(2,1)}, bf16[1024,2048]{1,0:T(8,128)(2,1)}, u32[]{:S(2)}, u32[]{:S(2)}) collective-permute-start(bf16[1024,2048]{1,0:T(8,128)(2,1)} %weight_back.2.refs_0_), channel_id=1, source_target_pairs={{0,8},{8,0},{16,24},{24,16},{1,9},{9,1},{17,25},{25,17},{2,10},{10... | collective-permute-start | bytes 12582920 | tf_op jit(solution)/shard_map/ppermute | solution.py:739
  658.4 49.0 %collective-permute-start.64 = (bf16[2048,512]{1,0:T(8,128)(2,1)}, bf16[2048,512]{1,0:T(8,128)(2,1)S(1)}, u32[]{:S(2)}, u32[]{:S(2)}) collective-permute-start(bf16[2048,512]{1,0:T(8,128)(2,1)} %get-tuple-element.247.refs_3_), channel_id=1, source_target_pairs={{0,16},{8,24},{16,0},{24,8},{1,17},{9,25},{17,1},{25,9},{2,18},{10... | collective-permute-start | bytes 6291464 | tf_op jit(solution)/shard_map/ppermute | solution.py:743
  683.4 66.6 %collective-permute-start.63 = (bf16[256,2048]{1,0:T(8,128)(2,1)}, bf16[256,2048]{1,0:T(8,128)(2,1)}, u32[]{:S(2)}, u32[]{:S(2)}) collective-permute-start(bf16[256,2048]{1,0:T(8,128)(2,1)} %get-tuple-element.257), channel_id=1, source_target_pairs={{2,0},{4,2},{6,4},{7,6},{5,7},{3,5},{1,3},{0,1},{10,8},{12,10},{14... | collective-permute-start | bytes 3145736 | tf_op jit(solution)/shard_map/ppermute | solution.py:641
  683.8 71.2 %collective-permute-start.62 = (bf16[256,2048]{1,0:T(8,128)(2,1)}, bf16[256,2048]{1,0:T(8,128)(2,1)}, u32[]{:S(2)}, u32[]{:S(2)}) collective-permute-start(bf16[256,2048]{1,0:T(8,128)(2,1)} %get-tuple-element.255), channel_id=1, source_target_pairs={{0,2},{2,4},{4,6},{6,7},{7,5},{5,3},{3,1},{1,0},{8,10},{10,12},{12... | collective-permute-start | bytes 3145736 | tf_op jit(solution)/shard_map/ppermute | solution.py:638
  730.2 47.3 %collective-permute-start.86 = (bf16[512,2048]{1,0:T(8,128)(2,1)}, bf16[512,2048]{1,0:T(8,128)(2,1)}, u32[]{:S(2)}, u32[]{:S(2)}) collective-permute-start(bf16[512,2048]{1,0:T(8,128)(2,1)} %slab_grads.14), channel_id=1, source_target_pairs={{0,8},{8,0},{16,24},{24,16},{1,9},{9,1},{17,25},{25,17},{2,10},{10... | collective-permute-start | bytes 6291464 | tf_op jit(solution)/shard_map/ppermute | solution.py:739
  772.9 62.0 %collective-permute-start.73 = (bf16[2048,512]{1,0:T(8,128)(2,1)}, bf16[2048,512]{1,0:T(8,128)(2,1)}, u32[]{:S(2)}, u32[]{:S(2)}) collective-permute-start(bf16[2048,512]{1,0:T(8,128)(2,1)} %get-tuple-element.267.refs_3_), channel_id=1, source_target_pairs={{0,8},{8,0},{16,24},{24,16},{1,9},{9,1},{17,25},{25,17},{2,10},{10... | collective-permute-start | bytes 6291464 | tf_op jit(solution)/shard_map/ppermute | solution.py:739
  775.4 59.5 %collective-permute-start.74 = (bf16[2048,512]{1,0:T(8,128)(2,1)}, bf16[2048,512]{1,0:T(8,128)(2,1)}, u32[]{:S(2)}, u32[]{:S(2)}) collective-permute-start(bf16[2048,512]{1,0:T(8,128)(2,1)} %get-tuple-element.268.refs_4_), channel_id=1, source_target_pairs={{0,8},{8,0},{16,24},{24,16},{1,9},{9,1},{17,25},{25,17},{2,10},{10... | collective-permute-start | bytes 6291464 | tf_op jit(solution)/shard_map/ppermute | solution.py:739
  776.4 75.5 %collective-permute-start.83 = (bf16[256,2048]{1,0:T(8,128)(2,1)}, bf16[256,2048]{1,0:T(8,128)(2,1)S(1)}, u32[]{:S(2)}, u32[]{:S(2)}) collective-permute-start(bf16[256,2048]{1,0:T(8,128)(2,1)} %after.57), channel_id=1, source_target_pairs={{0,16},{8,24},{16,0},{24,8},{1,17},{9,25},{17,1},{25,9},{2,18},{10... | collective-permute-start | bytes 3145736 | tf_op jit(solution)/shard_map/ppermute | solution.py:743
  852.9 51.3 %collective-permute-start.85 = (bf16[2048,512]{1,0:T(8,128)(2,1)}, bf16[2048,512]{1,0:T(8,128)(2,1)}, u32[]{:S(2)}, u32[]{:S(2)}) collective-permute-start(bf16[2048,512]{1,0:T(8,128)(2,1)} %after.59), channel_id=1, source_target_pairs={{0,16},{8,24},{16,0},{24,8},{1,17},{9,25},{17,1},{25,9},{2,18},{10... | collective-permute-start | bytes 6291464 | tf_op jit(solution)/shard_map/ppermute | solution.py:743
  (206 other events, 2486.0 us)
Sparse Core Ops, SparseCore 0:
  658.5 124.7 all-reduce.1

commit v3 on v2

--- a/solution.py
+++ b/solution.py
@@ -47,9 +47,9 @@
     return jnp.dot(left_side, right_side, preferred_element_type=jnp.float32)
 
 
-def cost(flops, moved, exps=0):
+def cost(flops, moved, share):
     return pl.CostEstimate(
-        flops=int(flops) // 3, bytes_accessed=int(moved) // 3, transcendentals=int(exps) // 3
+        flops=int(flops / share), bytes_accessed=int(moved / share), transcendentals=0
     )
 
 
@@ -74,7 +74,7 @@
         out_specs=[ANYWHERE] * len(leaves),
         out_shape=[Shape(leaf.shape, leaf.dtype) for leaf in leaves],
         input_output_aliases={i: i for i in range(len(leaves))},
-        cost_estimate=cost(0, 0),
+        cost_estimate=cost(0, 0, 1),
         name="after",
     )(*leaves, *tokens)
     return jax.tree.unflatten(tree, out)
@@ -82,6 +82,25 @@
 
 def fresh_body(value, *refs):
     refs[-1][...] = value[...]
+
+
+def stack_body(count, *refs):
+    for i in range(count):
+        pl.when(pl.program_id(0) == i)(functools.partial(fresh_body, refs[i], refs[-1]))
+
+
+def stack(values, *tokens):
+    tokens, count, (rows, columns) = jax.tree.leaves(tokens), len(values), values[0].shape
+    return pl.pallas_call(
+        functools.partial(stack_body, count),
+        grid=(count,),
+        in_specs=[fixed_block((rows, columns))] * count + [ANYWHERE] * len(tokens),
+        out_specs=pl.BlockSpec((rows, columns), lambda i: (i, 0)),
+        out_shape=Shape((count * rows, columns), values[0].dtype),
+        compiler_params=roomy(),
+        cost_estimate=cost(0, 4 * count * rows * columns, 2),
+        name="stack",
+    )(*values, *tokens)
 
 
 def fresh(value, first, rows, *tokens, steps=2):
@@ -96,19 +115,19 @@
         out_specs=pl.BlockSpec((step, value.shape[1]), lambda i: (i, 0)),
         out_shape=Shape((rows, value.shape[1]), value.dtype),
         compiler_params=roomy(),
-        cost_estimate=cost(0, 4 * rows * value.shape[1]),
+        cost_estimate=cost(0, 4 * rows * value.shape[1], 2),
         name="fresh",
     )(value, *tokens)
 
 
-def experts_body(blocks, experts, pieces, begun, given, ids_at, spots_at, numbers, *refs):
-    refs, slabs = list(refs), len(pieces)
+def experts_body(blocks, experts, slabs, begun, given, ids_at, slabs_at, spots_at, numbers, *refs):
+    refs = list(refs)
 
     def take(count):
         return [refs.pop(0) for _ in range(count)]
 
     rows_in, cot_in = take(blocks), take(blocks)
-    mats = [[take(count) for count in counts] for counts in pieces]
+    mats = [take(3) for _ in range(slabs)]
     start_rows, start_mixed = take(blocks * begun), take(blocks * begun)
     take(given)
     rows_out, mixed_out, kept_w_out, kept_g_out = take(blocks), take(blocks), *take(2)
@@ -139,19 +158,25 @@
             load(start_rows[b].at[:, rest], extra_begin.at[spans[b]]) for b in range(blocks)
         ]
 
-    def load_mat(parts, target):
-        height = parts[0].shape[0]
-        return [load(part, target.at[pl.ds(p * height, height)]) for p, part in enumerate(parts)]
+    def slab_rows(s, rows, first=0):
+        if slabs_at[s] is None:
+            return pl.ds(first, rows)
+        return pl.ds(pl.multiple_of(numbers[slabs_at[s]] * rows, rows), rows)
 
     def load_pre(s):
         gate, up, _ = mats[s]
-        return load_mat(gate, both.at[s, :, pl.ds(0, hidden)]) + load_mat(
-            up, both.at[s, :, pl.ds(hidden, hidden)]
-        )
+        last = up.shape[0] - width if slabs_at[s] is None else 0
+        return [
+            load(gate.at[slab_rows(s, width)], both.at[s, :, pl.ds(0, hidden)]),
+            load(up.at[slab_rows(s, width, last)], both.at[s, :, pl.ds(hidden, hidden)]),
+        ]
+
+    def load_down(s):
+        return load(mats[s][2].at[slab_rows(s, hidden)], down.at[s])
 
     mat_loads = [load_pre(0)]
     cot_loads = [load(cot_in[b], cot.at[spans[b]]) for b in range(blocks)]
-    down_loads = [load_mat(mats[0][2], down.at[0])]
+    down_loads = [load_down(0)]
     if begun:
         begin_loads = [
             [load(start_rows[b].at[:, main], begin.at[0, spans[b]]) for b in range(blocks)],
@@ -159,7 +184,7 @@
         ]
     for s in range(1, slabs):
         mat_loads.append(load_pre(s))
-        down_loads.append(load_mat(mats[s][2], down.at[s]))
+        down_loads.append(load_down(s))
     for copy in extra_loads:
         copy.wait()
     gates = extra[:, :experts].astype(FULL) + extra[:, experts : 2 * experts].astype(FULL)
@@ -177,8 +202,7 @@
             for held, copy_out in zip((rows, cot), copies):
                 for b in range(blocks):
                     store(held.at[spans[b]], copy_out.at[spots[b]])
-        for copy in down_loads[s]:
-            copy.wait()
+        down_loads[s].wait()
         plain_grad = outer_rows(cot[...], down[s])
         hit = lax.broadcasted_iota(jnp.int32, gates.shape, 1) == numbers[ids_at[s]]
         gate = jnp.sum(jnp.where(hit, gates, 0.0), axis=1, keepdims=True)
@@ -230,19 +254,28 @@
 
 
 def experts_call(
-    experts, numbers, ids_at, spots_at, rows, cot, mats, start, shared, total_rows, tokens
+    experts,
+    numbers,
+    ids_at,
+    slabs_at,
+    spots_at,
+    rows,
+    cot,
+    mats,
+    start,
+    shared,
+    total_rows,
+    tokens,
 ):
     blocks, slabs = len(rows), len(mats)
     size, width = cot[0].shape
     extra = rows[0].shape[1] - width
-    hidden, total = mats[0][0][0].shape[1], blocks * size
-    pieces = [[len(parts) for parts in trio] for trio in mats]
-    piece_count = sum(map(sum, pieces))
+    hidden, total = mats[0][0].shape[1], blocks * size
     operands = [numbers, *rows, *cot]
     specs = [pl.BlockSpec(memory_space=pltpu.SMEM)] + [ANYWHERE] * (2 * blocks)
     for trio in mats:
-        operands += [part for parts in trio for part in parts]
-    specs += [ANYWHERE] * piece_count
+        operands += trio
+    specs += [ANYWHERE] * (3 * slabs)
     if start is not None:
         operands += [*start[0], *start[1]]
         specs += [ANYWHERE] * (2 * blocks)
@@ -263,10 +296,11 @@
             experts_body,
             blocks,
             experts,
-            pieces,
+            slabs,
             int(start is not None),
             given,
             ids_at,
+            slabs_at,
             spots_at,
         ),
         in_specs=specs,
@@ -290,68 +324,75 @@
             pltpu.VMEM((total, extra), LOW),
             pltpu.VMEM((total, extra), LOW),
             pltpu.VMEM((total, extra), LOW),
-            pltpu.SemaphoreType.DMA((6 * blocks + piece_count,)),
+            pltpu.SemaphoreType.DMA((6 * blocks + 3 * slabs,)),
             pltpu.SemaphoreType.DMA((2 * slabs * blocks + 7 * blocks,)),
         ],
         compiler_params=roomy(),
-        cost_estimate=cost(
-            12 * total * width * hidden * slabs,
-            6 * width * hidden * slabs + 8 * total * width + 6 * total * hidden * slabs,
-            total * hidden * slabs,
-        ),
+        cost_estimate=cost(12 * total * width * hidden * slabs, 0, 2.7),
         name="experts",
     )(*operands)
     return out[:blocks], out[blocks:outs], out[outs:]
 
 
-def slab_grads_body(swapped, parts, term_count, rows, kept, *refs):
-    terms, outs = refs[: term_count * parts], refs[-parts:]
-    found = inner_rows(kept[...], rows[...])
+def slab_grads_body(swapped, parts, joined, rows, kept, *refs):
+    outs = refs[-parts:]
+    step, half = pl.program_id(0), pl.num_programs(0) // 2
+    total = inner_rows(kept[...], rows[...])
     if swapped:
-        found = found.astype(LOW).T.astype(FULL)
-    steps = pl.num_programs(0) // parts
+        total = total.astype(LOW).T.astype(FULL)
+    terms, refs = [], list(refs)
+    for one in joined:
+        if one:
+            total = total + refs.pop(0)[...].astype(FULL)
+        else:
+            terms.append((refs.pop(0), refs.pop(0)))
+    if parts == 1:
+        outs[0][...] = total.astype(outs[0].dtype)
+        return
 
     def put(part):
-        total = found
-        for term in terms[part::parts]:
-            total = total + term[...].astype(FULL)
-        outs[part][...] = total.astype(LOW)
-
-    for part in range(parts):
-        pl.when(pl.program_id(0) // steps == part)(functools.partial(put, part))
-
-
-def slab_grads_call(rows, kept, first, count, parts, swapped, terms, tokens, step=256):
+        found = total
+        for pair in terms:
+            found = found + pair[part][...].astype(FULL)
+        outs[part][...] = found.astype(outs[part].dtype)
+
+    pl.when(step < half)(functools.partial(put, 0))
+    pl.when(step >= half)(functools.partial(put, 1))
+
+
+def slab_grads_call(rows, kept, first, count, swapped, terms, tokens, parts=1, kind=LOW, step=256):
     total, width = rows.shape
     at, steps = first // step, count // step
-
-    def spec(part):
-        def place(i):
-            return jnp.clip(i - part * steps, 0, steps - 1)
-
-        if swapped:
-            return pl.BlockSpec((width, step), lambda i: (0, place(i)))
-        return pl.BlockSpec((step, width), lambda i: (place(i), 0))
-
-    specs = [spec(part) for part in range(parts)]
+    if swapped:
+        spec = pl.BlockSpec((width, step), lambda i: (i // steps, i % steps))
+        shape = (2 * width, count)
+    else:
+        spec = pl.BlockSpec((step, width), lambda i: (i, 0))
+        shape = (count, width)
+    apart = [
+        pl.BlockSpec((width, step), lambda i: (0, jnp.minimum(i, steps - 1))),
+        pl.BlockSpec((width, step), lambda i: (0, jnp.maximum(i - steps, 0))),
+    ]
+    out_specs, out_shapes = [spec], [Shape(shape, kind)]
+    if parts == 2:
+        out_specs, out_shapes = apart, [Shape((width, count), kind)] * 2
+    joined = [not isinstance(term, (list, tuple)) for term in terms]
+    term_specs = [part for one in joined for part in ([spec] if one else apart)]
     return pl.pallas_call(
-        functools.partial(slab_grads_body, swapped, parts, len(terms)),
-        grid=(parts * steps,),
+        functools.partial(slab_grads_body, swapped, parts, joined),
+        grid=((2 if swapped else 1) * steps,),
         in_specs=[
             pl.BlockSpec((total, width), lambda i: (0, 0), pipeline_mode=pl.Buffered(1)),
             pl.BlockSpec((total, step), lambda i: (0, at + i)),
         ]
-        + specs * len(terms)
+        + term_specs
         + [ANYWHERE] * len(tokens),
-        out_specs=specs,
-        out_shape=[Shape((width, count) if swapped else (count, width), LOW)] * parts,
+        out_specs=out_specs,
+        out_shape=out_shapes,
         compiler_params=roomy(),
-        cost_estimate=cost(
-            2 * total * width * count * parts,
-            2 * total * width + 2 * (total + width) * count * parts,
-        ),
+        cost_estimate=cost(2 * total * width * count * (2 if swapped else 1), 0, 3),
         name="slab_grads",
-    )(rows, kept, *[part for term in terms for part in term], *tokens)
+    )(rows, kept, *jax.tree.leaves(terms), *tokens)
 
 
 def rope_tables(length, head_size):
@@ -366,8 +407,8 @@
     return pltpu.roll(vectors, vectors.shape[1] // 2, 1)
 
 
-def project_body(rows, query, query_rest, key, key_rest, value, value_rest, gains, tables, *refs):
-    query_proj, query_low, key_proj, key_low, value_low = refs
+def project_body(rows, query, query_rest, key, key_rest, gains, tables, *refs):
+    query_proj, query_low, key_proj, key_low = refs[-4:]
     half = query.shape[0]
 
     def both_halves(mat, rest):
@@ -387,10 +428,9 @@
             head = head * lax.rsqrt(jnp.mean(head * head, axis=-1, keepdims=True) + EPSILON)
             head = head * gain
             low_out[:, columns] = (head * cos_two + half_turn(head) * sin_two).astype(LOW)
-    value_low[...] = both_halves(value, value_rest).astype(LOW)
-
-
-def project_call(rows, mats, gains, tables):
+
+
+def project_call(rows, mats, gains, tables, tokens):
     total, width = rows.shape
     mats = [half for halves in mats for half in halves]
     columns, step = mats[0].shape[1], min(256, total)
@@ -401,15 +441,41 @@
         grid=(total // step,),
         in_specs=[pl.BlockSpec((step, width), lambda i: (i, 0))]
         + [fixed_block(mat.shape) for mat in mats]
-        + [fixed_block(gains.shape), pl.BlockSpec((step, tables.shape[1]), lambda i: (i, 0))],
-        out_specs=[row_block] * 5,
-        out_shape=[full, low, full, low, low],
+        + [fixed_block(gains.shape), pl.BlockSpec((step, tables.shape[1]), lambda i: (i, 0))]
+        + [ANYWHERE] * len(tokens),
+        out_specs=[row_block] * 4,
+        out_shape=[full, low, full, low],
         compiler_params=roomy(),
-        cost_estimate=cost(
-            6 * total * width * columns, 2 * total * width + 6 * width * columns + 14 * total * columns
-        ),
+        cost_estimate=cost(4 * total * width * columns, 0, 2),
         name="project",
-    )(rows, *mats, gains, tables)
+    )(rows, *mats, gains, tables, *tokens)
+
+
+def value_body(rows, mat, rest, *refs):
+    half = mat.shape[0]
+    refs[-1][...] = (
+        plain_dot(rows[:, :half], mat[...]) + plain_dot(rows[:, half:], rest[...])
+    ).astype(LOW)
+
+
+def value_call(rows, mat, rest, tokens):
+    total, width = rows.shape
+    columns, step = mat.shape[1], min(256, total)
+    return pl.pallas_call(
+        value_body,
+        grid=(total // step,),
+        in_specs=[
+            pl.BlockSpec((step, width), lambda i: (i, 0)),
+            fixed_block(mat.shape),
+            fixed_block(rest.shape),
+        ]
+        + [ANYWHERE] * len(tokens),
+        out_specs=pl.BlockSpec((step, columns), lambda i: (i, 0)),
+        out_shape=Shape((total, columns), LOW),
+        compiler_params=roomy(),
+        cost_estimate=cost(2 * total * width * columns, 0, 2),
+        name="values",
+    )(rows, mat, rest, *tokens)
 
 
 def held_pairs(seg_col, seg_row, pos_col, pos_row):
@@ -456,9 +522,7 @@
         out_specs=pl.BlockSpec((rows, size), lambda h: (0, h)),
         out_shape=Shape((rows, columns), LOW),
         compiler_params=roomy(),
-        cost_estimate=cost(
-            4 * rows * total * columns, 4 * (total + rows) * columns, rows * total * heads
-        ),
+        cost_estimate=cost(4 * rows * total * columns, 0, 0.5),
         name="attend",
     )(query, key, value, *places, *tokens)
 
@@ -532,25 +596,56 @@
     grad_gains[1:2] += key_gain_part
 
 
-def attend_back_call(query, key, value, grad, query_proj, key_proj, gains, tables, places):
+def attend_back_call(
+    query, key, value, grad, query_proj, key_proj, gains, tables, places, tokens
+):
     total, columns = query.shape
     size = gains.shape[1]
     heads, step = columns // size, min(256, total)
     head = pl.BlockSpec((total, size), lambda h: (0, h))
     fixed = (gains, tables, *places)
     return pl.pallas_call(
-        functools.partial(attend_back_body, step),
+        lambda *refs: attend_back_body(
+            step, *refs[: 6 + len(fixed)], *refs[6 + len(fixed) + len(tokens) :]
+        ),
         grid=(heads,),
-        in_specs=[head] * 6 + [fixed_block(a.shape) for a in fixed],
+        in_specs=[head] * 6
+        + [fixed_block(a.shape) for a in fixed]
+        + [ANYWHERE] * len(tokens),
         out_specs=[head] * 3 + [fixed_block((2, size))],
         out_shape=[Shape((total, columns), LOW)] * 3 + [Shape((2, size), FULL)],
         scratch_shapes=[pltpu.VMEM((total, size), FULL)] * 3,
         compiler_params=roomy(),
-        cost_estimate=cost(
-            10 * total * total * columns, 22 * total * columns, total * total * heads
-        ),
+        cost_estimate=cost(10 * total * total * columns, 0, 5),
         name="attend_back",
-    )(query, key, value, grad, query_proj, key_proj, *fixed)
+    )(query, key, value, grad, query_proj, key_proj, *fixed, *tokens)
+
+
+def attended_back_body(count, mat, *refs):
+    out = refs[-1]
+    size = refs[0].shape[0]
+    for b in range(count):
+        out[b * size : (b + 1) * size] = outer_rows(refs[b][...], mat[...]).astype(LOW)
+
+
+def attended_back_call(blocks, mat, given, first, total):
+    size, width = blocks[0].shape
+    columns, count = mat.shape[0], len(blocks)
+    at = first // (count * size)
+    given = [] if given is None else [given]
+    return pl.pallas_call(
+        functools.partial(attended_back_body, count),
+        grid=(1,),
+        in_specs=[fixed_block((columns, width))]
+        + [fixed_block((size, width))] * count
+        + [ANYWHERE] * len(given),
+        out_specs=pl.BlockSpec((count * size, columns), lambda i: (at, 0)),
+        out_shape=Shape((total, columns), LOW),
+        input_output_aliases={1 + count: 0} if given else {},
+        compiler_params=roomy(),
+        cost_estimate=cost(2 * count * size * width * columns, 0, 10),
+        name="attended_back",
+    )(mat, *blocks, *given)
 
 
 def rows_back_body(count, *refs):
@@ -587,40 +682,77 @@
         out_specs=[pl.BlockSpec((size, step), lambda i: (0, i))] * blocks,
         out_shape=[Shape((size, 2 * half), LOW)] * blocks,
         compiler_params=roomy(),
-        cost_estimate=cost(
-            4 * count * rows * columns * half,
-            2 * count * (rows * columns + 2 * columns * half) + 4 * rows * half,
-        ),
+        cost_estimate=cost(4 * count * rows * columns * half, 0, 2.5),
         name="rows_back",
     )(*grads, *[mat[0] for mat in mats], *[mat[1] for mat in mats], *tokens)
 
 
-def weight_back_body(columns, rows, branch, query, key, value, attended, *refs):
-    out = refs[-1]
-    for place, (left, right) in enumerate(
-        ((rows, query), (rows, key), (rows, value), (branch, attended))
-    ):
+def weight_back_body(columns, count, rows, query, key, value, *refs):
+    branch, attended, out = refs[:count], refs[count : 2 * count], refs[-1]
+    for place, right in enumerate((query, key, value)):
         out[:, place * columns : (place + 1) * columns] = inner_rows(
-            left[...], right[...]
+            rows[...], right[...]
         ).astype(LOW)
+    out[:, 3 * columns :] = sum(
+        inner_rows(left[...], right[...]) for left, right in zip(branch, attended)
+    ).astype(LOW)
 
 
 def weight_back_call(rows, branch, grads, attended, half, tokens, step=512):
-    (total, width), columns = rows.shape, attended.shape[1]
+    (total, width), (size, columns), count = rows.shape, attended[0].shape, len(branch)
     steps = width // 2 // step
-    part = pl.BlockSpec((total, step), lambda i: (0, half * steps + i))
+
+    def part(height):
+        return pl.BlockSpec((height, step), lambda i: (0, half * steps + i))
+
     return pl.pallas_call(
-        functools.partial(weight_back_body, columns),
+        lambda *refs: weight_back_body(
+            columns, count, *refs[: 4 + 2 * count], refs[-1]
+        ),
         grid=(steps,),
-        in_specs=[part, part] + [fixed_block((total, columns))] * 4 + [ANYWHERE] * len(tokens),
+        in_specs=[part(total)]
+        + [fixed_block((total, columns))] * 3
+        + [part(size)] * count
+        + [fixed_block((size, columns))] * count
+        + [ANYWHERE] * len(tokens),
         out_specs=pl.BlockSpec((step, 4 * columns), lambda i: (i, 0)),
         out_shape=Shape((width // 2, 4 * columns), LOW),
         compiler_params=roomy(),
-        cost_estimate=cost(
-            4 * total * width * columns, 2 * total * width + 8 * (total + width // 2) * columns
-        ),
+        cost_estimate=cost(4 * total * width * columns, 0, 2.5),
         name="weight_back",
-    )(rows, branch, *grads, attended, *tokens)
+    )(rows, *grads, *branch, *attended, *tokens)
+
+
+def gain_body(columns, others, mine, *refs):
+    mats, out = refs[:6], refs[-1]
+    half = mine.shape[0]
+    for place, grads in enumerate((mine, others)):
+        out[place * half : (place + 1) * half] = sum(
+            jnp.sum(
+                grads[:, m * columns : (m + 1) * columns].astype(FULL)
+                * mats[2 * m + place][...].astype(FULL),
+                axis=1,
+                keepdims=True,
+            )
+            for m in range(3)
+        )
+
+
+def gain_call(others, mine, mats, columns, tokens):
+    half = mine.shape[0]
+    part = fixed_block((half, 3 * columns))
+    return pl.pallas_call(
+        functools.partial(gain_body, columns),
+        grid=(1,),
+        in_specs=[part, part]
+        + [fixed_block((half, columns))] * 6
+        + [ANYWHERE] * len(tokens),
+        out_specs=fixed_block((2 * half, 1)),
+        out_shape=Shape((2 * half, 1), FULL),
+        compiler_params=roomy(),
+        cost_estimate=cost(0, 12 * half * columns, 2),
+        name="gain",
+    )(others, mine, *mats, *tokens)
 
 
 class Ring:
@@ -677,19 +809,20 @@
 class Spread:
     def __init__(self, ring, value):
         self.ring, self.pair, self.blocks, self.hops = ring, (value, value), [value], 0
+        self.settled = True
 
     def hop(self, *tokens):
         ring = self.ring
-        if self.hops:
+        if not self.settled:
             self.settle(*tokens)
         left, right = self.pair
-        self.hops += 1
+        self.hops, self.settled = self.hops + 1, False
         if self.hops == ring.count // 2:
             left, right = left[: left.shape[0] // 2], right[right.shape[0] // 2 :]
         self.pair = (ring.right(left), ring.left(right))
 
     def settle(self, *tokens):
-        self.pair = after(self.pair, *tokens)
+        self.pair, self.settled = after(self.pair, *tokens), True
         if self.hops == self.ring.count // 2:
             self.blocks.append(jnp.concatenate(self.pair))
         else:
@@ -722,6 +855,7 @@
             if tokens:
                 sent = after(sent, *tokens)
             self.pair = (ring.right(sent[0]), ring.left(sent[1]))
+        self.sent = sent
         return sent
 
     def total(self, own):
@@ -741,6 +875,22 @@
     def along(self, value, shift):
         pairs = [(i, (i + 2 * shift) % self.count) for i in range(self.count)]
         return jax.tree.map(lambda v: lax.ppermute(v, "expert", pairs), value)
+
+    def over_cores(self, value):
+        groups = [[2 * i, 2 * i + 1] for i in range(self.chips)]
+        return lax.all_gather(value, "expert", axis_index_groups=groups, axis=0, tiled=True)
+
+    def from_core(self, value):
+        rows = value.shape[0]
+        at = (self.here + 1) % 2 * rows
+        return lax.dynamic_slice_in_dim(self.over_cores(value), at, rows, 0)
+
+    def over_chips(self, value, shift):
+        groups = [[2 * i + core for i in range(self.chips)] for core in range(2)]
+        found = lax.all_gather(value, "expert", axis_index_groups=groups, axis=0, tiled=True)
+        rows = value.shape[0]
+        at = (self.here // 2 + shift) % self.chips
+        return lax.dynamic_slice_in_dim(found, at * rows, rows, 0)
 
     def listed(self):
         chip, core = self.here // 2, self.here % 2
@@ -782,14 +932,21 @@
         return self.pick_columns(rows, self.places())
 
 
-def everywhere(value):
-    for axis in ("expert", "tensor"):
-        size, step = lax.axis_size(axis), 1
-        while step < size:
-            pairs = [(i, i ^ step) for i in range(size)]
-            value = jax.tree.map(lambda v: v + lax.ppermute(v, axis, pairs), value)
-            step *= 2
-    return value
+class Everywhere:
+    def __init__(self, value):
+        self.value, self.own, self.hops = None, value, []
+        for axis in ("expert", "tensor"):
+            size, step = lax.axis_size(axis), 1
+            while step < size:
+                self.hops.append((axis, [(i, i ^ step) for i in range(size)]))
+                step *= 2
+        self.hops = [self.hops[0], self.hops[-1], *self.hops[1:-1]]
+
+    def hop(self):
+        if self.value is not None:
+            self.own, self.value = self.own + self.value, None
+        if self.hops:
+            self.value = lax.ppermute(self.own, *self.hops.pop(0))
 
 
 def per_device(
@@ -838,61 +995,55 @@
     own_slab = (w_gate[0], w_up[0], w_down[0])
     copies = [
         fresh(cotangent, 0, tok_rows, normed_one),
-        fresh(own_slab[0], 0, model_width, normed_one),
-        fresh(own_slab[1], 0, model_width, normed_one),
-        fresh(own_slab[2], 0, hidden // 2, normed_one),
-        fresh(own_slab[2], hidden // 2, hidden // 2, normed_one),
+        stack(own_slab[:2], normed_one),
+        fresh(own_slab[2], 0, hidden, normed_one),
+        fresh(w_value, 0, w_value.shape[0], normed_one),
+        fresh(w_out, 0, w_out.shape[0], normed_one),
     ]
+    both_slabs = [owners.over_cores(w) for w in own_slab]
     query_key = jnp.concatenate([w_query, w_key], axis=1)
-    wave = [
-        *[seq_swap(query_key, s) for s in seq_shifts],
-        *[owners.along(w, s) for w in (w_value, w_out) for s in chip_shifts],
-    ]
     gathered, found = [], {}
+    wave = [seq_swap(query_key, s) for s in seq_shifts]
 
     def between(k, pair):
         nonlocal wave
         if k == 1:
             pair, moved, copies[:] = after((pair, wave, copies))
-            moved, others = moved[seq_count - 1 :], moved[: seq_count - 1]
-            heads = [query_key, *others]
+            heads = [query_key, *moved]
             found["pair"] = jnp.concatenate(
                 [h[:, :block_width] for h in heads] + [h[:, block_width:] for h in heads], axis=1
             )
-            count = owners.chips - 1
-            found["value"] = jnp.concatenate([w_value, *moved[:count]], axis=0)
-            found["out"] = jnp.concatenate([w_out, *moved[count:]], axis=1)
             wave = [
                 *[owners.along(found["pair"], s) for s in chip_shifts],
-                *[seq_swap(found["value"], s) for s in seq_shifts],
+                *[seq_swap(w, s) for s in seq_shifts for w in copies[3:]],
             ]
         elif k == part_count // 2:
             pair, moved = after((pair, wave))
             count = owners.chips - 1
             found["pair"] = jnp.concatenate([found["pair"], *moved[:count]], axis=0)
-            found["value"] = jnp.concatenate([found["value"], *moved[count:]], axis=1)
-            wave = moved[:1]
+            found["value"] = jnp.concatenate([w_value, *moved[count::2]], axis=1)
+            found["out"] = jnp.concatenate([w_out, *moved[count + 1 :: 2]], axis=0)
+            wave = [owners.along(found[w], s) for w in ("value", "out") for s in chip_shifts]
+            found["token"] = moved
         return pair
 
     seq_ring.gather(normed_one, lambda k, blocks: gathered.extend(blocks), between)
     normed_all = jnp.concatenate(gathered)
-    pair_rest, value_rest = owners.cross(found["pair"]), owners.cross(found["value"])
-    full_mats = [
+    own_cot, own_both, own_down = copies[:3]
+    pair_rest = owners.cross(found["pair"])
+    cot_steps = Spread(whole_ring, after(own_cot, pair_rest))
+    cot_steps.hop()
+    pair_mats = [
         (found["pair"][:, :local_width], pair_rest[:, :local_width]),
         (found["pair"][:, local_width:], pair_rest[:, local_width:]),
-        (found["value"], value_rest),
     ]
-    own_cot, own_gate, own_up, *own_down = copies
-    cot_steps = Spread(whole_ring, after(own_cot, wave))
-    cot_steps.hop()
-    far_gate = [owners.along(after(own_gate, wave), s) for s in chip_shifts]
-    far_up = [owners.along(after(own_up, far_gate), s) for s in chip_shifts]
 
     whole_members = whole_ring.members(tensor_at)
     seq_members = seq_ring.members(part_at)
     numbers = jnp.stack(
         [at * tok_rows for at in whole_members]
         + [(at * tensor_count + tensor_at) // 2 for at in owners.listed()]
+        + [(owners.here + 1) % 2]
     )
     ids_from = tensor_count
 
@@ -910,24 +1061,31 @@
     places = (marks[:, :1], marks[:, :1].T, marks[:, 1:], marks[:, 1:].T)
     gains = jnp.stack([query_gain, key_gain])
 
-    query_proj, query_low, key_proj, key_low, value_low = project_call(
-        normed_all, full_mats, gains, tables
-    )
+    query_proj, query_low, key_proj, key_low = project_call(
+        normed_all, pair_mats, gains, tables, []
+    )
+    wave = after(wave, query_low)
+    count = owners.chips - 1
+    found["value"] = jnp.concatenate([found["value"], *wave[:count]], axis=0)
+    found["out"] = jnp.concatenate([found["out"], *wave[count:]], axis=1)
+    value_rest, out_rest = owners.cross((found["value"], found["out"]))
+    full_mats = [*pair_mats, (found["value"], value_rest)]
+    cot_steps.hop(query_low)
+    value_low = value_call(normed_all, found["value"], value_rest, cot_steps.blocks[1:])
+    out_full = jnp.concatenate([found["out"], out_rest], axis=1)
+    far_down = [owners.along(after(own_down, wave), s) for s in chip_shifts]
 
     def place_of(ring, k):
         return {0: [0], ring.count // 2: [ring.count - 1]}.get(k, [2 * k - 1, 2 * k])
 
-    cot_steps.hop(query_low)
-    out_chips = after(found["out"], pair_rest)
-    out_heads = jnp.concatenate(
-        [out_chips, *after([seq_swap(out_chips, s) for s in seq_shifts], query_low)], axis=0
-    )
-    out_full = jnp.concatenate([out_heads, owners.cross(out_heads)], axis=1)
+    far_both = []
     attended = [None] * part_count
 
     def branch_parts(k, tokens):
-        parts = []
-        tokens = list(tokens) + (far_gate if k == 0 else [])
+        parts, tokens = [], list(tokens)
+        if k == 0:
+            tokens += far_down
+            far_both.extend(owners.along(after(own_both, *far_down), s) for s in chip_shifts)
         for b in place_of(seq_ring, k):
             attended[b] = attend_call(
                 query_low,
@@ -940,14 +1098,15 @@
                 tokens,
             )
             parts.append(plain_dot(attended[b], out_full).astype(LOW))
+        if k == 1:
+            cot_steps.settle(parts)
+            parts = after(parts, cot_steps.pair)
         return parts
 
-    def branch_done(pair):
-        cot_steps.hop(pair)
-        return pair
-
-    residual = inputs + owners.unlist_columns(seq_ring.scatter(branch_parts, branch_done))
-    attn_rows = jnp.concatenate(attended)
+    branch = seq_ring.scatter(branch_parts)
+    cot_steps.pair = after(cot_steps.pair, branch)
+    cot_steps.hop()
+    residual = inputs + owners.unlist_columns(branch)
     inv_two = lax.rsqrt(jnp.mean(residual * residual, axis=-1, keepdims=True) + EPSILON)
     unit_two = residual * inv_two
     normed_two = (unit_two * mix_gain).astype(jnp.bfloat16)
@@ -960,8 +1119,7 @@
     gate_table = raised / jnp.sum(raised, axis=-1, keepdims=True)
 
     grad_out = cotangent.astype(jnp.float32)
-    far_down = []
-    slab_mats = {0: [[[w] for w in own_slab], [[w] for w in owners.cross(own_slab)]]}
+    slab_mats = {0: [own_slab, both_slabs]}
     row_blocks, sums, mixed = ([None] * tensor_count for _ in range(3))
     shared_all = []
 
@@ -973,6 +1131,7 @@
             expert_count,
             numbers,
             [ids_from + shift, ids_from + owners.chips + shift],
+            [None, None if shift else ids_from + owners.count],
             at,
             [row_blocks[b] for b in at],
             [cot_steps.blocks[b] for b in at],
@@ -994,18 +1153,18 @@
     def next_hop(k, pair):
         done = [sums[b] for b in place_of(whole_ring, k - 1)]
         if k == 1:
+            pair, cot_steps.pair = after((pair, cot_steps.pair), *done)
             while cot_steps.hops < tensor_count // 2:
-                cot_steps.hop(pair)
-            pair, far_up[:] = after((pair, far_up), *done)
-        elif k <= 3:
-            pair, far_down[-1] = after((pair, far_down[-1]), *done)
-            if k == 2:
-                cot_steps.settle(pair)
+                cot_steps.hop()
+        elif k == 2:
+            pair, cot_steps.pair = after((pair, cot_steps.pair), *done)
+            cot_steps.settle()
+            far_down[:] = after(far_down, pair)
+            found["down"] = owners.cross(far_down)
+        elif k == tensor_count // 2 - 1:
+            pair, far_both[:], found["down"] = after((pair, far_both, found["down"]), *done)
         elif k < tensor_count // 2:
             pair = after(pair, *done)
-        if k <= 2:
-            piece = after(own_down[k - 1], pair[0])
-            far_down.append([owners.along(piece, s) for s in chip_shifts])
         return pair
 
     high = lax.reduce_precision(gate_table, 8, 7)
@@ -1020,9 +1179,12 @@
         axis=1,
     )
     whole_ring.gather(payload, first_pair, next_hop)
-    for shift in chip_shifts:
-        mine = [[far_gate[shift - 1]], [far_up[shift - 1]], [piece[shift - 1] for piece in far_down]]
-        slab_mats[shift] = [mine, owners.cross(mine)]
+    far_other = owners.cross(far_both)
+    for i, shift in enumerate(chip_shifts):
+        slab_mats[shift] = [
+            (far_both[i], far_both[i], far_down[i]),
+            (far_other[i], far_other[i], found["down"][i]),
+        ]
     for shift in range(1, owners.chips - 1):
         for k in range(tensor_count // 2 + 1):
             run_experts(shift, k, [])
@@ -1032,28 +1194,21 @@
 
     def down_grads(shift, other, terms, tokens):
         kept, all_cot = shared_all[shift][0], shared_all[0][3]
-        return slab_grads_call(
-            all_cot, kept, other * hidden, hidden, 1, False, [[t] for t in terms], tokens
-        )[0]
+        return slab_grads_call(all_cot, kept, other * hidden, hidden, False, terms, tokens)[0]
 
     def pre_grads(shift, other, terms, tokens):
         kept, rows = shared_all[shift][1], shared_all[0][2]
-        return slab_grads_call(
-            rows, kept, 2 * other * hidden, hidden, 2, True, terms, tokens
-        )
-
-    def far_down_grads(tokens):
-        others = [owners.cross(down_grads(s, 1, [], tokens)) for s in chip_shifts]
-        return [down_grads(s, 0, [other], tokens) for s, other in zip(chip_shifts, others)]
+        return slab_grads_call(rows, kept, 2 * other * hidden, hidden, True, terms, tokens)[0]
 
     def finish(pair):
-        pair, found["down"] = after((pair, far_down_grads([sums[0]])))
+        others = [down_grads(s, 1, [], [sums[0]]) for s in chip_shifts]
+        pair, others = after((pair, others))
+        found["down"] = owners.cross(others)
         return pair
 
     summed_rows = whole_ring.scatter(last_pair, finish)
     grad_rows_sum = summed_rows[:, :model_width]
     grad_gates = summed_rows[:, model_width : model_width + expert_count]
-    sent_down = [owners.along(part, -s) for s, part in zip(chip_shifts, found["down"])]
 
     grad_logits = gate_table * (
         grad_gates - jnp.sum(gate_table * grad_gates, axis=-1, keepdims=True)
@@ -1066,44 +1221,97 @@
         grad_unit_two - unit_two * jnp.mean(grad_unit_two * unit_two, axis=-1, keepdims=True)
     )
     grad_branch = owners.list_columns(grad_residual.astype(jnp.bfloat16))
-    gathered_back = []
+    gathered_back, sent_down = [], []
+    mixture_steps = Reduction(whole_ring)
 
     def back_hop(k, pair):
         if k == 1:
-            others = [owners.cross(pre_grads(s, 1, [], [grad_branch])) for s in chip_shifts]
-            pair = after(pair)
+            down = [
+                down_grads(s, 0, [other], [grad_branch])
+                for s, other in zip(chip_shifts, found["down"])
+            ]
+            sent_down.extend(owners.along(part, -s) for s, part in zip(chip_shifts, down))
+            others = [pre_grads(s, 1, [], down) for s in chip_shifts]
+            pair, others = after((pair, others))
+            mixture_steps.hop(mixed[-1:], pair[0])
+            others = [owners.cross(other) for other in others]
+            found["attn"] = None
+            for b, block in enumerate([*gathered_back, *pair]):
+                found["attn"] = attended_back_call(
+                    [block], out_full, found["attn"], b * tok_rows, length
+                )
             found["pre"] = [
-                pre_grads(s, 0, [other], [pair[0]]) for s, other in zip(chip_shifts, others)
+                pre_grads(s, 0, [other], [found["attn"]]) for s, other in zip(chip_shifts, others)
             ]
         elif k == part_count // 2:
-            pair, sent_down[:] = after((pair, sent_down), found["pre"])
+            pair, mixture_steps.pair = after((pair, mixture_steps.pair), found["pre"])
         return pair
 
     seq_ring.gather(grad_branch, lambda k, blocks: gathered_back.extend(blocks), back_hop)
-    sent_gate = [owners.along(part[0], -s) for s, part in zip(chip_shifts, found["pre"])]
-    mixture_steps = Reduction(whole_ring)
-    mixture_steps.hop(mixed[-1:], gathered_back[-1])
-    grad_attn = jnp.concatenate(
-        [outer_rows(block, out_full).astype(jnp.bfloat16) for block in gathered_back]
-    )
-    *head_grads, grad_gains = attend_back_call(
-        query_low, key_low, value_low, grad_attn, query_proj, key_proj, gains, tables, places
-    )
+    grad_attn = found["attn"]
+    for b in range(3, part_count):
+        grad_attn = attended_back_call(
+            [gathered_back[b]], out_full, grad_attn, b * tok_rows, length
+        )
 
     def mixture_hop(k, *tokens):
         mixture_steps.hop([mixed[b] for b in place_of(whole_ring, k)], *tokens)
 
-    mixture_hop(tensor_count // 2 - 1, head_grads[0])
-    grad_branch_all = jnp.concatenate(gathered_back)
+    mixture_steps.pair, sent_down[:] = after((mixture_steps.pair, sent_down), grad_attn)
+    mixture_hop(tensor_count // 2 - 1)
+    sent_pre = [
+        owners.along(after(part, sent_down), -s) for s, part in zip(chip_shifts, found["pre"])
+    ]
+    *head_grads, grad_gains = attend_back_call(
+        query_low,
+        key_low,
+        value_low,
+        grad_attn,
+        query_proj,
+        key_proj,
+        gains,
+        tables,
+        places,
+        list(mixture_steps.sent),
+    )
+
     own_other_half = weight_back_call(
-        normed_all, grad_branch_all, head_grads, attn_rows, 1, []
+        normed_all,
+        gathered_back,
+        head_grads,
+        attended,
+        1,
+        list(mixture_steps.pair),
     )
     other_half = owners.cross(own_other_half)
     mine_half = weight_back_call(
-        normed_all, grad_branch_all, head_grads, attn_rows, 0, [own_other_half]
-    )
-    normed_parts = rows_back_call(head_grads, full_mats, tok_rows, [mine_half, *sent_gate])
-    own_other_down = owners.cross(down_grads(0, 1, [], [normed_parts[0]]))
+        normed_all, gathered_back, head_grads, attended, 0, [own_other_half]
+    )
+    mixture_steps.pair = after(mixture_steps.pair, own_other_half)
+    mixture_hop(max(tensor_count // 2 - 2, 1))
+    normed_parts = rows_back_call(
+        head_grads, full_mats, tok_rows, [mine_half, *mixture_steps.sent]
+    )
+    listed_norm = gain_call(
+        own_other_half,
+        mine_half,
+        [m for pair in full_mats for m in pair],
+        local_width,
+        [normed_parts[-1], *mixture_steps.pair, *sent_pre],
+    )
+    grad_norm_gain = owners.unlist_columns(listed_norm.T) / norm_gain
+    room = model_width - grad_gains.size
+    small_steps = Everywhere(
+        jnp.concatenate(
+            [
+                grad_router,
+                grad_mix_gain[None],
+                grad_norm_gain,
+                jnp.pad(grad_gains.reshape(1, -1), ((0, 0), (0, room))),
+            ]
+        )
+    )
+    small_steps.hop()
     chip_rows = model_width // owners.count
     piece_rows = chip_rows // 2
     pieces = [slice(p * piece_rows, (p + 1) * piece_rows) for p in range(2)]
@@ -1118,30 +1326,58 @@
     def give_parts(k, tokens):
         parts = [normed_parts[b] for b in place_of(seq_ring, k)]
         if k == 1:
-            parts, sent_parts[:] = after((parts, sent_parts))
+            parts, sent_parts[:], small_steps.value = after(
+                (parts, sent_parts, small_steps.value)
+            )
+            small_steps.hop()
         if k == 0:
             sent = after(sent_parts[0], tokens)
             come.append([owners.along(part, -s) for s, part in zip(chip_shifts, sent)])
-            found["own_other"] = pre_grads(0, 1, [], tokens)
+            found["own_other_down"] = down_grads(0, 1, [], tokens)
+            found["own_other"] = pre_grads(0, 1, [], [found["own_other_down"]])
         return parts
 
     def normed_done(pair):
-        pair, come[0] = after((pair, come[0]), found["own_other"])
+        pair, come[0], small_steps.value = after(
+            (pair, come[0], small_steps.value), found["own_other"]
+        )
+        small_steps.hop()
         return pair
 
-    back_steps = seq_ring.scatter(give_parts, normed_done)
-    grad_normed_one = owners.unlist_columns(back_steps)
-    done = come[0][0]
-    mixture_hop(max(tensor_count // 2 - 2, 1), done)
+    grad_normed_one = seq_ring.scatter(give_parts, normed_done)
+    done = grad_normed_one
+    grad_normed_one = owners.unlist_columns(grad_normed_one)
     sent = after(sent_parts[1], done)
     come.append([owners.along(part, -s) for s, part in zip(chip_shifts, sent)])
-    own_other = owners.cross(found["own_other"])
-    own_down_grad = down_grads(0, 0, [own_other_down], [done])
-    own_pre_grads = pre_grads(0, 0, [own_other], [done])
+    mixture_steps.pair = after(mixture_steps.pair, done)
     for k in range(tensor_count // 2 - 3, 0, -1):
-        mixture_hop(k, own_pre_grads)
-    layer_out = (residual + mixture_steps.total(mixed[0])).astype(jnp.bfloat16)
-
+        mixture_hop(k)
+    own_other_down, own_other = owners.cross(
+        after((found["own_other_down"], found["own_other"]), done)
+    )
+    (grad_down,) = slab_grads_call(
+        shared_all[0][3],
+        shared_all[0][0],
+        0,
+        hidden,
+        False,
+        [own_other_down, *sent_down],
+        [done],
+        kind=FULL,
+    )
+    come[1], small_steps.value = after((come[1], small_steps.value), grad_down)
+    small_steps.hop()
+    grad_gate, grad_up = slab_grads_call(
+        shared_all[0][2],
+        shared_all[0][1],
+        0,
+        hidden,
+        True,
+        [own_other, *sent_pre],
+        come[1],
+        parts=2,
+        kind=FULL,
+    )
     def columns_of(place, seq):
         first = (place * seq_count + seq) * block_width
         return slice(first, first + block_width)
@@ -1151,9 +1387,8 @@
             part[:, columns].astype(FULL) for part in come[p]
         )
 
-    owned = [[] for _ in range(4)]
-    for p in range(2):
-        swapped = [
+    swapped_pieces = [
+        [
             seq_swap(
                 jnp.concatenate(
                     [summed_piece(p, columns_of(place, s)).astype(LOW) for place in range(4)],
@@ -1163,6 +1398,20 @@
             )
             for s in seq_shifts
         ]
+        for p in range(2)
+    ]
+    mixture_steps.pair, small_steps.value = after(
+        (mixture_steps.pair, small_steps.value), grad_gate
+    )
+    layer_out = (residual + mixture_steps.total(mixed[0])).astype(jnp.bfloat16)
+    grad_unit_one = grad_normed_one * norm_gain
+    grad_tokens = grad_residual + inv_one * (
+        grad_unit_one - unit_one * jnp.mean(grad_unit_one * unit_one, axis=-1, keepdims=True)
+    )
+    grad_tokens = grad_tokens.astype(jnp.bfloat16)
+    swapped_pieces = after(swapped_pieces, layer_out, grad_tokens)
+    owned = [[] for _ in range(4)]
+    for p, swapped in enumerate(swapped_pieces):
         for place in range(4):
             columns = slice(place * block_width, (place + 1) * block_width)
             owned[place].append(
@@ -1171,52 +1420,22 @@
             )
     owned_query, owned_key, owned_value, owned_out = map(jnp.concatenate, owned)
     owned_out = owned_out.T
-    sent_up = [
-        owners.along(after(part[1], come[1]), -s) for s, part in zip(chip_shifts, found["pre"])
-    ]
-
-    def together(own, *parts):
-        return own.astype(FULL) + sum(part.astype(FULL) for part in parts)
-
-    grad_gate = together(own_pre_grads[0], *sent_gate)
-    grad_up = together(own_pre_grads[1], *sent_up)
-    grad_down = together(own_down_grad, *sent_down)
-    def gain_part(grad, place):
-        return sum(
-            jnp.sum(
-                grad[:, m * local_width : (m + 1) * local_width].astype(FULL)
-                * mat[place].astype(FULL),
-                axis=1,
-            )
-            for m, mat in enumerate(full_mats)
-        )
-
-    listed_norm = jnp.concatenate([gain_part(mine_half, 0), gain_part(own_other_half, 1)])
-    grad_norm_gain = owners.unlist_columns(listed_norm[None])[0] / norm_gain
-
-    grad_unit_one = grad_normed_one * norm_gain
-    grad_tokens = grad_residual + inv_one * (
-        grad_unit_one - unit_one * jnp.mean(grad_unit_one * unit_one, axis=-1, keepdims=True)
-    )
-    early = lax.psum(
-        jnp.concatenate([grad_router, grad_mix_gain[None]]), ("expert", "tensor")
-    )
-    early = after(early, done)
-    late = everywhere(
-        after(jnp.concatenate([grad_norm_gain.reshape(-1, head_size), grad_gains]), done)
-    )
+    while small_steps.value is not None:
+        small_steps.hop()
+    small = small_steps.own
+    small_gains = small[-1, : grad_gains.size].reshape(grad_gains.shape)
     return (
         layer_out,
-        grad_tokens.astype(jnp.bfloat16),
-        late[:-2].reshape(-1),
+        grad_tokens,
+        small[-2],
         owned_query,
         owned_key,
         owned_value,
-        late[-2],
-        late[-1],
+        small_gains[0],
+        small_gains[1],
         owned_out,
-        early[-1],
-        early[:-1].T,
+        small[-3],
+        small[:-3].T,
         grad_gate[None],
         grad_up[None],
         grad_down[None],

time: 928 us -> 822 us (0.89)
  waiting for transfers between devices: 247 us -> 142 us
  other arithmetic: 96.5 us -> 67.1 us
  Pallas kernels: 380 us -> 401 us
  local copies, waits for them, and re-layouts: 68.3 us -> 84.4 us
    ppermute x24, waiting for transfers between devices: 53.5 us -> 19.2 us  [left(): lax.ppermute(v, self.axis, self.leftward)]
    ppermute x12 -> x9, waiting for transfers between devices: 54.3 us -> 28 us  [along(): return jax.tree.map(lambda v: lax.ppermute(v, 'expert', pairs), value)]
    pallas_call x21 -> x28, Pallas kernels: 323 us -> 349 us  [the longest x10 172 us: experts_call(): pl.pallas_call(functools.partial(experts_body, blocks, experts, slabs, in...]
    ppermute x24, waiting for transfers between devices: 61.5 us -> 37.9 us  [right(): lax.ppermute(v, self.axis, self.rightward)]
    unnamed x296 -> x281, local copies, waits for them, and re-layouts: 32.6 us -> 52.6 us
    ppermute x24, starting transfers between devices: 14.8 us -> 28.7 us  [left(): lax.ppermute(v, self.axis, self.leftward)]
    ppermute x5, waiting for transfers between devices: 18.1 us -> 4.25 us  [hop(): self.value = lax.ppermute(self.own, *self.hops.pop(0))]
    broadcast_in_dim x3 -> x0, other arithmetic: 13.7 us -> none  [the longest x1 5.14 us: per_device(): grad_down[None]]
  transfers between devices with their start and end apart: 88 -> 80, of which waited for: 33 -> 26; matrix products, arithmetic and copies ran while one was open for 15% -> 14% of each run, Pallas kernels for 34% -> 48%
where the time goes in v3:
time: 822 us; the launch traced here: 811 us
  Pallas kernels  401 us (49%)
  waiting for transfers between devices  142 us (17%)
  starting transfers between devices  85.9 us (10%)
  local copies, waits for them, and re-layouts  84.4 us (10%)
  other arithmetic  67.1 us (8%)
  between operations  16.1 us (2%)
  matrix products  15.4 us (2%)
    pallas_call x10, Pallas kernels, experts_call(): pl.pallas_call(functools.partial(experts_body, blocks, experts, slabs, in...  172 us
    pallas_call x8, Pallas kernels, slab_grads_call(): pl.pallas_call(functools.partial(slab_grads_body, swapped, parts, joined)...  101 us
    unnamed x281, local copies, waits for them, and re-layouts  52.6 us
    ppermute x5, waiting for transfers between devices, seq_swap(): return lax.ppermute(value, 'tensor', pairs)  51.5 us
    ppermute x24, waiting for transfers between devices, right(): lax.ppermute(v, self.axis, self.rightward)  37.9 us
    ppermute x24, starting transfers between devices, left(): lax.ppermute(v, self.axis, self.leftward)  28.7 us
    ppermute x9, waiting for transfers between devices, along(): return jax.tree.map(lambda v: lax.ppermute(v, 'expert', pairs), value)  28 us
    pallas_call x1, Pallas kernels, attend_back_call(): pl.pallas_call(lambda *refs: attend_back_body(step, *refs[:6 + len(fixed)...  26.9 us
  transfers between devices with their start and end apart: 80, of which 26 were waited for; matrix products, arithmetic and copies ran while one was open for 14% of the time, Pallas kernels for 48%

profile of v3, /device:TPU:0, one launch (start us, length us, event | category | flops | bytes accessed | tf_op | source)
XLA Modules:
  0.0 811.4 jit_solution(1483677685922936545)
XLA Ops:
  29.3 18.0 %collective-permute-done.2.refs_2_ = bf16[512,512]{1,0:T(8,128)(2,1)S(1)} collective-permute-done((bf16[512,512]{1,0:T(8,128)(2,1)S(1)}, bf16[512,512]{1,0:T(8,128)(2,1)S(1)}, u32[]{:S(2)}, u32[]{:S(2)}) %collective-permute-start.2) | collective-permute-done | bytes 524320 | tf_op jit(solution)/shard_map/ppermute | solution.py:986
  62.8 14.4 %collective-permute-done.6.refs_3_ = bf16[512,256]{1,0:T(8,128)(2,1)S(1)} collective-permute-done((bf16[512,256]{1,0:T(8,128)(2,1)}, bf16[512,256]{1,0:T(8,128)(2,1)S(1)}, u32[]{:S(2)}, u32[]{:S(2)}) %collective-permute-start.6) | collective-permute-done | bytes 262176 | tf_op jit(solution)/shard_map/ppermute | solution.py:986
  182.4 10.4 %collective-permute-done.21 = bf16[256,2048]{1,0:T(8,128)(2,1)} collective-permute-done((bf16[256,2048]{1,0:T(8,128)(2,1)S(1)}, bf16[256,2048]{1,0:T(8,128)(2,1)}, u32[]{:S(2)}, u32[]{:S(2)}) %collective-permute-start.21) | collective-permute-done | bytes 1048608 | tf_op jit(solution)/shard_map/ppermute | solution.py:773
  213.1 12.1 %experts.10 = (bf16[256,2176]{1,0:T(8,128)(2,1)}, bf16[256,2048]{1,0:T(8,128)(2,1)}, bf16[2048,1024]{1,0:T(8,128)(2,1)}, bf16[2048,2048]{1,0:T(8,128)(2,1)}, bf1...) custom-call(s32[13]{0:T(128)} %stack.77.numbers, bf16[256,2176]{1,0:T(8,128)(2,1)} %concatenate.130.refs_0_, ...), custom_call_target="tpu_custom_call" | custom-call | flops 2386093056 | tf_op jit(solution)/shard_map/experts/pallas_call | solution.py:294
  225.2 24.4 %collective-permute-done.24.refs_2_ = bf16[256,2048]{1,0:T(8,128)(2,1)S(1)} collective-permute-done((bf16[256,2048]{1,0:T(8,128)(2,1)}, bf16[256,2048]{1,0:T(8,128)(2,1)S(1)}, u32[]{:S(2)}, u32[]{:S(2)}) %collective-permute-start.24) | collective-permute-done | bytes 1048608 | tf_op jit(solution)/shard_map/ppermute | solution.py:770
  258.9 19.8 %experts.11 = (bf16[256,2176]{1,0:T(8,128)(2,1)}, bf16[256,2176]{1,0:T(8,128)(2,1)}, bf16[256,2048]{1,0:T(8,128)(2,1)}, bf16[256,2048]{1,0:T(8,128)(2,1)}, bf16[...) custom-call(s32[13]{0:T(128)} %stack.77.numbers, ...), custom_call_target="tpu_custom_call", output_to_operand_aliasing={{4}: (11, {}), {5}: (12, {}), {6}: (13, {}), {7}: (14, {})} | custom-call | flops 4772186112 | tf_op jit(solution)/shard_map/experts/pallas_call | solution.py:294
  292.1 19.7 %experts.12 = (bf16[256,2176]{1,0:T(8,128)(2,1)}, bf16[256,2176]{1,0:T(8,128)(2,1)}, bf16[256,2048]{1,0:T(8,128)(2,1)}, bf16[256,2048]{1,0:T(8,128)(2,1)}, bf16[...) custom-call(s32[13]{0:T(128)} %stack.77.numbers, ...), custom_call_target="tpu_custom_call", output_to_operand_aliasing={{4}: (11, {}), {5}: (12, {}), {6}: (13, {}), {7}: (14, {})} | custom-call | flops 4772186112 | tf_op jit(solution)/shard_map/experts/pallas_call | solution.py:294
  322.0 19.7 %experts.13 = (bf16[256,2176]{1,0:T(8,128)(2,1)}, bf16[256,2176]{1,0:T(8,128)(2,1)}, bf16[256,2048]{1,0:T(8,128)(2,1)}, bf16[256,2048]{1,0:T(8,128)(2,1)}, bf16[...) custom-call(s32[13]{0:T(128)} %stack.77.numbers, ...), custom_call_target="tpu_custom_call", output_to_operand_aliasing={{4}: (11, {}), {5}: (12, {}), {6}: (13, {}), {7}: (14, {})} | custom-call | flops 4772186112 | tf_op jit(solution)/shard_map/experts/pallas_call | solution.py:294
  342.9 12.6 %experts.14 = (bf16[256,2176]{1,0:T(8,128)(2,1)}, bf16[256,2048]{1,0:T(8,128)(2,1)}, bf16[2048,1024]{1,0:T(8,128)(2,1)}, bf16[2048,2048]{1,0:T(8,128)(2,1)}, bf1...) custom-call(s32[13]{0:T(128)} %stack.77.numbers, ...), custom_call_target="tpu_custom_call", output_to_operand_aliasing={{2}: (9, {}), {3}: (10, {}), {4}: (11, {}), {5}: (12, {})} | custom-call | flops 2386093056 | tf_op jit(solution)/shard_map/experts/pallas_call | solution.py:294
  355.5 12.9 %experts.15 = (bf16[256,2176]{1,0:T(8,128)(2,1)}, bf16[256,2048]{1,0:T(8,128)(2,1)}, bf16[2048,1024]{1,0:T(8,128)(2,1)}, bf16[2048,2048]{1,0:T(8,128)(2,1)}) custom-call(s32[13]{0:T(128)} %stack.77.numbers, bf16[256,2176]{1,0:T(8,128)(2,1)} %copy-done.46, bf16[256,2048]{1,0:T(8,128)(2,1)} %copy-done.47, ...), custom_call_target="tpu_custom_call" | custom-call | flops 2386093056 | tf_op jit(solution)/shard_map/experts/pallas_call | solution.py:294
  371.8 20.8 %experts.16 = (bf16[256,2176]{1,0:T(8,128)(2,1)}, bf16[256,2176]{1,0:T(8,128)(2,1)}, bf16[256,2048]{1,0:T(8,128)(2,1)}, bf16[256,2048]{1,0:T(8,128)(2,1)}, bf16[...) custom-call(s32[13]{0:T(128)} %stack.77.numbers, ...), custom_call_target="tpu_custom_call", output_to_operand_aliasing={{4}: (15, {}), {5}: (16, {})} | custom-call | flops 4772186112 | tf_op jit(solution)/shard_map/experts/pallas_call | solution.py:294
  397.3 20.7 %experts.17 = (bf16[256,2176]{1,0:T(8,128)(2,1)}, bf16[256,2176]{1,0:T(8,128)(2,1)}, bf16[256,2048]{1,0:T(8,128)(2,1)}, bf16[256,2048]{1,0:T(8,128)(2,1)}, bf16[...) custom-call(s32[13]{0:T(128)} %stack.77.numbers, ...), custom_call_target="tpu_custom_call", output_to_operand_aliasing={{4}: (15, {}), {5}: (16, {})} | custom-call | flops 4772186112 | tf_op jit(solution)/shard_map/experts/pallas_call | solution.py:294
  424.6 20.7 %experts.18 = (bf16[256,2176]{1,0:T(8,128)(2,1)}, bf16[256,2176]{1,0:T(8,128)(2,1)}, bf16[256,2048]{1,0:T(8,128)(2,1)}, bf16[256,2048]{1,0:T(8,128)(2,1)}, bf16[...) custom-call(s32[13]{0:T(128)} %stack.77.numbers, ...), custom_call_target="tpu_custom_call", output_to_operand_aliasing={{4}: (15, {}), {5}: (16, {})} | custom-call | flops 4772186112 | tf_op jit(solution)/shard_map/experts/pallas_call | solution.py:294
  450.9 12.7 %experts.19 = (bf16[256,2176]{1,0:T(8,128)(2,1)}, bf16[256,2048]{1,0:T(8,128)(2,1)}, bf16[2048,1024]{1,0:T(8,128)(2,1)}, bf16[2048,2048]{1,0:T(8,128)(2,1)}) custom-call(s32[13]{0:T(128)} %stack.77.numbers, bf16[256,2176]{1,0:T(8,128)(2,1)} %concatenate.130.refs_0_, ...), custom_call_target="tpu_custom_call", output_to_operand_aliasing={{2}: (11, {}), {3}: (12, {})} | custom-call | flops 2386093056 | tf_op jit(solution)/shard_map/experts/pallas_call | solution.py:294
  485.2 10.1 %slab_grads.9.refs_0_ = bf16[512,2048]{1,0:T(8,128)(2,1)} custom-call(bf16[2048,2048]{1,0:T(8,128)(2,1)} %get-tuple-element.257.rows, bf16[2048,1024]{1,0:T(8,128)(2,1)} %get-tuple-element.258.kept, bf16[512,2048]{1,0:T(8,128)(2,1)} %copy-done.88, bf16[256,2048]{1,0:T(8,128)(2,1)} %copy-done.10), custom_call_target="tpu_custom_call" | custom-call | flops 1431655808 | tf_op jit(solution)/shard_map/slab_grads/pallas_call | solution.py:381
  495.4 14.5 %slab_grads.10.refs_2_ = bf16[4096,512]{1,0:T(8,128)(2,1)} custom-call(bf16[2048,2048]{1,0:T(8,128)(2,1)} %get-tuple-element.261.rows, bf16[2048,2048]{1,0:T(8,128)(2,1)} %get-tuple-element.262.kept, bf16[512,2048]{1,0:T(8,128)(2,1)} %slab_grads.9.refs_0_), custom_call_target="tpu_custom_call" | custom-call | flops 2863311616 | tf_op jit(solution)/shard_map/slab_grads/pallas_call | solution.py:381
  534.4 15.0 %slab_grads.11.refs_4_.refs_0_ = bf16[4096,512]{1,0:T(8,128)(2,1)} custom-call(bf16[2048,2048]{1,0:T(8,128)(2,1)} %get-tuple-element.261.rows, bf16[2048,2048]{1,0:T(8,128)(2,1)} %get-tuple-element.262.kept, bf16[4096,512]{1,0:T(8,128)(2,1)} %collective-permute-done.52.refs_0_, bf16[1024,512]{1,0:T(8,128)(2,1)} %attended_back.6.refs_1_), custom_call_target="tpu_custom_call" | custom-call | flops 2863311616 | tf_op jit(solution)/shard_map/slab_grads/pallas_call | solution.py:381
  570.4 26.9 %attend_back.1 = (bf16[1024,512]{1,0:T(8,128)(2,1)}, bf16[1024,512]{1,0:T(8,128)(2,1)}, bf16[1024,512]{1,0:T(8,128)(2,1)}, f32[2,128]{1,0:T(2,128)}) custom-call(bf16[1024,512]{1,0:T(8,128)(2,1)} %get-tuple-element.172.refs_2_.query.refs_0_, bf16[1024,512]{1,0:T(8,128)(2,1)} %get-tuple-element.173.key.refs_1_, bf16[1024,512]{1,0:T(8,128)(2,1)} %values.1.value.refs_2_, ...), custom_call_target="tpu_custom_call" | custom-call | flops 1073741824 | tf_op jit(solution)/shard_map/attend_back/pallas_call | solution.py:607
  623.9 11.6 %rows_back.1 = (bf16[256,2048]{1,0:T(8,128)(2,1)}, bf16[256,2048]{1,0:T(8,128)(2,1)}, bf16[256,2048]{1,0:T(8,128)(2,1)}, bf16[256,2048]{1,0:T(8,128)(2,1)}) custom-call(bf16[1024,512]{1,0:T(8,128)(2,1)} %get-tuple-element.277.refs_1_.refs_0_, bf16[1024,512]{1,0:T(8,128)(2,1)} %get-tuple-element.278.refs_2_.refs_1_, ...), custom_call_target="tpu_custom_call" | custom-call | flops 2576980480 | tf_op jit(solution)/shard_map/rows_back/pallas_call | solution.py:675
  640.8 19.8 %collective-permute-done.59.refs_9_.refs_1_ = bf16[4096,512]{1,0:T(8,128)(2,1)} collective-permute-done((bf16[4096,512]{1,0:T(8,128)(2,1)}, bf16[4096,512]{1,0:T(8,128)(2,1)}, u32[]{:S(2)}, u32[]{:S(2)}) %collective-permute-start.59) | collective-permute-done | bytes 4194336 | tf_op jit(solution)/shard_map/ppermute | solution.py:877
  694.1 14.6 %slab_grads.13.refs_4_.refs_1_ = bf16[4096,512]{1,0:T(8,128)(2,1)} custom-call(bf16[2048,2048]{1,0:T(8,128)(2,1)} %get-tuple-element.261.rows, bf16[2048,2048]{1,0:T(8,128)(2,1)} %get-tuple-element.293.kept, bf16[512,2048]{1,0:T(8,128)(2,1)} %slab_grads.12.refs_0_), custom_call_target="tpu_custom_call" | custom-call | flops 2863311616 | tf_op jit(solution)/shard_map/slab_grads/pallas_call | solution.py:381
  730.6 10.9 %slab_grads.14.refs_2_ = f32[512,2048]{1,0:T(8,128)} custom-call(bf16[2048,2048]{1,0:T(8,128)(2,1)} %get-tuple-element.257.rows, bf16[2048,1024]{1,0:T(8,128)(2,1)} %get-tuple-element.294.kept, bf16[512,2048]{1,0:T(8,128)(2,1)} %collective-permute-done.71.refs_0_, bf16[512,2048]{1,0:T(8,128)(2,1)} %get-tuple-element.287.refs_1_, ...), custom_call_target="tpu_custom_call" | custom-call | flops 1431655808 | tf_op jit(solution)/shard_map/slab_grads/pallas_call | solution.py:381
  752.1 17.3 %slab_grads.15 = (f32[2048,512]{1,0:T(8,128)}, f32[2048,512]{1,0:T(8,128)}) custom-call(bf16[2048,2048]{1,0:T(8,128)(2,1)} %get-tuple-element.261.rows, bf16[2048,2048]{1,0:T(8,128)(2,1)} %get-tuple-element.293.kept, bf16[4096,512]{1,0:T(8,128)(2,1)} %collective-permute-done.73.refs_0_, bf16[4096,512]{1,0:T(8,128)(2,1)} %collective-permute-done.59.refs_9_.refs_1_, ...), custom_call_target="tpu_custom_call" | custom-call | flops 2863311616 | tf_op jit(solution)/shard_map/slab_grads/pallas_call | solution.py:381
  784.4 10.2 %collective-permute-done.76.refs_1_ = bf16[256,1024]{1,0:T(8,128)(2,1)} collective-permute-done((bf16[256,1024]{1,0:T(8,128)(2,1)}, bf16[256,1024]{1,0:T(8,128)(2,1)}, u32[]{:S(2)}, u32[]{:S(2)}) %collective-permute-start.76) | collective-permute-done | bytes 524320 | tf_op jit(solution)/shard_map/ppermute | solution.py:986
  (605 shorter events, 405.5 us)
Async XLA Ops:
  7.2 205.8 %all-gather.7.cloned.1.call-start = ((), (), s32[]{:S(2)}) async-start(), calls=%async_computation | async-start | bytes 6291456 | tf_op jit(solution)/shard_map/all_gather | solution.py:881
  8.0 205.1 %all-gather.9.cloned.1.call-start = ((), (), s32[]{:S(2)}) async-start(), calls=%async_computation.1 | async-start | bytes 6291456 | tf_op jit(solution)/shard_map/all_gather | solution.py:881
  10.6 36.7 %collective-permute-start = (bf16[256,2048]{1,0:T(8,128)(2,1)S(1)}, bf16[256,2048]{1,0:T(8,128)(2,1)S(1)}, u32[]{:S(2)}, u32[]{:S(2)}) collective-permute-start(bf16[256,2048]{1,0:T(8,128)(2,1)S(1)} %get-tuple-element.444.refs_0_.refs_2_), channel_id=1, source_target_pairs={{0,2},{2,3},{3,1},{1,0},{4,6},{6,7},{7,5},{5,4},{8,10},{10,11},{11... | collective-permute-start | bytes 3145736 | tf_op jit(solution)/shard_map/ppermute | solution.py:770
  13.6 35.9 %collective-permute-start.1 = (bf16[256,2048]{1,0:T(8,128)(2,1)S(1)}, bf16[256,2048]{1,0:T(8,128)(2,1)S(1)}, u32[]{:S(2)}, u32[]{:S(2)}) collective-permute-start(bf16[256,2048]{1,0:T(8,128)(2,1)S(1)} %get-tuple-element.444.refs_0_.refs_2_), channel_id=1, source_target_pairs={{2,0},{3,2},{1,3},{0,1},{6,4},{7,6},{5,7},{4,5},{10,8},{11,10},{9,... | collective-permute-start | bytes 3145736 | tf_op jit(solution)/shard_map/ppermute | solution.py:773
  62.6 150.5 %all-gather.11.cloned.1.call-start = ((), (), s32[]{:S(2)}) async-start(), calls=%async_computation.2 | async-start | bytes 6291456 | tf_op jit(solution)/shard_map/all_gather | solution.py:881
  127.5 47.7 %collective-permute-start.19 = (bf16[512,2048]{1,0:T(8,128)(2,1)}, bf16[512,2048]{1,0:T(8,128)(2,1)S(1)}, u32[]{:S(2)}, u32[]{:S(2)}) collective-permute-start(bf16[512,2048]{1,0:T(8,128)(2,1)} %after.39), channel_id=1, source_target_pairs={{0,16},{8,24},{16,0},{24,8},{1,17},{9,25},{17,1},{25,9},{2,18},{10... | collective-permute-start | bytes 6291464 | tf_op jit(solution)/shard_map/ppermute | solution.py:877
  129.3 36.8 %collective-permute-start.15 = (bf16[256,2048]{1,0:T(8,128)(2,1)}, bf16[256,2048]{1,0:T(8,128)(2,1)S(1)}, u32[]{:S(2)}, u32[]{:S(2)}) collective-permute-start(bf16[256,2048]{1,0:T(8,128)(2,1)} %get-tuple-element.178.refs_0_.refs_2_), channel_id=1, source_target_pairs={{0,2},{2,4},{4,6},{6,7},{7,5},{5,3},{3,1},{1,0},{8,10},{10,12},{12... | collective-permute-start | bytes 3145736 | tf_op jit(solution)/shard_map/ppermute | solution.py:770
  129.5 36.5 %collective-permute-start.16 = (bf16[256,2048]{1,0:T(8,128)(2,1)}, bf16[256,2048]{1,0:T(8,128)(2,1)}, u32[]{:S(2)}, u32[]{:S(2)}) collective-permute-start(bf16[256,2048]{1,0:T(8,128)(2,1)} %get-tuple-element.179.refs_1_.refs_3_), channel_id=1, source_target_pairs={{2,0},{4,2},{6,4},{7,6},{5,7},{3,5},{1,3},{0,1},{10,8},{12,10},{14... | collective-permute-start | bytes 3145736 | tf_op jit(solution)/shard_map/ppermute | solution.py:773
  203.6 47.6 %collective-permute-start.22 = (bf16[256,2176]{1,0:T(8,128)(2,1)}, bf16[256,2176]{1,0:T(8,128)(2,1)}, u32[]{:S(2)}, u32[]{:S(2)}) collective-permute-start(bf16[256,2176]{1,0:T(8,128)(2,1)} %concatenate.130.refs_0_), channel_id=1, source_target_pairs={{0,2},{2,4},{4,6},{6,7},{7,5},{5,3},{3,1},{1,0},{8,10},{10,12},{12... | collective-permute-start | bytes 3342344 | tf_op jit(solution)/shard_map/ppermute | solution.py:770
  205.1 46.1 %collective-permute-start.23 = (bf16[256,2176]{1,0:T(8,128)(2,1)}, bf16[256,2176]{1,0:T(8,128)(2,1)}, u32[]{:S(2)}, u32[]{:S(2)}) collective-permute-start(bf16[256,2176]{1,0:T(8,128)(2,1)} %concatenate.130.refs_0_), channel_id=1, source_target_pairs={{2,0},{4,2},{6,4},{7,6},{5,7},{3,5},{1,3},{0,1},{10,8},{12,10},{14... | collective-permute-start | bytes 3342344 | tf_op jit(solution)/shard_map/ppermute | solution.py:773
  208.9 40.7 %collective-permute-start.24 = (bf16[256,2048]{1,0:T(8,128)(2,1)}, bf16[256,2048]{1,0:T(8,128)(2,1)S(1)}, u32[]{:S(2)}, u32[]{:S(2)}) collective-permute-start(bf16[256,2048]{1,0:T(8,128)(2,1)} %get-tuple-element.186), channel_id=1, source_target_pairs={{0,2},{2,4},{4,6},{6,7},{7,5},{5,3},{3,1},{1,0},{8,10},{10,12},{12... | collective-permute-start | bytes 3145736 | tf_op jit(solution)/shard_map/ppermute | solution.py:770
  210.4 40.7 %collective-permute-start.25 = (bf16[256,2048]{1,0:T(8,128)(2,1)}, bf16[256,2048]{1,0:T(8,128)(2,1)S(1)}, u32[]{:S(2)}, u32[]{:S(2)}) collective-permute-start(bf16[256,2048]{1,0:T(8,128)(2,1)} %get-tuple-element.187), channel_id=1, source_target_pairs={{2,0},{4,2},{6,4},{7,6},{5,7},{3,5},{1,3},{0,1},{10,8},{12,10},{14... | collective-permute-start | bytes 3145736 | tf_op jit(solution)/shard_map/ppermute | solution.py:773
  210.9 100.9 %collective-permute-start.32 = (bf16[4096,512]{1,0:T(8,128)(2,1)}, bf16[4096,512]{1,0:T(8,128)(2,1)}, u32[]{:S(2)}, u32[]{:S(2)}) collective-permute-start(bf16[4096,512]{1,0:T(8,128)(2,1)} %after.44), channel_id=1, source_target_pairs={{0,16},{8,24},{16,0},{24,8},{1,17},{9,25},{17,1},{25,9},{2,18},{10... | collective-permute-start | bytes 12582920 | tf_op jit(solution)/shard_map/ppermute | solution.py:877
  317.9 37.6 %collective-permute-start.34 = (bf16[4096,512]{1,0:T(8,128)(2,1)}, bf16[4096,512]{1,0:T(8,128)(2,1)}, u32[]{:S(2)}, u32[]{:S(2)}) collective-permute-start(bf16[4096,512]{1,0:T(8,128)(2,1)} %get-tuple-element.210.refs_2_.refs_3_.refs_4_.refs_5_), channel_id=1, source_target_pairs={{0,8},{8,0},{16,24},{24,16},{1,9},{9,1},{17,25},{25,17},{2,10},{10... | collective-permute-start | bytes 12582920 | tf_op jit(solution)/shard_map/ppermute | solution.py:873
  511.9 48.4 %collective-permute-start.53 = (bf16[512,2048]{1,0:T(8,128)(2,1)}, bf16[512,2048]{1,0:T(8,128)(2,1)S(1)}, u32[]{:S(2)}, u32[]{:S(2)}) collective-permute-start(bf16[512,2048]{1,0:T(8,128)(2,1)} %slab_grads.9.refs_0_), channel_id=1, source_target_pairs={{0,16},{8,24},{16,0},{24,8},{1,17},{9,25},{17,1},{25,9},{2,18},{10... | collective-permute-start | bytes 6291464 | tf_op jit(solution)/shard_map/ppermute | solution.py:877
  568.6 92.1 %collective-permute-start.59 = (bf16[4096,512]{1,0:T(8,128)(2,1)}, bf16[4096,512]{1,0:T(8,128)(2,1)}, u32[]{:S(2)}, u32[]{:S(2)}) collective-permute-start(bf16[4096,512]{1,0:T(8,128)(2,1)} %after.54), channel_id=1, source_target_pairs={{0,16},{8,24},{16,0},{24,8},{1,17},{9,25},{17,1},{25,9},{2,18},{10... | collective-permute-start | bytes 12582920 | tf_op jit(solution)/shard_map/ppermute | solution.py:877
  607.7 62.7 %collective-permute-start.58 = (bf16[1024,2048]{1,0:T(8,128)(2,1)}, bf16[1024,2048]{1,0:T(8,128)(2,1)}, u32[]{:S(2)}, u32[]{:S(2)}) collective-permute-start(bf16[1024,2048]{1,0:T(8,128)(2,1)} %weight_back.2.refs_2_.refs_12_.others), channel_id=1, source_target_pairs={{0,8},{8,0},{16,24},{24,16},{1,9},{9,1},{17,25},{25,17},{2,10},{10... | collective-permute-start | bytes 12582920 | tf_op jit(solution)/shard_map/ppermute | solution.py:873
  637.8 37.0 %collective-permute-start.63 = (bf16[128,2048]{1,0:T(8,128)(2,1)}, bf16[128,2048]{1,0:T(8,128)(2,1)}, u32[]{:S(2)}, u32[]{:S(2)}) collective-permute-start(bf16[128,2048]{1,0:T(8,128)(2,1)} %get-tuple-element.420), channel_id=1, source_target_pairs={{2,0},{3,2},{1,3},{0,1},{6,4},{7,6},{5,7},{4,5},{10,8},{11,10},{9,... | collective-permute-start | bytes 1572872 | tf_op jit(solution)/shard_map/ppermute | solution.py:773
  638.9 38.5 %collective-permute-start.61 = (bf16[128,2048]{1,0:T(8,128)(2,1)}, bf16[128,2048]{1,0:T(8,128)(2,1)S(1)}, u32[]{:S(2)}, u32[]{:S(2)}) collective-permute-start(bf16[128,2048]{1,0:T(8,128)(2,1)} %get-tuple-element.421), channel_id=1, source_target_pairs={{0,2},{2,3},{3,1},{1,0},{4,6},{6,7},{7,5},{5,4},{8,10},{10,11},{11... | collective-permute-start | bytes 1572872 | tf_op jit(solution)/shard_map/ppermute | solution.py:770
  715.0 36.8 %collective-permute-start.73 = (bf16[4096,512]{1,0:T(8,128)(2,1)}, bf16[4096,512]{1,0:T(8,128)(2,1)}, u32[]{:S(2)}, u32[]{:S(2)}) collective-permute-start(bf16[4096,512]{1,0:T(8,128)(2,1)} %get-tuple-element.304), channel_id=1, source_target_pairs={{0,8},{8,0},{16,24},{24,16},{1,9},{9,1},{17,25},{25,17},{2,10},{10... | collective-permute-start | bytes 12582920 | tf_op jit(solution)/shard_map/ppermute | solution.py:873
  722.3 47.2 %collective-permute-start.68 = (bf16[256,2048]{1,0:T(8,128)(2,1)}, bf16[256,2048]{1,0:T(8,128)(2,1)S(1)}, u32[]{:S(2)}, u32[]{:S(2)}) collective-permute-start(bf16[256,2048]{1,0:T(8,128)(2,1)} %add.657), channel_id=1, source_target_pairs={{2,0},{4,2},{6,4},{7,6},{5,7},{3,5},{1,3},{0,1},{10,8},{12,10},{14... | collective-permute-start | bytes 3145736 | tf_op jit(solution)/shard_map/ppermute | solution.py:773
  724.5 45.0 %collective-permute-start.67 = (bf16[256,2048]{1,0:T(8,128)(2,1)}, bf16[256,2048]{1,0:T(8,128)(2,1)S(1)}, u32[]{:S(2)}, u32[]{:S(2)}) collective-permute-start(bf16[256,2048]{1,0:T(8,128)(2,1)} %add.656), channel_id=1, source_target_pairs={{0,2},{2,4},{4,6},{6,7},{7,5},{5,3},{3,1},{1,0},{8,10},{10,12},{12... | collective-permute-start | bytes 3145736 | tf_op jit(solution)/shard_map/ppermute | solution.py:770
  745.7 38.6 %collective-permute-start.75 = (bf16[256,1024]{1,0:T(8,128)(2,1)}, bf16[256,1024]{1,0:T(8,128)(2,1)}, u32[]{:S(2)}, u32[]{:S(2)}) collective-permute-start(bf16[256,1024]{1,0:T(8,128)(2,1)} %pad_maximum_fusion.17), channel_id=1, source_target_pairs={{0,4},{1,5},{2,6},{3,7},{4,0},{5,1},{6,2},{7,3},{8,12},{9,13},{10,... | collective-permute-start | bytes 1572872 | tf_op jit(solution)/shard_map/ppermute | solution.py:986
  751.7 42.9 %collective-permute-start.76 = (bf16[256,1024]{1,0:T(8,128)(2,1)}, bf16[256,1024]{1,0:T(8,128)(2,1)}, u32[]{:S(2)}, u32[]{:S(2)}) collective-permute-start(bf16[256,1024]{1,0:T(8,128)(2,1)} %pad_maximum_fusion.18), channel_id=1, source_target_pairs={{0,4},{1,5},{2,6},{3,7},{4,0},{5,1},{6,2},{7,3},{8,12},{9,13},{10,... | collective-permute-start | bytes 1572872 | tf_op jit(solution)/shard_map/ppermute | solution.py:986
  (190 other events, 2240.1 us)
Sparse Core Ops, SparseCore 0:
  9.6 16.3 all-gather.6
  62.7 11.4 all-gather.8
  172.6 11.7 all-gather.10

commit v4 on v3

--- a/solution.py
+++ b/solution.py
@@ -628,7 +628,7 @@
         out[b * size : (b + 1) * size] = outer_rows(refs[b][...], mat[...]).astype(LOW)
 
 
-def attended_back_call(blocks, mat, given, first, total):
+def attended_back_call(blocks, mat, given, first, total, tokens):
     size, width = blocks[0].shape
     columns, count = mat.shape[0], len(blocks)
     at = first // (count * size)
@@ -638,14 +638,14 @@
         grid=(1,),
         in_specs=[fixed_block((columns, width))]
         + [fixed_block((size, width))] * count
-        + [ANYWHERE] * len(given),
+        + [ANYWHERE] * (len(given) + len(tokens)),
         out_specs=pl.BlockSpec((count * size, columns), lambda i: (at, 0)),
         out_shape=Shape((total, columns), LOW),
         input_output_aliases={1 + count: 0} if given else {},
         compiler_params=roomy(),
         cost_estimate=cost(2 * count * size * width * columns, 0, 10),
         name="attended_back",
-    )(mat, *blocks, *given)
+    )(mat, *blocks, *given, *tokens)
 
 
 def rows_back_body(count, *refs):
@@ -682,7 +682,7 @@
         out_specs=[pl.BlockSpec((size, step), lambda i: (0, i))] * blocks,
         out_shape=[Shape((size, 2 * half), LOW)] * blocks,
         compiler_params=roomy(),
-        cost_estimate=cost(4 * count * rows * columns * half, 0, 2.5),
+        cost_estimate=cost(4 * count * rows * columns * half, 0, 25),
         name="rows_back",
     )(*grads, *[mat[0] for mat in mats], *[mat[1] for mat in mats], *tokens)
 
@@ -718,7 +718,7 @@
         out_specs=pl.BlockSpec((step, 4 * columns), lambda i: (i, 0)),
         out_shape=Shape((width // 2, 4 * columns), LOW),
         compiler_params=roomy(),
-        cost_estimate=cost(4 * total * width * columns, 0, 2.5),
+        cost_estimate=cost(4 * total * width * columns, 0, 25),
         name="weight_back",
     )(rows, *grads, *branch, *attended, *tokens)
 
@@ -750,7 +750,7 @@
         out_specs=fixed_block((2 * half, 1)),
         out_shape=Shape((2 * half, 1), FULL),
         compiler_params=roomy(),
-        cost_estimate=cost(0, 12 * half * columns, 2),
+        cost_estimate=cost(0, 12 * half * columns, 20),
         name="gain",
     )(others, mine, *mats, *tokens)
 
@@ -940,7 +940,9 @@
             while step < size:
                 self.hops.append((axis, [(i, i ^ step) for i in range(size)]))
                 step *= 2
-        self.hops = [self.hops[0], self.hops[-1], *self.hops[1:-1]]
+        along_tensor = [hop for hop in self.hops[1:] if hop[0] == "tensor"]
+        along_expert = [hop for hop in self.hops[1:] if hop[0] == "expert"]
+        self.hops = [self.hops[0], *along_tensor[:-1], *along_expert, along_tensor[-1]]
 
     def hop(self):
         if self.value is not None:
@@ -1235,23 +1237,21 @@
             pair, others = after((pair, others))
             mixture_steps.hop(mixed[-1:], pair[0])
             others = [owners.cross(other) for other in others]
-            found["attn"] = None
-            for b, block in enumerate([*gathered_back, *pair]):
-                found["attn"] = attended_back_call(
-                    [block], out_full, found["attn"], b * tok_rows, length
-                )
             found["pre"] = [
-                pre_grads(s, 0, [other], [found["attn"]]) for s, other in zip(chip_shifts, others)
+                pre_grads(s, 0, [other], [pair[0]]) for s, other in zip(chip_shifts, others)
             ]
+            found["attn"] = attended_back_call(
+                [*gathered_back, *pair], out_full, None, 0, length, found["pre"]
+            )
         elif k == part_count // 2:
-            pair, mixture_steps.pair = after((pair, mixture_steps.pair), found["pre"])
+            pair, mixture_steps.pair = after((pair, mixture_steps.pair), found["attn"])
         return pair
 
     seq_ring.gather(grad_branch, lambda k, blocks: gathered_back.extend(blocks), back_hop)
     grad_attn = found["attn"]
     for b in range(3, part_count):
         grad_attn = attended_back_call(
-            [gathered_back[b]], out_full, grad_attn, b * tok_rows, length
+            [gathered_back[b]], out_full, grad_attn, b * tok_rows, length, []
         )
 
     def mixture_hop(k, *tokens):
@@ -1260,7 +1260,7 @@
     mixture_steps.pair, sent_down[:] = after((mixture_steps.pair, sent_down), grad_attn)
     mixture_hop(tensor_count // 2 - 1)
     sent_pre = [
-        owners.along(after(part, sent_down), -s) for s, part in zip(chip_shifts, found["pre"])
+        owners.along(part, -s) for s, part in zip(chip_shifts, found["pre"])
     ]
     *head_grads, grad_gains = attend_back_call(
         query_low,
@@ -1292,12 +1292,15 @@
     normed_parts = rows_back_call(
         head_grads, full_mats, tok_rows, [mine_half, *mixture_steps.sent]
     )
+    mixture_steps.pair = after(mixture_steps.pair, normed_parts[-1])
+    for k in range(tensor_count // 2 - 3, 0, -1):
+        mixture_hop(k)
     listed_norm = gain_call(
         own_other_half,
         mine_half,
         [m for pair in full_mats for m in pair],
         local_width,
-        [normed_parts[-1], *mixture_steps.pair, *sent_pre],
+        [*mixture_steps.sent, *sent_pre],
     )
     grad_norm_gain = owners.unlist_columns(listed_norm.T) / norm_gain
     room = model_width - grad_gains.size
@@ -1329,7 +1332,6 @@
             parts, sent_parts[:], small_steps.value = after(
                 (parts, sent_parts, small_steps.value)
             )
-            small_steps.hop()
         if k == 0:
             sent = after(sent_parts[0], tokens)
             come.append([owners.along(part, -s) for s, part in zip(chip_shifts, sent)])
@@ -1338,10 +1340,9 @@
         return parts
 
     def normed_done(pair):
-        pair, come[0], small_steps.value = after(
-            (pair, come[0], small_steps.value), found["own_other"]
+        pair, come[0], mixture_steps.pair = after(
+            (pair, come[0], mixture_steps.pair), found["own_other"]
         )
-        small_steps.hop()
         return pair
 
     grad_normed_one = seq_ring.scatter(give_parts, normed_done)
@@ -1349,9 +1350,29 @@
     grad_normed_one = owners.unlist_columns(grad_normed_one)
     sent = after(sent_parts[1], done)
     come.append([owners.along(part, -s) for s, part in zip(chip_shifts, sent)])
-    mixture_steps.pair = after(mixture_steps.pair, done)
-    for k in range(tensor_count // 2 - 3, 0, -1):
-        mixture_hop(k)
+    small_steps.value = after(small_steps.value, done)
+    small_steps.hop()
+    def columns_of(place, seq):
+        first = (place * seq_count + seq) * block_width
+        return slice(first, first + block_width)
+
+    def summed_piece(p, columns):
+        return both_cores(0, pieces[p], columns) + sum(
+            part[:, columns].astype(FULL) for part in come[p]
+        )
+
+    def swap_piece(p):
+        return [
+            seq_swap(
+                jnp.concatenate(
+                    [summed_piece(p, columns_of(place, s)).astype(LOW) for place in range(4)],
+                    axis=1,
+                ),
+                -s,
+            )
+            for s in seq_shifts
+        ]
+
     own_other_down, own_other = owners.cross(
         after((found["own_other_down"], found["own_other"]), done)
     )
@@ -1365,7 +1386,10 @@
         [done],
         kind=FULL,
     )
-    come[1], small_steps.value = after((come[1], small_steps.value), grad_down)
+    swapped_pieces = [swap_piece(0)]
+    come[1], small_steps.value, swapped_pieces[0] = after(
+        (come[1], small_steps.value, swapped_pieces[0]), grad_down
+    )
     small_steps.hop()
     grad_gate, grad_up = slab_grads_call(
         shared_all[0][2],
@@ -1378,38 +1402,15 @@
         parts=2,
         kind=FULL,
     )
-    def columns_of(place, seq):
-        first = (place * seq_count + seq) * block_width
-        return slice(first, first + block_width)
-
-    def summed_piece(p, columns):
-        return both_cores(0, pieces[p], columns) + sum(
-            part[:, columns].astype(FULL) for part in come[p]
-        )
-
-    swapped_pieces = [
-        [
-            seq_swap(
-                jnp.concatenate(
-                    [summed_piece(p, columns_of(place, s)).astype(LOW) for place in range(4)],
-                    axis=1,
-                ),
-                -s,
-            )
-            for s in seq_shifts
-        ]
-        for p in range(2)
-    ]
-    mixture_steps.pair, small_steps.value = after(
-        (mixture_steps.pair, small_steps.value), grad_gate
-    )
+    swapped_pieces.append(swap_piece(1))
+    small_steps.value = after(small_steps.value, grad_gate)
     layer_out = (residual + mixture_steps.total(mixed[0])).astype(jnp.bfloat16)
     grad_unit_one = grad_normed_one * norm_gain
     grad_tokens = grad_residual + inv_one * (
         grad_unit_one - unit_one * jnp.mean(grad_unit_one * unit_one, axis=-1, keepdims=True)
     )
     grad_tokens = grad_tokens.astype(jnp.bfloat16)
-    swapped_pieces = after(swapped_pieces, layer_out, grad_tokens)
+    swapped_pieces = after(swapped_pieces, layer_out, grad_tokens, grad_gate)
     owned = [[] for _ in range(4)]
     for p, swapped in enumerate(swapped_pieces):
         for place in range(4):

time: 822 us -> 809 us (0.984)
    unnamed x281 -> x279, local copies, waits for them, and re-layouts: 52.6 us -> 53.5 us
  transfers between devices with their start and end apart: 80 -> 80, of which waited for: 26 -> 25; matrix products, arithmetic and copies ran while one was open for 14% -> 14% of each run, Pallas kernels for 48% -> 48%
where the time goes in v4:
time: 809 us; the launch traced here: 799 us
  Pallas kernels  397 us (49%)
  waiting for transfers between devices  138 us (17%)
  local copies, waits for them, and re-layouts  84.1 us (10%)
  starting transfers between devices  82.5 us (10%)
  other arithmetic  65.5 us (8%)
  between operations  16.1 us (2%)
  matrix products  15.4 us (2%)
    pallas_call x10, Pallas kernels, experts_call(): pl.pallas_call(functools.partial(experts_body, blocks, experts, slabs, in...  172 us
    pallas_call x8, Pallas kernels, slab_grads_call(): pl.pallas_call(functools.partial(slab_grads_body, swapped, parts, joined)...  101 us
    unnamed x279, local copies, waits for them, and re-layouts  53.5 us
    ppermute x5, waiting for transfers between devices, seq_swap(): return lax.ppermute(value, 'tensor', pairs)  47.3 us
    ppermute x24, waiting for transfers between devices, right(): lax.ppermute(v, self.axis, self.rightward)  37.8 us
    ppermute x24, starting transfers between devices, left(): lax.ppermute(v, self.axis, self.leftward)  29 us
    ppermute x9, waiting for transfers between devices, along(): return jax.tree.map(lambda v: lax.ppermute(v, 'expert', pairs), value)  27.7 us
    pallas_call x1, Pallas kernels, attend_back_call(): pl.pallas_call(lambda *refs: attend_back_body(step, *refs[:6 + len(fixed)...  26.9 us
  transfers between devices with their start and end apart: 80, of which 25 were waited for; matrix products, arithmetic and copies ran while one was open for 14% of the time, Pallas kernels for 48%

profile of v4, /device:TPU:0, one launch (start us, length us, event | category | flops | bytes accessed | tf_op | source)
XLA Modules:
  0.0 798.6 jit_solution(8336334873999131444)
XLA Ops:
  29.3 17.9 %collective-permute-done.2.refs_2_ = bf16[512,512]{1,0:T(8,128)(2,1)S(1)} collective-permute-done((bf16[512,512]{1,0:T(8,128)(2,1)S(1)}, bf16[512,512]{1,0:T(8,128)(2,1)S(1)}, u32[]{:S(2)}, u32[]{:S(2)}) %collective-permute-start.2) | collective-permute-done | bytes 524320 | tf_op jit(solution)/shard_map/ppermute | solution.py:988
  62.8 14.4 %collective-permute-done.6.refs_3_ = bf16[512,256]{1,0:T(8,128)(2,1)S(1)} collective-permute-done((bf16[512,256]{1,0:T(8,128)(2,1)}, bf16[512,256]{1,0:T(8,128)(2,1)S(1)}, u32[]{:S(2)}, u32[]{:S(2)}) %collective-permute-start.6) | collective-permute-done | bytes 262176 | tf_op jit(solution)/shard_map/ppermute | solution.py:988
  108.1 9.6 %project.1 = (f32[1024,512]{1,0:T(8,128)}, bf16[1024,512]{1,0:T(8,128)(2,1)}, f32[1024,512]{1,0:T(8,128)}, bf16[1024,512]{1,0:T(8,128)(2,1)}) custom-call(bf16[1024,2048]{1,0:T(8,128)(2,1)} %constant_dynamic-update-slice_fusion.rows.refs_0_, bf16[1024,512]{1,0:T(8,128)(2,1)} %get-tuple-element.409.query.refs_3_.refs_0_, ...), custom_call_target="tpu_custom_call" | custom-call | flops 2147483648 | tf_op jit(solution)/shard_map/project/pallas_call | solution.py:439
  182.3 10.3 %collective-permute-done.21 = bf16[256,2048]{1,0:T(8,128)(2,1)} collective-permute-done((bf16[256,2048]{1,0:T(8,128)(2,1)S(1)}, bf16[256,2048]{1,0:T(8,128)(2,1)}, u32[]{:S(2)}, u32[]{:S(2)}) %collective-permute-start.21) | collective-permute-done | bytes 1048608 | tf_op jit(solution)/shard_map/ppermute | solution.py:773
  213.0 12.1 %experts.10 = (bf16[256,2176]{1,0:T(8,128)(2,1)}, bf16[256,2048]{1,0:T(8,128)(2,1)}, bf16[2048,1024]{1,0:T(8,128)(2,1)}, bf16[2048,2048]{1,0:T(8,128)(2,1)}, bf1...) custom-call(s32[13]{0:T(128)} %stack.77.numbers, bf16[256,2176]{1,0:T(8,128)(2,1)} %concatenate.130.refs_0_, ...), custom_call_target="tpu_custom_call" | custom-call | flops 2386093056 | tf_op jit(solution)/shard_map/experts/pallas_call | solution.py:294
  225.1 24.4 %collective-permute-done.24.refs_2_ = bf16[256,2048]{1,0:T(8,128)(2,1)S(1)} collective-permute-done((bf16[256,2048]{1,0:T(8,128)(2,1)}, bf16[256,2048]{1,0:T(8,128)(2,1)S(1)}, u32[]{:S(2)}, u32[]{:S(2)}) %collective-permute-start.24) | collective-permute-done | bytes 1048608 | tf_op jit(solution)/shard_map/ppermute | solution.py:770
  258.7 19.9 %experts.11 = (bf16[256,2176]{1,0:T(8,128)(2,1)}, bf16[256,2176]{1,0:T(8,128)(2,1)}, bf16[256,2048]{1,0:T(8,128)(2,1)}, bf16[256,2048]{1,0:T(8,128)(2,1)}, bf16[...) custom-call(s32[13]{0:T(128)} %stack.77.numbers, ...), custom_call_target="tpu_custom_call", output_to_operand_aliasing={{4}: (11, {}), {5}: (12, {}), {6}: (13, {}), {7}: (14, {})} | custom-call | flops 4772186112 | tf_op jit(solution)/shard_map/experts/pallas_call | solution.py:294
  291.9 19.8 %experts.12 = (bf16[256,2176]{1,0:T(8,128)(2,1)}, bf16[256,2176]{1,0:T(8,128)(2,1)}, bf16[256,2048]{1,0:T(8,128)(2,1)}, bf16[256,2048]{1,0:T(8,128)(2,1)}, bf16[...) custom-call(s32[13]{0:T(128)} %stack.77.numbers, ...), custom_call_target="tpu_custom_call", output_to_operand_aliasing={{4}: (11, {}), {5}: (12, {}), {6}: (13, {}), {7}: (14, {})} | custom-call | flops 4772186112 | tf_op jit(solution)/shard_map/experts/pallas_call | solution.py:294
  321.8 19.7 %experts.13 = (bf16[256,2176]{1,0:T(8,128)(2,1)}, bf16[256,2176]{1,0:T(8,128)(2,1)}, bf16[256,2048]{1,0:T(8,128)(2,1)}, bf16[256,2048]{1,0:T(8,128)(2,1)}, bf16[...) custom-call(s32[13]{0:T(128)} %stack.77.numbers, ...), custom_call_target="tpu_custom_call", output_to_operand_aliasing={{4}: (11, {}), {5}: (12, {}), {6}: (13, {}), {7}: (14, {})} | custom-call | flops 4772186112 | tf_op jit(solution)/shard_map/experts/pallas_call | solution.py:294
  342.7 12.6 %experts.14 = (bf16[256,2176]{1,0:T(8,128)(2,1)}, bf16[256,2048]{1,0:T(8,128)(2,1)}, bf16[2048,1024]{1,0:T(8,128)(2,1)}, bf16[2048,2048]{1,0:T(8,128)(2,1)}, bf1...) custom-call(s32[13]{0:T(128)} %stack.77.numbers, ...), custom_call_target="tpu_custom_call", output_to_operand_aliasing={{2}: (9, {}), {3}: (10, {}), {4}: (11, {}), {5}: (12, {})} | custom-call | flops 2386093056 | tf_op jit(solution)/shard_map/experts/pallas_call | solution.py:294
  355.3 12.9 %experts.15 = (bf16[256,2176]{1,0:T(8,128)(2,1)}, bf16[256,2048]{1,0:T(8,128)(2,1)}, bf16[2048,1024]{1,0:T(8,128)(2,1)}, bf16[2048,2048]{1,0:T(8,128)(2,1)}) custom-call(s32[13]{0:T(128)} %stack.77.numbers, bf16[256,2176]{1,0:T(8,128)(2,1)} %copy-done.45, bf16[256,2048]{1,0:T(8,128)(2,1)} %copy-done.46, ...), custom_call_target="tpu_custom_call" | custom-call | flops 2386093056 | tf_op jit(solution)/shard_map/experts/pallas_call | solution.py:294
  371.6 20.8 %experts.16 = (bf16[256,2176]{1,0:T(8,128)(2,1)}, bf16[256,2176]{1,0:T(8,128)(2,1)}, bf16[256,2048]{1,0:T(8,128)(2,1)}, bf16[256,2048]{1,0:T(8,128)(2,1)}, bf16[...) custom-call(s32[13]{0:T(128)} %stack.77.numbers, ...), custom_call_target="tpu_custom_call", output_to_operand_aliasing={{4}: (15, {}), {5}: (16, {})} | custom-call | flops 4772186112 | tf_op jit(solution)/shard_map/experts/pallas_call | solution.py:294
  397.1 20.8 %experts.17 = (bf16[256,2176]{1,0:T(8,128)(2,1)}, bf16[256,2176]{1,0:T(8,128)(2,1)}, bf16[256,2048]{1,0:T(8,128)(2,1)}, bf16[256,2048]{1,0:T(8,128)(2,1)}, bf16[...) custom-call(s32[13]{0:T(128)} %stack.77.numbers, ...), custom_call_target="tpu_custom_call", output_to_operand_aliasing={{4}: (15, {}), {5}: (16, {})} | custom-call | flops 4772186112 | tf_op jit(solution)/shard_map/experts/pallas_call | solution.py:294
  424.5 20.7 %experts.18 = (bf16[256,2176]{1,0:T(8,128)(2,1)}, bf16[256,2176]{1,0:T(8,128)(2,1)}, bf16[256,2048]{1,0:T(8,128)(2,1)}, bf16[256,2048]{1,0:T(8,128)(2,1)}, bf16[...) custom-call(s32[13]{0:T(128)} %stack.77.numbers, ...), custom_call_target="tpu_custom_call", output_to_operand_aliasing={{4}: (15, {}), {5}: (16, {})} | custom-call | flops 4772186112 | tf_op jit(solution)/shard_map/experts/pallas_call | solution.py:294
  450.8 12.7 %experts.19 = (bf16[256,2176]{1,0:T(8,128)(2,1)}, bf16[256,2048]{1,0:T(8,128)(2,1)}, bf16[2048,1024]{1,0:T(8,128)(2,1)}, bf16[2048,2048]{1,0:T(8,128)(2,1)}) custom-call(s32[13]{0:T(128)} %stack.77.numbers, bf16[256,2176]{1,0:T(8,128)(2,1)} %concatenate.130.refs_0_, ...), custom_call_target="tpu_custom_call", output_to_operand_aliasing={{2}: (11, {}), {3}: (12, {})} | custom-call | flops 2386093056 | tf_op jit(solution)/shard_map/experts/pallas_call | solution.py:294
  485.1 10.1 %slab_grads.9.refs_0_ = bf16[512,2048]{1,0:T(8,128)(2,1)} custom-call(bf16[2048,2048]{1,0:T(8,128)(2,1)} %get-tuple-element.253.rows, bf16[2048,1024]{1,0:T(8,128)(2,1)} %get-tuple-element.254.kept, bf16[512,2048]{1,0:T(8,128)(2,1)} %copy-done.90, bf16[256,2048]{1,0:T(8,128)(2,1)} %copy-done.10), custom_call_target="tpu_custom_call" | custom-call | flops 1431655808 | tf_op jit(solution)/shard_map/slab_grads/pallas_call | solution.py:381
  495.2 14.5 %slab_grads.10.refs_2_ = bf16[4096,512]{1,0:T(8,128)(2,1)} custom-call(bf16[2048,2048]{1,0:T(8,128)(2,1)} %get-tuple-element.257.rows, bf16[2048,2048]{1,0:T(8,128)(2,1)} %get-tuple-element.258.kept, bf16[512,2048]{1,0:T(8,128)(2,1)} %slab_grads.9.refs_0_), custom_call_target="tpu_custom_call" | custom-call | flops 2863311616 | tf_op jit(solution)/shard_map/slab_grads/pallas_call | solution.py:381
  524.4 15.0 %slab_grads.11.refs_3_ = bf16[4096,512]{1,0:T(8,128)(2,1)} custom-call(bf16[2048,2048]{1,0:T(8,128)(2,1)} %get-tuple-element.257.rows, bf16[2048,2048]{1,0:T(8,128)(2,1)} %get-tuple-element.258.kept, bf16[4096,512]{1,0:T(8,128)(2,1)} %collective-permute-done.52.refs_0_, bf16[256,2048]{1,0:T(8,128)(2,1)} %get-tuple-element.260.refs_1_.refs_5_), custom_call_target="tpu_custom_call" | custom-call | flops 2863311616 | tf_op jit(solution)/shard_map/slab_grads/pallas_call | solution.py:381
  569.5 26.9 %attend_back.1 = (bf16[1024,512]{1,0:T(8,128)(2,1)}, bf16[1024,512]{1,0:T(8,128)(2,1)}, bf16[1024,512]{1,0:T(8,128)(2,1)}, f32[2,128]{1,0:T(2,128)}) custom-call(bf16[1024,512]{1,0:T(8,128)(2,1)} %get-tuple-element.171.refs_2_.query.refs_0_, bf16[1024,512]{1,0:T(8,128)(2,1)} %get-tuple-element.172.key.refs_1_, bf16[1024,512]{1,0:T(8,128)(2,1)} %values.1.value.refs_2_, ...), custom_call_target="tpu_custom_call" | custom-call | flops 1073741824 | tf_op jit(solution)/shard_map/attend_back/pallas_call | solution.py:607
  623.2 11.5 %rows_back.1 = (bf16[256,2048]{1,0:T(8,128)(2,1)}, bf16[256,2048]{1,0:T(8,128)(2,1)}, bf16[256,2048]{1,0:T(8,128)(2,1)}, bf16[256,2048]{1,0:T(8,128)(2,1)}) custom-call(bf16[1024,512]{1,0:T(8,128)(2,1)} %get-tuple-element.274.refs_1_.refs_0_, bf16[1024,512]{1,0:T(8,128)(2,1)} %get-tuple-element.275.refs_2_.refs_1_, ...), custom_call_target="tpu_custom_call" | custom-call | flops 257698032 | tf_op jit(solution)/shard_map/rows_back/pallas_call | solution.py:675
  645.4 14.4 %collective-permute-done.59.refs_8_.refs_1_ = bf16[4096,512]{1,0:T(8,128)(2,1)} collective-permute-done((bf16[4096,512]{1,0:T(8,128)(2,1)}, bf16[4096,512]{1,0:T(8,128)(2,1)}, u32[]{:S(2)}, u32[]{:S(2)}) %collective-permute-start.59) | collective-permute-done | bytes 4194336 | tf_op jit(solution)/shard_map/ppermute | solution.py:877
  692.5 14.5 %slab_grads.13.refs_5_.refs_1_ = bf16[4096,512]{1,0:T(8,128)(2,1)} custom-call(bf16[2048,2048]{1,0:T(8,128)(2,1)} %get-tuple-element.257.rows, bf16[2048,2048]{1,0:T(8,128)(2,1)} %get-tuple-element.292.kept, bf16[512,2048]{1,0:T(8,128)(2,1)} %slab_grads.12.refs_0_), custom_call_target="tpu_custom_call" | custom-call | flops 2863311616 | tf_op jit(solution)/shard_map/slab_grads/pallas_call | solution.py:381
  724.2 10.9 %slab_grads.14.refs_3_ = f32[512,2048]{1,0:T(8,128)} custom-call(bf16[2048,2048]{1,0:T(8,128)(2,1)} %get-tuple-element.253.rows, bf16[2048,1024]{1,0:T(8,128)(2,1)} %get-tuple-element.293.kept, bf16[512,2048]{1,0:T(8,128)(2,1)} %collective-permute-done.71.refs_0_, bf16[512,2048]{1,0:T(8,128)(2,1)} %get-tuple-element.303.refs_1_, ...), custom_call_target="tpu_custom_call" | custom-call | flops 1431655808 | tf_op jit(solution)/shard_map/slab_grads/pallas_call | solution.py:381
  753.1 17.4 %slab_grads.15 = (f32[2048,512]{1,0:T(8,128)}, f32[2048,512]{1,0:T(8,128)}) custom-call(bf16[2048,2048]{1,0:T(8,128)(2,1)} %get-tuple-element.257.rows, bf16[2048,2048]{1,0:T(8,128)(2,1)} %get-tuple-element.292.kept, bf16[4096,512]{1,0:T(8,128)(2,1)} %collective-permute-done.73.refs_0_, bf16[4096,512]{1,0:T(8,128)(2,1)} %collective-permute-done.59.refs_8_.refs_1_, ...), custom_call_target="tpu_custom_call" | custom-call | flops 2863311616 | tf_op jit(solution)/shard_map/slab_grads/pallas_call | solution.py:381
  (601 shorter events, 398.6 us)
Async XLA Ops:
  7.2 205.8 %all-gather.7.cloned.1.call-start = ((), (), s32[]{:S(2)}) async-start(), calls=%async_computation | async-start | bytes 6291456 | tf_op jit(solution)/shard_map/all_gather | solution.py:881
  8.0 205.0 %all-gather.9.cloned.1.call-start = ((), (), s32[]{:S(2)}) async-start(), calls=%async_computation.1 | async-start | bytes 6291456 | tf_op jit(solution)/shard_map/all_gather | solution.py:881
  10.6 36.7 %collective-permute-start = (bf16[256,2048]{1,0:T(8,128)(2,1)S(1)}, bf16[256,2048]{1,0:T(8,128)(2,1)S(1)}, u32[]{:S(2)}, u32[]{:S(2)}) collective-permute-start(bf16[256,2048]{1,0:T(8,128)(2,1)S(1)} %get-tuple-element.442.refs_0_.refs_2_), channel_id=1, source_target_pairs={{0,2},{2,3},{3,1},{1,0},{4,6},{6,7},{7,5},{5,4},{8,10},{10,11},{11... | collective-permute-start | bytes 3145736 | tf_op jit(solution)/shard_map/ppermute | solution.py:770
  13.6 35.9 %collective-permute-start.1 = (bf16[256,2048]{1,0:T(8,128)(2,1)S(1)}, bf16[256,2048]{1,0:T(8,128)(2,1)S(1)}, u32[]{:S(2)}, u32[]{:S(2)}) collective-permute-start(bf16[256,2048]{1,0:T(8,128)(2,1)S(1)} %get-tuple-element.442.refs_0_.refs_2_), channel_id=1, source_target_pairs={{2,0},{3,2},{1,3},{0,1},{6,4},{7,6},{5,7},{4,5},{10,8},{11,10},{9,... | collective-permute-start | bytes 3145736 | tf_op jit(solution)/shard_map/ppermute | solution.py:773
  62.6 150.4 %all-gather.11.cloned.1.call-start = ((), (), s32[]{:S(2)}) async-start(), calls=%async_computation.2 | async-start | bytes 6291456 | tf_op jit(solution)/shard_map/all_gather | solution.py:881
  127.5 47.7 %collective-permute-start.19 = (bf16[512,2048]{1,0:T(8,128)(2,1)}, bf16[512,2048]{1,0:T(8,128)(2,1)S(1)}, u32[]{:S(2)}, u32[]{:S(2)}) collective-permute-start(bf16[512,2048]{1,0:T(8,128)(2,1)} %after.39), channel_id=1, source_target_pairs={{0,16},{8,24},{16,0},{24,8},{1,17},{9,25},{17,1},{25,9},{2,18},{10... | collective-permute-start | bytes 6291464 | tf_op jit(solution)/shard_map/ppermute | solution.py:877
  129.3 36.8 %collective-permute-start.15 = (bf16[256,2048]{1,0:T(8,128)(2,1)}, bf16[256,2048]{1,0:T(8,128)(2,1)S(1)}, u32[]{:S(2)}, u32[]{:S(2)}) collective-permute-start(bf16[256,2048]{1,0:T(8,128)(2,1)} %get-tuple-element.177.refs_0_.refs_2_), channel_id=1, source_target_pairs={{0,2},{2,4},{4,6},{6,7},{7,5},{5,3},{3,1},{1,0},{8,10},{10,12},{12... | collective-permute-start | bytes 3145736 | tf_op jit(solution)/shard_map/ppermute | solution.py:770
  129.6 36.5 %collective-permute-start.16 = (bf16[256,2048]{1,0:T(8,128)(2,1)}, bf16[256,2048]{1,0:T(8,128)(2,1)}, u32[]{:S(2)}, u32[]{:S(2)}) collective-permute-start(bf16[256,2048]{1,0:T(8,128)(2,1)} %get-tuple-element.178.refs_1_.refs_3_), channel_id=1, source_target_pairs={{2,0},{4,2},{6,4},{7,6},{5,7},{3,5},{1,3},{0,1},{10,8},{12,10},{14... | collective-permute-start | bytes 3145736 | tf_op jit(solution)/shard_map/ppermute | solution.py:773
  203.5 47.5 %collective-permute-start.22 = (bf16[256,2176]{1,0:T(8,128)(2,1)}, bf16[256,2176]{1,0:T(8,128)(2,1)}, u32[]{:S(2)}, u32[]{:S(2)}) collective-permute-start(bf16[256,2176]{1,0:T(8,128)(2,1)} %concatenate.130.refs_0_), channel_id=1, source_target_pairs={{0,2},{2,4},{4,6},{6,7},{7,5},{5,3},{3,1},{1,0},{8,10},{10,12},{12... | collective-permute-start | bytes 3342344 | tf_op jit(solution)/shard_map/ppermute | solution.py:770
  205.0 46.0 %collective-permute-start.23 = (bf16[256,2176]{1,0:T(8,128)(2,1)}, bf16[256,2176]{1,0:T(8,128)(2,1)}, u32[]{:S(2)}, u32[]{:S(2)}) collective-permute-start(bf16[256,2176]{1,0:T(8,128)(2,1)} %concatenate.130.refs_0_), channel_id=1, source_target_pairs={{2,0},{4,2},{6,4},{7,6},{5,7},{3,5},{1,3},{0,1},{10,8},{12,10},{14... | collective-permute-start | bytes 3342344 | tf_op jit(solution)/shard_map/ppermute | solution.py:773
  208.8 40.6 %collective-permute-start.24 = (bf16[256,2048]{1,0:T(8,128)(2,1)}, bf16[256,2048]{1,0:T(8,128)(2,1)S(1)}, u32[]{:S(2)}, u32[]{:S(2)}) collective-permute-start(bf16[256,2048]{1,0:T(8,128)(2,1)} %get-tuple-element.185), channel_id=1, source_target_pairs={{0,2},{2,4},{4,6},{6,7},{7,5},{5,3},{3,1},{1,0},{8,10},{10,12},{12... | collective-permute-start | bytes 3145736 | tf_op jit(solution)/shard_map/ppermute | solution.py:770
  210.3 40.7 %collective-permute-start.25 = (bf16[256,2048]{1,0:T(8,128)(2,1)}, bf16[256,2048]{1,0:T(8,128)(2,1)S(1)}, u32[]{:S(2)}, u32[]{:S(2)}) collective-permute-start(bf16[256,2048]{1,0:T(8,128)(2,1)} %get-tuple-element.186), channel_id=1, source_target_pairs={{2,0},{4,2},{6,4},{7,6},{5,7},{3,5},{1,3},{0,1},{10,8},{12,10},{14... | collective-permute-start | bytes 3145736 | tf_op jit(solution)/shard_map/ppermute | solution.py:773
  210.9 100.8 %collective-permute-start.32 = (bf16[4096,512]{1,0:T(8,128)(2,1)}, bf16[4096,512]{1,0:T(8,128)(2,1)}, u32[]{:S(2)}, u32[]{:S(2)}) collective-permute-start(bf16[4096,512]{1,0:T(8,128)(2,1)} %after.44), channel_id=1, source_target_pairs={{0,16},{8,24},{16,0},{24,8},{1,17},{9,25},{17,1},{25,9},{2,18},{10... | collective-permute-start | bytes 12582920 | tf_op jit(solution)/shard_map/ppermute | solution.py:877
  252.0 34.6 %collective-permute-start.26 = (bf16[256,2176]{1,0:T(8,128)(2,1)}, bf16[256,2176]{1,0:T(8,128)(2,1)S(1)}, u32[]{:S(2)}, u32[]{:S(2)}) collective-permute-start(bf16[256,2176]{1,0:T(8,128)(2,1)} %get-tuple-element.188.refs_0_), channel_id=1, source_target_pairs={{0,2},{2,4},{4,6},{6,7},{7,5},{5,3},{3,1},{1,0},{8,10},{10,12},{12... | collective-permute-start | bytes 3342344 | tf_op jit(solution)/shard_map/ppermute | solution.py:770
  252.6 34.0 %collective-permute-start.27 = (bf16[256,2176]{1,0:T(8,128)(2,1)}, bf16[256,2176]{1,0:T(8,128)(2,1)S(1)}, u32[]{:S(2)}, u32[]{:S(2)}) collective-permute-start(bf16[256,2176]{1,0:T(8,128)(2,1)} %get-tuple-element.189.refs_1_), channel_id=1, source_target_pairs={{2,0},{4,2},{6,4},{7,6},{5,7},{3,5},{1,3},{0,1},{10,8},{12,10},{14... | collective-permute-start | bytes 3342344 | tf_op jit(solution)/shard_map/ppermute | solution.py:773
  317.7 37.6 %collective-permute-start.34 = (bf16[4096,512]{1,0:T(8,128)(2,1)}, bf16[4096,512]{1,0:T(8,128)(2,1)}, u32[]{:S(2)}, u32[]{:S(2)}) collective-permute-start(bf16[4096,512]{1,0:T(8,128)(2,1)} %get-tuple-element.209.refs_2_.refs_3_.refs_4_.refs_5_), channel_id=1, source_target_pairs={{0,8},{8,0},{16,24},{24,16},{1,9},{9,1},{17,25},{25,17},{2,10},{10... | collective-permute-start | bytes 12582920 | tf_op jit(solution)/shard_map/ppermute | solution.py:873
  511.8 48.5 %collective-permute-start.53 = (bf16[512,2048]{1,0:T(8,128)(2,1)}, bf16[512,2048]{1,0:T(8,128)(2,1)S(1)}, u32[]{:S(2)}, u32[]{:S(2)}) collective-permute-start(bf16[512,2048]{1,0:T(8,128)(2,1)} %slab_grads.9.refs_0_), channel_id=1, source_target_pairs={{0,16},{8,24},{16,0},{24,8},{1,17},{9,25},{17,1},{25,9},{2,18},{10... | collective-permute-start | bytes 6291464 | tf_op jit(solution)/shard_map/ppermute | solution.py:877
  567.7 92.1 %collective-permute-start.59 = (bf16[4096,512]{1,0:T(8,128)(2,1)}, bf16[4096,512]{1,0:T(8,128)(2,1)}, u32[]{:S(2)}, u32[]{:S(2)}) collective-permute-start(bf16[4096,512]{1,0:T(8,128)(2,1)} %slab_grads.11.refs_3_), channel_id=1, source_target_pairs={{0,16},{8,24},{16,0},{24,8},{1,17},{9,25},{17,1},{25,9},{2,18},{10... | collective-permute-start | bytes 12582920 | tf_op jit(solution)/shard_map/ppermute | solution.py:877
  606.9 63.0 %collective-permute-start.56 = (bf16[1024,2048]{1,0:T(8,128)(2,1)}, bf16[1024,2048]{1,0:T(8,128)(2,1)}, u32[]{:S(2)}, u32[]{:S(2)}) collective-permute-start(bf16[1024,2048]{1,0:T(8,128)(2,1)} %weight_back.2.refs_12_.refs_2_.others), channel_id=1, source_target_pairs={{0,8},{8,0},{16,24},{24,16},{1,9},{9,1},{17,25},{25,17},{2,10},{10... | collective-permute-start | bytes 12582920 | tf_op jit(solution)/shard_map/ppermute | solution.py:873
  637.0 37.4 %collective-permute-start.63 = (bf16[128,2048]{1,0:T(8,128)(2,1)}, bf16[128,2048]{1,0:T(8,128)(2,1)}, u32[]{:S(2)}, u32[]{:S(2)}) collective-permute-start(bf16[128,2048]{1,0:T(8,128)(2,1)} %get-tuple-element.418), channel_id=1, source_target_pairs={{2,0},{3,2},{1,3},{0,1},{6,4},{7,6},{5,7},{4,5},{10,8},{11,10},{9,... | collective-permute-start | bytes 1572872 | tf_op jit(solution)/shard_map/ppermute | solution.py:773
  638.1 38.9 %collective-permute-start.61 = (bf16[128,2048]{1,0:T(8,128)(2,1)}, bf16[128,2048]{1,0:T(8,128)(2,1)}, u32[]{:S(2)}, u32[]{:S(2)}) collective-permute-start(bf16[128,2048]{1,0:T(8,128)(2,1)} %get-tuple-element.419), channel_id=1, source_target_pairs={{0,2},{2,3},{3,1},{1,0},{4,6},{6,7},{7,5},{5,4},{8,10},{10,11},{11... | collective-permute-start | bytes 1572872 | tf_op jit(solution)/shard_map/ppermute | solution.py:770
  642.9 64.1 %collective-permute-start.67 = (bf16[256,2048]{1,0:T(8,128)(2,1)}, bf16[256,2048]{1,0:T(8,128)(2,1)S(1)}, u32[]{:S(2)}, u32[]{:S(2)}) collective-permute-start(bf16[256,2048]{1,0:T(8,128)(2,1)} %add.652.refs_7_), channel_id=1, source_target_pairs={{2,0},{4,2},{6,4},{7,6},{5,7},{3,5},{1,3},{0,1},{10,8},{12,10},{14... | collective-permute-start | bytes 3145736 | tf_op jit(solution)/shard_map/ppermute | solution.py:773
  659.9 47.2 %collective-permute-start.66 = (bf16[256,2048]{1,0:T(8,128)(2,1)}, bf16[256,2048]{1,0:T(8,128)(2,1)}, u32[]{:S(2)}, u32[]{:S(2)}) collective-permute-start(bf16[256,2048]{1,0:T(8,128)(2,1)} %add.651.refs_6_), channel_id=1, source_target_pairs={{0,2},{2,4},{4,6},{6,7},{7,5},{5,3},{3,1},{1,0},{8,10},{10,12},{12... | collective-permute-start | bytes 3145736 | tf_op jit(solution)/shard_map/ppermute | solution.py:770
  713.7 39.4 %collective-permute-start.73 = (bf16[4096,512]{1,0:T(8,128)(2,1)}, bf16[4096,512]{1,0:T(8,128)(2,1)}, u32[]{:S(2)}, u32[]{:S(2)}) collective-permute-start(bf16[4096,512]{1,0:T(8,128)(2,1)} %get-tuple-element.305), channel_id=1, source_target_pairs={{0,8},{8,0},{16,24},{24,16},{1,9},{9,1},{17,25},{25,17},{2,10},{10... | collective-permute-start | bytes 12582920 | tf_op jit(solution)/shard_map/ppermute | solution.py:873
  (189 other events, 1932.3 us)
Sparse Core Ops, SparseCore 0:
  9.6 16.3 all-gather.6
  62.7 11.4 all-gather.8
  172.6 11.6 all-gather.10
